TPU v7x, 512 devices: a whole 4x8x8 slice. The times are simulated.
512 devices in a mesh: dp: 128 (over x, z_lo, y, core), mp: 4 (over z_hi).
Axes of the slice: x: 4, y: 8, z: 8 (z_hi: 4, z_lo: 2; z = z_hi * 2 + z_lo), core: 2. Of those that a mesh axis runs over, the one named last changes fastest.
Arguments:
- pooled: bfloat16 [32768, 1152], P('dp'), may hold values from -24 to 24
- ln_gain: float32 [1152], replicated, may hold values from 0.5 to 1.5
- w_up: bfloat16 [1152, 2560], P(None, 'mp'), may hold values from -0.1875 to 0.1875
- b_up: float32 [2560], P('mp'), may hold values from -6 to 6
- w_down: bfloat16 [2560, 1152], P('mp'), may hold values from -0.125 to 0.125
- text: bfloat16 [32768, 1152], P(('dp', 'mp')), may hold values from -0.625 to 0.625
- logit_scale: float32 [1], replicated, may hold values from 20 to 40
- logit_bias: float32 [1], replicated, may hold values from -3 to -1
Outputs:
- up_grad: float32 [1152, 2560], P('dp', 'mp')
- text_grad: float32 [32768, 1152], P(('dp', 'mp'))
- text_loss: float32 [32768], P(('dp', 'mp'))
All inputs are finite; a program needn't handle non-finite values.
Results may differ from a plain program's by a relative error of at most 0.023.
Values may be sent and summed in bfloat16 or wider, within the bound.
No kernel may reach another device: no remote copies, remote signals or barrier semaphores. Data moves between devices by JAX's collectives and lax.ppermute only.
A program may use at most 64 MiB of HBM per device.

v0:
```python
import math

import jax
import jax.numpy as jnp
from jax import lax
from jax.sharding import PartitionSpec as P

REACH = 3


gelu_coeff = 0.044715
root_two_pi = math.sqrt(2.0 / math.pi)


def shifted(value, axis, by):
    devices = lax.axis_size(axis)
    return lax.ppermute(value, axis, [(i, (i + by) % devices) for i in range(devices)])


def gelu_value(hidden_pre):
    inner = root_two_pi * (hidden_pre + gelu_coeff * hidden_pre * hidden_pre * hidden_pre)
    return 0.5 * hidden_pre * (1.0 + jnp.tanh(inner))


def gelu_slope(hidden_pre):
    inner = root_two_pi * (hidden_pre + gelu_coeff * hidden_pre * hidden_pre * hidden_pre)
    tanh_value = jnp.tanh(inner)
    return 0.5 * (1.0 + tanh_value) + 0.5 * hidden_pre * (
        1.0 - tanh_value * tanh_value
    ) * root_two_pi * (1.0 + 3.0 * gelu_coeff * hidden_pre * hidden_pre)


def layer_norm(rows_in, ln_gain):
    values = rows_in.astype(jnp.float32)
    center = values - jnp.mean(values, axis=-1, keepdims=True)
    spread = jnp.mean(center * center, axis=-1, keepdims=True)
    return (center * lax.rsqrt(spread + 1e-06) * ln_gain).astype(jnp.bfloat16)


def unit_rows(rows_float):
    inverse = lax.rsqrt(jnp.sum(rows_float * rows_float, axis=-1, keepdims=True) + 1e-06)
    return (inverse, rows_float * inverse)


def body(pooled, ln_gain, w_up, b_up, w_down, text, logit_scale, logit_bias):
    rows_count = pooled.shape[0]
    quarter = text.shape[0]
    width = pooled.shape[1]
    window = 2 * REACH + 1
    scale_value = logit_scale[0]
    bias_value = logit_bias[0]
    normed = layer_norm(pooled, ln_gain)
    hidden_pre = jnp.dot(normed, w_up, preferred_element_type=jnp.float32) + b_up
    activation = gelu_value(hidden_pre).astype(jnp.bfloat16)
    partial_out = jnp.dot(activation, w_down, preferred_element_type=jnp.float32)
    embedded = pooled.astype(jnp.float32) + lax.psum(partial_out.astype(jnp.bfloat16), "mp").astype(
        jnp.float32
    )
    inverse, image_unit = unit_rows(embedded)
    unit_half = image_unit.astype(jnp.bfloat16)
    text_inv, text_unit = unit_rows(text.astype(jnp.float32))
    text_half = text_unit.astype(jnp.bfloat16)
    group_index = lax.axis_index("mp")
    row_ids = lax.broadcasted_iota(jnp.int32, (rows_count, quarter), 0)
    col_ids = lax.broadcasted_iota(jnp.int32, (rows_count, quarter), 1)
    positive = (row_ids == col_ids + group_index * quarter).astype(jnp.float32)
    no_match = jnp.zeros((rows_count, quarter), jnp.float32)
    current = shifted(text_half, "dp", -REACH)
    grad_unit = jnp.zeros((rows_count, width), jnp.float32)
    carried_grad = jnp.zeros((quarter, width), jnp.float32)
    carried_loss = jnp.zeros((quarter,), jnp.float32)
    for position in range(window):
        is_pair = positive if position == REACH else no_match
        logits = (
            scale_value
            * lax.dot_general(
                unit_half, current, (((1,), (1,)), ((), ())), preferred_element_type=jnp.float32
            )
            + bias_value
        )
        pair_loss = jax.nn.softplus(logits) - is_pair * logits
        coefficient = ((jax.nn.sigmoid(logits) - is_pair) * (scale_value / window)).astype(
            jnp.bfloat16
        )
        image_part = jnp.dot(coefficient, current, preferred_element_type=jnp.float32)
        text_part = lax.dot_general(
            coefficient, unit_half, (((0,), (0,)), ((), ())), preferred_element_type=jnp.float32
        )
        image_part, text_part, loss_col = (image_part, text_part, jnp.sum(pair_loss, axis=0))
        grad_unit = grad_unit + image_part
        carried_grad = carried_grad + text_part
        carried_loss = carried_loss + loss_col
        if position + 1 < window:
            current = shifted(current, "dp", 1)
            carried_grad, carried_loss = (
                shifted(carried_grad.astype(jnp.bfloat16), "dp", 1).astype(carried_grad.dtype),
                shifted(carried_loss.astype(jnp.bfloat16), "dp", 1).astype(carried_loss.dtype),
            )
    text_acc, loss_acc = (
        shifted(carried_grad.astype(jnp.bfloat16), "dp", -REACH).astype(carried_grad.dtype),
        shifted(carried_loss.astype(jnp.bfloat16), "dp", -REACH).astype(carried_loss.dtype),
    )
    grad_sum = lax.psum(grad_unit.astype(jnp.bfloat16), "mp").astype(jnp.float32)
    radial = jnp.sum(image_unit * grad_sum, axis=-1, keepdims=True)
    grad_image = (inverse * (grad_sum - image_unit * radial)).astype(jnp.bfloat16)
    grad_act = lax.dot_general(
        grad_image, w_down, (((1,), (1,)), ((), ())), preferred_element_type=jnp.float32
    )
    grad_pre = (grad_act * gelu_slope(hidden_pre)).astype(jnp.bfloat16)
    up_grad = lax.psum_scatter(
        lax.dot_general(
            normed, grad_pre, (((0,), (0,)), ((), ())), preferred_element_type=jnp.float32
        ),
        "dp",
        scatter_dimension=0,
        tiled=True,
    )
    text_radial = jnp.sum(text_unit * text_acc, axis=-1, keepdims=True)
    text_grad = text_inv * (text_acc - text_unit * text_radial)
    text_loss = loss_acc / (window * rows_count)
    return (up_grad, text_grad, text_loss)


def solution(mesh):
    placed = (
        P("dp", None),
        P(),
        P(None, "mp"),
        P("mp"),
        P("mp", None),
        P(("dp", "mp"), None),
        P(),
        P(),
    )
    return jax.shard_map(
        body,
        mesh=mesh,
        in_specs=placed,
        out_specs=(P("dp", "mp"), P(("dp", "mp"), None), P(("dp", "mp"))),
        check_vma=False,
    )
```

profile of v0, /device:TPU:1, one launch (start us, length us, event | category | flops | bytes accessed | tf_op | source)
XLA Modules:
  0.0 1303.4 jit_solution(11616843304278911998)
XLA Ops:
  10.6 2.1 convolution_add_fusion.6
  15.4 10.5 collective-permute-start
  25.9 4.3 collective-permute-done
  32.8 2.1 collective-permute-done.1
  34.9 4.3 collective-permute-start.2
  42.5 3.8 collective-permute-done.2
  48.2 33.7 %all-reduce.5.cloned.1.call-done = bf16[256,1152]{1,0:T(8,128)(2,1)} async-done(((bf16[256,1152]{1,0:T(8,128)(2,1)}), bf16[256,1152]{1,0:T(8,128)(2,1)}) %all-reduce.5.cloned.1.call-update) | async-done | bytes 589840 | tf_op jit(solution)/shard_map/psum | solution.py:56
  84.7 4.1 collective-permute-start.14
  94.8 1.9 collective-permute-start.15
  97.8 3.8 collective-permute-start.16
  101.5 1.9 collective-permute-start.7
  103.5 3.3 collective-permute-start.4
  106.8 1.9 collective-permute-start.17
  110.9 4.5 collective-permute-done.17
  115.4 1.9 collective-permute-start.18
  117.6 1.9 collective-permute-start.8
  119.5 1.9 collective-permute-start.5
  122.7 4.2 collective-permute-done.8
  127.6 1.9 collective-permute-start.9
  129.5 1.9 collective-permute-start.6
  132.3 7.9 collective-permute-done.6
  143.0 2.0 collective-permute-start.19
  146.7 1.9 collective-permute-start.10
  148.6 53.7 %all-reduce.7.cloned.1.call-done = bf16[256,1152]{1,0:T(8,128)(2,1)} async-done(((bf16[256,1152]{1,0:T(8,128)(2,1)}), bf16[256,1152]{1,0:T(8,128)(2,1)}) %all-reduce.7.cloned.1.call-update) | async-done | bytes 589840 | tf_op jit(solution)/shard_map/psum | solution.py:103
  203.8 4.5 fusion.4
  210.2 4.1 collective-permute-start.11
  214.3 5.9 collective-permute-start.20
  220.2 3.8 collective-permute-start.12
  224.3 1.9 collective-permute-done.12
  226.2 5.0 collective-permute-start.13
  231.8 4.2 collective-permute-done.13
  237.1 1058.3 %all-reduce.9.cloned.1.call-done = f32[1152,640]{1,0:T(8,128)} async-done(((f32[1152,640]{1,0:T(8,128)}), f32[1152,640]{1,0:T(8,128)}) %all-reduce.9.cloned.1.call-update) | async-done | bytes 2949136
  (103 shorter events, 37.8 us)
Async XLA Ops:
  7.2 6.4 copy-start
  7.2 3.4 copy-start.1
  7.2 3.4 copy-start.13
  7.2 3.4 copy-start.11
  7.2 74.7 %all-reduce.5.cloned.1.call-start = ((), (), s32[]{:S(2)}) async-start(), calls=%async_computation | async-start | bytes 1179648 | tf_op jit(solution)/shard_map/psum | solution.py:56
  15.1 187.2 %all-reduce.7.cloned.1.call-start = ((), (), s32[]{:S(2)}) async-start(), calls=%async_computation.1 | async-start | bytes 1179648 | tf_op jit(solution)/shard_map/psum | solution.py:103
  15.4 14.8 %collective-permute-start = (bf16[64,1152]{1,0:T(8,128)(2,1)S(1)}, bf16[64,1152]{1,0:T(8,128)(2,1)S(1)}, u32[]{:S(2)}, u32[]{:S(2)}) collective-permute-start(bf16[64,1152]{1,0:T(8,128)(2,1)S(1)} %fusion.47), channel_id=1, source_target_pairs={{0,500},{4,504},{8,508},{12,0},{16,4},{20,8},{24,12},{28,16},{32,2... | collective-permute-start | bytes 442376 | tf_op jit(solution)/shard_map/ppermute | solution.py:17
  30.9 4.0 collective-permute-start.1
  34.9 48.4 %copy-start.7 = (bf16[64,1152]{1,0:T(8,128)(2,1)}, bf16[64,1152]{1,0:T(8,128)(2,1)S(1)}, u32[]{:S(2)}) copy-start(bf16[64,1152]{1,0:T(8,128)(2,1)S(1)} %collective-permute-done.1) | copy-start | bytes 442372
  34.9 11.4 collective-permute-start.2
  46.3 42.5 %collective-permute-start.3 = (bf16[64,1152]{1,0:T(8,128)(2,1)}, bf16[64,1152]{1,0:T(8,128)(2,1)S(1)}, u32[]{:S(2)}, u32[]{:S(2)}) collective-permute-start(bf16[64,1152]{1,0:T(8,128)(2,1)} %collective-permute-done.2), channel_id=1, source_target_pairs={{0,4},{4,8},{8,12},{12,16},{16,20},{20,24},{24,28},{28,32},{32,36}... | collective-permute-start | bytes 442376 | tf_op jit(solution)/shard_map/ppermute | solution.py:17
  84.7 10.0 collective-permute-start.14
  94.8 3.0 collective-permute-start.15
  97.8 9.0 collective-permute-start.16
  101.5 15.8 %collective-permute-start.7 = (bf16[64,1152]{1,0:T(8,128)(2,1)S(1)}, bf16[64,1152]{1,0:T(8,128)(2,1)S(1)}, u32[]{:S(2)}, u32[]{:S(2)}) collective-permute-start(bf16[64,1152]{1,0:T(8,128)(2,1)S(1)} %convolution_convert_fusion.1), channel_id=1, source_target_pairs={{0,4},{4,8},{8,12},{12,16},{16,20},{20,24},{24,28},{28,32},{32,36}... | collective-permute-start | bytes 442376 | tf_op jit(solution)/shard_map/ppermute | solution.py:17
  103.5 7.0 collective-permute-start.4
  106.8 8.6 collective-permute-start.17
  115.4 27.0 %collective-permute-start.18 = (bf16[64]{0:T(256)(128)(2,1)S(1)}, bf16[64]{0:T(256)(128)(2,1)S(1)}, u32[]{:S(2)}, u32[]{:S(2)}) collective-permute-start(bf16[64]{0:T(256)(128)(2,1)S(1)} %add_convert_fusion.8), channel_id=1, source_target_pairs={{0,4},{4,8},{8,12},{12,16},{16,20},{20,24},{24,28},{28,32},{32,36}... | collective-permute-start | bytes 392 | tf_op jit(solution)/shard_map/ppermute | solution.py:17
  117.6 9.3 collective-permute-start.8
  119.5 10.0 collective-permute-start.5
  127.6 17.4 %collective-permute-start.9 = (bf16[64,1152]{1,0:T(8,128)(2,1)}, bf16[64,1152]{1,0:T(8,128)(2,1)}, u32[]{:S(2)}, u32[]{:S(2)}) collective-permute-start(bf16[64,1152]{1,0:T(8,128)(2,1)} %add_convert_fusion.4), channel_id=1, source_target_pairs={{0,4},{4,8},{8,12},{12,16},{16,20},{20,24},{24,28},{28,32},{32,36}... | collective-permute-start | bytes 442376 | tf_op jit(solution)/shard_map/ppermute | solution.py:17
  129.5 10.7 collective-permute-start.6
  142.4 1153.0 %all-reduce.9.cloned.1.call-start = ((), (), s32[]{:S(2)}) async-start(), calls=%async_computation.2 | async-start | bytes 5898240
  143.0 60.8 %copy-start.10 = (f32[256]{0:T(256)S(1)}, f32[256]{0:T(256)}, u32[]{:S(2)}) copy-start(f32[256]{0:T(256)} %copy-done.9) | copy-start | bytes 3076
  143.0 60.8 %copy-start.12 = (f32[1152]{0:T(1024)S(1)}, f32[1152]{0:T(1024)}, u32[]{:S(2)}) copy-start(f32[1152]{0:T(1024)} %param.9) | copy-start | bytes 13828
  143.0 71.3 %collective-permute-start.19 = (bf16[64]{0:T(256)(128)(2,1)}, bf16[64]{0:T(256)(128)(2,1)S(1)}, u32[]{:S(2)}, u32[]{:S(2)}) collective-permute-start(bf16[64]{0:T(256)(128)(2,1)} %add_convert_fusion.7), channel_id=1, source_target_pairs={{0,4},{4,8},{8,12},{12,16},{16,20},{20,24},{24,28},{28,32},{32,36}... | collective-permute-start | bytes 392 | tf_op jit(solution)/shard_map/ppermute | solution.py:17
  146.7 61.8 %collective-permute-start.10 = (bf16[64,1152]{1,0:T(8,128)(2,1)}, bf16[64,1152]{1,0:T(8,128)(2,1)}, u32[]{:S(2)}, u32[]{:S(2)}) collective-permute-start(bf16[64,1152]{1,0:T(8,128)(2,1)} %add_convert_fusion.3), channel_id=1, source_target_pairs={{0,4},{4,8},{8,12},{12,16},{16,20},{20,24},{24,28},{28,32},{32,36}... | collective-permute-start | bytes 442376 | tf_op jit(solution)/shard_map/ppermute | solution.py:17
  208.3 6.0 copy-start.14
  210.2 10.0 collective-permute-start.11
  214.3 17.0 %collective-permute-start.20 = (bf16[64]{0:T(256)(128)(2,1)S(1)}, bf16[64]{0:T(256)(128)(2,1)S(1)}, u32[]{:S(2)}, u32[]{:S(2)}) collective-permute-start(bf16[64]{0:T(256)(128)(2,1)S(1)} %add_convert_fusion.6), channel_id=1, source_target_pairs={{0,500},{4,504},{8,508},{12,0},{16,4},{20,8},{24,12},{28,16},{32,2... | collective-permute-start | bytes 392 | tf_op jit(solution)/shard_map/ppermute | solution.py:17
  220.2 6.0 collective-permute-start.12
  226.2 9.7 collective-permute-start.13
  (8 other events, 8.3 us)
Sparse Core Ops, SparseCore 0:
  15.2 66.6 all-reduce.4
  142.5 59.7 all-reduce.6
  208.4 1086.9 all-reduce.8
where the time goes:
time: 1300 us
  waiting for transfers between devices  1180 us (91%)
  starting transfers between devices  67.9 us (5%)
  matrix products  20 us (2%)
  between operations  16.2 us (1%)
    unnamed x4, waiting for transfers between devices  1060 us
    ppermute x21, starting transfers between devices, shifted(): lax.ppermute(value, axis, [(i, (i + by) % devices) for i in range(devices)])  67.8 us
    psum x1, waiting for transfers between devices, body(): lax.psum(grad_unit.astype(jnp.bfloat16), 'mp').astype(jnp.float32)  53.7 us
    ppermute x21, waiting for transfers between devices, shifted(): lax.ppermute(value, axis, [(i, (i + by) % devices) for i in range(devices)])  35.7 us
    psum x1, waiting for transfers between devices, body(): lax.psum(partial_out.astype(jnp.bfloat16), 'mp').astype(jnp.float32)  33.7 us
  transfers between devices with their start and end apart: 24, of which 13 were waited for; matrix products, arithmetic and copies ran while one was open for 2% of the time, Pallas kernels for 0%

commit v1 on v0

v1 whole, which is shorter than its diff:
```python
import math

import jax
import jax.numpy as jnp
from jax import lax
from jax.sharding import Mesh, PartitionSpec as P

REACH = 3
WINDOW = 2 * REACH + 1
CHIPS = ("x", "zl", "y")
DP = ("x", "zl", "y", "c")
N_DP = 128

gelu_coeff = 0.044715
root_two_pi = math.sqrt(2.0 / math.pi)
f32 = jnp.float32
bf16 = jnp.bfloat16


def moved(value, pairs):
    return lax.ppermute(value, DP, [(s % N_DP, d % N_DP) for s, d in pairs])


def swapped(value):
    return lax.ppermute(value, "c", [(0, 1), (1, 0)])


def gelu_value(hidden_pre):
    inner = root_two_pi * (hidden_pre + gelu_coeff * hidden_pre * hidden_pre * hidden_pre)
    return 0.5 * hidden_pre * (1.0 + jnp.tanh(inner))


def gelu_slope(hidden_pre):
    inner = root_two_pi * (hidden_pre + gelu_coeff * hidden_pre * hidden_pre * hidden_pre)
    tanh_value = jnp.tanh(inner)
    return 0.5 * (1.0 + tanh_value) + 0.5 * hidden_pre * (
        1.0 - tanh_value * tanh_value
    ) * root_two_pi * (1.0 + 3.0 * gelu_coeff * hidden_pre * hidden_pre)


def layer_norm(rows_in, ln_gain):
    values = rows_in.astype(f32)
    center = values - jnp.mean(values, axis=-1, keepdims=True)
    spread = jnp.mean(center * center, axis=-1, keepdims=True)
    return (center * lax.rsqrt(spread + 1e-06) * ln_gain).astype(bf16)


def unit_rows(rows_float):
    inverse = lax.rsqrt(jnp.sum(rows_float * rows_float, axis=-1, keepdims=True) + 1e-06)
    return (inverse, rows_float * inverse)


def dot(a, b, ca, cb):
    return lax.dot_general(a, b, (((ca,), (cb,)), ((), ())), preferred_element_type=f32)


def mp_sum_rows(partial, quarter):
    parts = lax.all_to_all(partial.reshape(4, quarter, -1), "mp", 0, 0, tiled=True)
    return jnp.sum(parts.astype(f32), axis=0)


def body(pooled, ln_gain, w_up, b_up, w_down, text, logit_scale, logit_bias):
    rows_count, width = pooled.shape
    quarter = text.shape[0]
    units = w_up.shape[1]
    own_rows = width // N_DP
    scale_value = logit_scale[0]
    bias_value = logit_bias[0]
    core = lax.axis_index("c")
    group = lax.axis_index("mp")

    normed = layer_norm(pooled, ln_gain)
    hidden_pre = jnp.dot(normed, w_up, preferred_element_type=f32) + b_up
    activation = gelu_value(hidden_pre).astype(bf16)
    partial_out = jnp.dot(activation, w_down, preferred_element_type=f32).astype(bf16)
    summed = mp_sum_rows(partial_out, quarter)

    text_inv, text_unit = unit_rows(text.astype(f32))
    text_half = text_unit.astype(bf16)
    pair = lax.all_gather(text_half, "c", axis=0, tiled=True)
    left = moved(pair, [(i, i + 2) for i in range(N_DP)])
    right = moved(pair, [(i, i - 2) for i in range(N_DP)])
    far_out = [(i - 3, i) if i % 2 == 0 else (i + 3, i) for i in range(N_DP)]
    far = moved(text_half, far_out)
    texts = jnp.concatenate([left, pair, right, far], axis=0)

    feature = lax.broadcasted_iota(jnp.int32, (width, width // 2), 0)
    slot = lax.broadcasted_iota(jnp.int32, (width, width // 2), 1)
    wanted = (slot // own_rows) * (2 * own_rows) + slot % own_rows
    mine = (feature == wanted + core * own_rows).astype(bf16)
    theirs = (feature == wanted + (1 - core) * own_rows).astype(bf16)
    normed_mine = jnp.dot(normed, mine, preferred_element_type=f32).astype(bf16)
    normed_theirs = swapped(jnp.dot(normed, theirs, preferred_element_type=f32).astype(bf16))

    own_pooled = lax.dynamic_slice_in_dim(pooled, group * quarter, quarter, 0)
    embedded = own_pooled.astype(f32) + summed
    inverse, image_unit = unit_rows(embedded)
    unit_half = lax.all_gather(image_unit.astype(bf16), "mp", axis=0, tiled=True)

    logits = scale_value * dot(unit_half, texts, 1, 1) + bias_value
    row_ids = lax.broadcasted_iota(jnp.int32, logits.shape, 0)
    col_ids = lax.broadcasted_iota(jnp.int32, logits.shape, 1)
    own_col = col_ids - (2 + core) * quarter
    is_pair = (
        (own_col >= 0) & (own_col < quarter) & (row_ids == own_col + group * quarter)
    ).astype(f32)
    pair_loss = jax.nn.softplus(logits) - is_pair * logits
    coefficient = ((jax.nn.sigmoid(logits) - is_pair) * (scale_value / WINDOW)).astype(bf16)
    image_part = dot(coefficient, texts, 1, 0).astype(bf16)
    grad_sum = mp_sum_rows(image_part, quarter)

    radial = jnp.sum(image_unit * grad_sum, axis=-1, keepdims=True)
    grad_own = (inverse * (grad_sum - image_unit * radial)).astype(bf16)
    grad_image = lax.all_gather(grad_own, "mp", axis=0, tiled=True)
    grad_act = dot(grad_image, w_down, 1, 1)
    grad_pre = (grad_act * gelu_slope(hidden_pre)).astype(bf16)
    grad_other = swapped(grad_pre)
    up_part = dot(normed_mine, grad_pre, 0, 0) + dot(normed_theirs, grad_other, 0, 0)
    chips = N_DP // 2
    lanes = 128
    packed = own_rows * units // lanes
    up_wire = jnp.pad(
        up_part.astype(bf16).reshape(chips, packed, lanes), ((0, 0), (0, -packed % 16), (0, 0))
    )
    up_terms = lax.all_to_all(up_wire, CHIPS, 0, 0, tiled=True)
    up_grad = jnp.sum(up_terms.astype(f32), axis=0)[:packed].reshape(own_rows, units)

    text_part = dot(coefficient, unit_half, 0, 0)
    loss_part = jnp.sum(pair_loss, axis=0)
    loss_high = loss_part.astype(bf16)
    loss_low = (loss_part - loss_high.astype(f32)).astype(bf16)
    loss_cols = jnp.pad(jnp.stack([loss_high, loss_low], axis=1).astype(f32), ((0, 0), (0, lanes - 2)))
    both = jnp.concatenate([text_part, loss_cols], axis=1)
    q = quarter
    left_part, right_part, far_part = both[: 2 * q], both[4 * q : 6 * q], both[6 * q :]
    own_first, own_second = both[2 * q : 3 * q], both[3 * q : 4 * q]
    first = core == 0
    keep_side = jnp.where(first, left_part, right_part)
    give_side = jnp.where(first, right_part, left_part)
    keep_own = jnp.where(first, own_first, own_second)
    give_own = jnp.where(first, own_second, own_first)
    got = swapped(jnp.concatenate([give_side, give_own], axis=0).astype(bf16)).astype(f32)
    side = (keep_side + got[: 2 * q]).astype(bf16)
    own_sum = keep_own + got[2 * q :]
    came = moved(side, [(i, i - 2) if i % 2 == 0 else (i, i + 2) for i in range(N_DP)])
    far_back = moved(far_part.astype(bf16), [(d, s) for s, d in far_out])
    came_first, came_second = came[:q], came[q:]
    last = swapped(jnp.where(first, came_second, came_first))
    total = (
        own_sum
        + jnp.where(first, came_first, came_second).astype(f32)
        + last.astype(f32)
        + far_back.astype(f32)
    )
    text_acc = total[:, :width]
    text_loss = (total[:, width] + total[:, width + 1]) / (WINDOW * rows_count)
    text_radial = jnp.sum(text_unit * text_acc, axis=-1, keepdims=True)
    text_grad = text_inv * (text_acc - text_unit * text_radial)
    return (up_grad, text_grad, text_loss)


def solution(mesh):
    fine = Mesh(mesh.devices.reshape(4, 2, 8, 2, 4), ("x", "zl", "y", "c", "mp"))
    every = (*DP, "mp")
    placed = (
        P(DP, None),
        P(),
        P(None, "mp"),
        P("mp"),
        P("mp", None),
        P(every, None),
        P(),
        P(),
    )
    return jax.shard_map(
        body,
        mesh=fine,
        in_specs=placed,
        out_specs=(P(DP, "mp"), P(every, None), P(every)),
        check_vma=False,
    )
```

time: 1300 us -> 173 us (0.13)
  waiting for transfers between devices: 1180 us -> 25 us
  blocking collectives: 0 us -> 41.2 us
  starting transfers between devices: 67.9 us -> 51.3 us
  between operations: 16.2 us -> 2.36 us
    unnamed x4 -> x0, waiting for transfers between devices: 1060 us -> none
    psum x2 -> x0, waiting for transfers between devices: 87.4 us -> none  [the longest x1 53.7 us: body(): lax.psum(grad_unit.astype(jnp.bfloat16), 'mp').astype(jnp.float32)]
    all_gather x0 -> x3, blocking collectives: none -> 41.2 us  [the longest x1 17.6 us: body(): grad_image = lax.all_gather(grad_own, 'mp', axis=0, tiled=True)]
    ppermute x21 -> x9, starting transfers between devices: 67.8 us -> 32.1 us  [the longest x5 18.7 us: moved(): return lax.ppermute(value, DP, [(s % N_DP, d % N_DP) for s, d in pairs])]
    ppermute x21 -> x9, waiting for transfers between devices: 35.7 us -> 1.09 us  [the longest x4 1.08 us: swapped(): return lax.ppermute(value, 'c', [(0, 1), (1, 0)])]
    all_to_all x0 -> x3, waiting for transfers between devices: none -> 23.9 us  [the longest x1 13.8 us: body(): up_terms = lax.all_to_all(up_wire, CHIPS, 0, 0, tiled=True)]
    all_to_all x0 -> x3, starting transfers between devices: none -> 19.1 us  [the longest x2 10.2 us: mp_sum_rows(): lax.all_to_all(partial.reshape(4, quarter, -1), 'mp', 0, 0, tiled=True)]
  transfers between devices with their start and end apart: 24 -> 12, of which waited for: 13 -> 4; matrix products, arithmetic and copies ran while one was open for 2% -> 23% of each run, Pallas kernels for 0% -> 0%
where the time goes in v1:
time: 173 us; the launch traced here: 170 us
  starting transfers between devices  51.3 us (30%)
  blocking collectives  41.2 us (24%)
  waiting for transfers between devices  25 us (14%)
  matrix products  21.6 us (12%)
  other arithmetic  18.9 us (11%)
  local copies, waits for them, and re-layouts  9.97 us (6%)
  between operations  2.36 us (1%)
    ppermute x5, starting transfers between devices, moved(): return lax.ppermute(value, DP, [(s % N_DP, d % N_DP) for s, d in pairs])  18.7 us
    all_gather x1, blocking collectives, body(): grad_image = lax.all_gather(grad_own, 'mp', axis=0, tiled=True)  17.6 us
    dot_general x6, matrix products, dot(): lax.dot_general(a, b, (((ca,), (cb,)), ((), ())), preferred_element_type=...  15.8 us
    all_gather x1, blocking collectives, body(): lax.all_gather(image_unit.astype(bf16), 'mp', axis=0, tiled=True)  15.1 us
    all_to_all x1, waiting for transfers between devices, body(): up_terms = lax.all_to_all(up_wire, CHIPS, 0, 0, tiled=True)  13.8 us
    ppermute x4, starting transfers between devices, swapped(): return lax.ppermute(value, 'c', [(0, 1), (1, 0)])  13.5 us
    all_to_all x2, starting transfers between devices, mp_sum_rows(): lax.all_to_all(partial.reshape(4, quarter, -1), 'mp', 0, 0, tiled=True)  10.2 us
    all_to_all x2, waiting for transfers between devices, mp_sum_rows(): lax.all_to_all(partial.reshape(4, quarter, -1), 'mp', 0, 0, tiled=True)  10.1 us
  transfers between devices with their start and end apart: 12, of which 4 were waited for; matrix products, arithmetic and copies ran while one was open for 23% of the time, Pallas kernels for 0%

profile of v1, /device:TPU:1, one launch (start us, length us, event | category | flops | bytes accessed | tf_op | source)
XLA Modules:
  0.0 170.3 jit_solution(18389427574397056322)
XLA Ops:
  2.9 8.5 %all_gather.10 = bf16[128,1152]{1,0:T(8,128)(2,1)S(1)} all-gather(bf16[64,1152]{1,0:T(8,128)(2,1)S(1)} %fusion.41), channel_id=1, replica_groups=mesh['x'=4,'zl'=2,'y'=8,'c'=2,'mp'=4] {'c'}, dimensions={0}, use_global_device_ids=true | all-gather | bytes 442368 | tf_op jit(solution)/shard_map/all_gather | solution.py:80
  11.4 1.9 %collective-permute-start = (bf16[128,1152]{1,0:T(8,128)(2,1)S(1)}, bf16[128,1152]{1,0:T(8,128)(2,1)}, u32[]{:S(2)}, u32[]{:S(2)}) collective-permute-start(bf16[128,1152]{1,0:T(8,128)(2,1)S(1)} %all_gather.10), channel_id=1, source_target_pairs={{0,8},{4,12},{8,16},{12,20},{16,24},{20,28},{24,32},{28,36},{32,40... | collective-permute-start | bytes 884744 | tf_op jit(solution)/shard_map/ppermute | solution.py:21
  13.3 7.6 %collective-permute-start.1 = (bf16[128,1152]{1,0:T(8,128)(2,1)S(1)}, bf16[128,1152]{1,0:T(8,128)(2,1)S(1)}, u32[]{:S(2)}, u32[]{:S(2)}) collective-permute-start(bf16[128,1152]{1,0:T(8,128)(2,1)S(1)} %all_gather.10), channel_id=1, source_target_pairs={{0,504},{4,508},{8,0},{12,4},{16,8},{20,12},{24,16},{28,20},{32,24... | collective-permute-start | bytes 884744 | tf_op jit(solution)/shard_map/ppermute | solution.py:21
  20.9 1.9 %collective-permute-start.2 = (bf16[64,1152]{1,0:T(8,128)(2,1)S(1)}, bf16[64,1152]{1,0:T(8,128)(2,1)S(1)}, u32[]{:S(2)}, u32[]{:S(2)}) collective-permute-start(bf16[64,1152]{1,0:T(8,128)(2,1)S(1)} %fusion.41), channel_id=1, source_target_pairs={{500,0},{16,4},{508,8},{24,12},{4,16},{32,20},{12,24},{40,28},{20,... | collective-permute-start | bytes 442376 | tf_op jit(solution)/shard_map/ppermute | solution.py:21
  24.4 1.4 convolution_add_fusion
  25.9 1.5 convolution_convert_fusion.1
  27.4 5.3 %all-to-all-start = ((bf16[4,64,1152]{2,1,0:T(8,128)(2,1)}), bf16[4,64,1152]{2,1,0:T(8,128)(2,1)S(1)}, u32[]{:S(2)}, u32[]{:S(2)}) async-start(bf16[4,64,1152]{2,1,0:T(8,128)(2,1)} %bitcast.20), calls=%async_computation | async-start | bytes 1179648 | tf_op jit(solution)/shard_map/all_to_all | solution.py:58
  36.3 1.7 %constant_dynamic-update-slice_fusion.3 = bf16[448,1152]{1,0:T(8,128)(2,1)} fusion(bf16[128,1152]{1,0:T(8,128)(2,1)} %collective-permute-done), kind=kLoop, calls=%fused_computation.105 | loop fusion | bytes 589824
  40.2 8.0 %all-to-all-done = bf16[4,64,1152]{2,1,0:T(8,128)(2,1)S(1)} async-done(((bf16[4,64,1152]{2,1,0:T(8,128)(2,1)}), bf16[4,64,1152]{2,1,0:T(8,128)(2,1)S(1)}, u32[]{:S(2)}, u32[]{:S(2)}) %all-to-all-start) | async-done | bytes 589856 | tf_op jit(solution)/shard_map/all_to_all | solution.py:58
  49.1 15.1 %all_gather.9 = bf16[256,1152]{1,0:T(8,128)(2,1)S(1)} all-gather(bf16[64,1152]{1,0:T(8,128)(2,1)S(1)} %multiply_convert_fusion.4), channel_id=1, replica_groups=mesh['x'=4,'zl'=2,'y'=8,'c'=2,'mp'=4] {'mp'}, dimensions={0}, use_global_device_ids=true | all-gather | bytes 737280 | tf_op jit(solution)/shard_map/all_gather | solution.py:98
  64.2 3.0 %fusion.37 = (f32[448]{0:T(512)S(1)}, f32[256,448]{0,1:T(8,128)}) fusion(s32[448]{0:T(512)S(1)} %copy-done.10, pred[448]{0:T(512)(128)(4,1)S(1)} %copy-done.18, f32[]{:T(128)} %bitcast.19, bf16[256,1152]{1,0:T(8,128)(2,1)S(1)} %all_gather.9, bf16[448,1152]{1,0:T(8,128)(2,1)} %constant_dynamic-update-slice_fusion, f32[]{:T(128)} %bitcast.17), kind=kOutput, calls=%fused_computation.66 | convolution fusion | flops 265731648 | bytes 2084808 | tf_op jit(solution)/shard_map/dot_general | solution.py:54
  67.4 1.9 %fusion.75 = f32[448,1152]{1,0:T(8,128)S(1)} fusion(bf16[256,1152]{1,0:T(8,128)(2,1)} %copy-done.8, f32[256,448]{0,1:T(8,128)} %get-tuple-element.6, f32[]{:T(128)S(6)} %div.33, s32[448]{0:T(512)} %fusion.64, pred[448]{0:T(512)(128)(4,1)} %fusion.67), kind=kOutput, calls=%fused_computation.133 | convolution fusion | flops 265273344 | bytes 3115204 | tf_op jit(solution)/shard_map/dot_general | solution.py:54
  70.9 4.8 %collective-permute-start.5 = (bf16[192,1280]{1,0:T(8,128)(2,1)}, bf16[192,1280]{1,0:T(8,128)(2,1)}, u32[]{:S(2)}, u32[]{:S(2)}) collective-permute-start(bf16[192,1280]{1,0:T(8,128)(2,1)} %pad_maximum_fusion), channel_id=1, source_target_pairs={{0,4},{4,0},{1,5},{5,1},{2,6},{6,2},{3,7},{7,3},{8,12},{12,8},{9,1... | collective-permute-start | bytes 1474568 | tf_op jit(solution)/shard_map/ppermute | solution.py:25
  75.8 2.7 %convolution_convert_fusion = bf16[256,1152]{1,0:T(8,128)(2,1)} fusion(bf16[448,1152]{1,0:T(8,128)(2,1)} %constant_dynamic-update-slice_fusion, f32[256,448]{0,1:T(8,128)S(1)} %copy-done.17, f32[]{:T(128)S(6)} %div.33, s32[448]{0:T(512)S(1)} %copy-done.11, pred[448]{0:T(512)(128)(4,1)S(1)} %copy-done.19), kind=kOutput, calls=%fused_computation.9 | convolution fusion | flops 265568256 | bytes 2083012 | tf_op jit(solution)/shard_map/dot_general | solution.py:54
  78.5 4.9 %all-to-all-start.1 = ((bf16[4,64,1152]{2,1,0:T(8,128)(2,1)}), bf16[4,64,1152]{2,1,0:T(8,128)(2,1)}, u32[]{:S(2)}, u32[]{:S(2)}) async-start(bf16[4,64,1152]{2,1,0:T(8,128)(2,1)} %bitcast.21), calls=%async_computation.1 | async-start | bytes 1179648 | tf_op jit(solution)/shard_map/all_to_all | solution.py:58
  83.4 2.9 %fusion.22 = bf16[256,576]{0,1:T(8,128)(2,1)} fusion(s32[]{:T(128)S(6)} %mul.200, s32[576]{0:T(1024)} %get-tuple-element.8, s32[576]{0:T(1024)} %get-tuple-element.9, s32[576]{0:T(1024)S(1)} %get-tuple-element.7, s32[576]{0:T(1024)} %get-tuple-element.10, pred[576]{0:T(1024)(128)(4,1)S(1)} %get-tuple-element.11, pred[576]{0:T(1024)(128)(4,1)S(1)} %get-tuple-element.12, ...), kind=kOutput, calls=%fused_computation.43 | convolution fusion | flops 345341952 | bytes 901764 | tf_op jit(solution)/shard_map/dot_general | solution.py:93
  86.3 2.2 %collective-permute-start.3 = (bf16[256,576]{0,1:T(8,128)(2,1)}, bf16[256,576]{0,1:T(8,128)(2,1)}, u32[]{:S(2)}, u32[]{:S(2)}) collective-permute-start(bf16[256,576]{0,1:T(8,128)(2,1)} %fusion.22), channel_id=1, source_target_pairs={{0,4},{4,0},{1,5},{5,1},{2,6},{6,2},{3,7},{7,3},{8,12},{12,8},{9,1... | collective-permute-start | bytes 884744 | tf_op jit(solution)/shard_map/ppermute | solution.py:25
  88.5 5.4 %collective-permute-start.8 = (bf16[64,1280]{1,0:T(8,128)(2,1)}, bf16[64,1280]{1,0:T(8,128)(2,1)}, u32[]{:S(2)}, u32[]{:S(2)}) collective-permute-start(bf16[64,1280]{1,0:T(8,128)(2,1)} %get-tuple-element.3), channel_id=1, source_target_pairs={{0,500},{4,16},{8,508},{12,24},{16,4},{20,32},{24,12},{28,40},{32,... | collective-permute-start | bytes 491528 | tf_op jit(solution)/shard_map/ppermute | solution.py:21
  96.1 1.9 %collective-permute-start.6 = (bf16[128,1280]{1,0:T(8,128)(2,1)}, bf16[128,1280]{1,0:T(8,128)(2,1)}, u32[]{:S(2)}, u32[]{:S(2)}) collective-permute-start(bf16[128,1280]{1,0:T(8,128)(2,1)} %fusion.35), channel_id=1, source_target_pairs={{0,504},{4,12},{8,0},{12,20},{16,8},{20,28},{24,16},{28,36},{32,24... | collective-permute-start | bytes 983048 | tf_op jit(solution)/shard_map/ppermute | solution.py:21
  98.0 2.1 %all-to-all-done.1 = bf16[4,64,1152]{2,1,0:T(8,128)(2,1)} async-done(((bf16[4,64,1152]{2,1,0:T(8,128)(2,1)}), bf16[4,64,1152]{2,1,0:T(8,128)(2,1)}, u32[]{:S(2)}, u32[]{:S(2)}) %all-to-all-start.1) | async-done | bytes 589856 | tf_op jit(solution)/shard_map/all_to_all | solution.py:58
  103.7 17.6 %all_gather.11 = bf16[256,1152]{1,0:T(8,128)(2,1)S(1)} all-gather(bf16[64,1152]{1,0:T(8,128)(2,1)S(1)} %multiply_convert_fusion.3), channel_id=1, replica_groups=mesh['x'=4,'zl'=2,'y'=8,'c'=2,'mp'=4] {'mp'}, dimensions={0}, use_global_device_ids=true | all-gather | bytes 737280 | tf_op jit(solution)/shard_map/all_gather | solution.py:114
  121.3 1.5 fusion.20
  122.8 4.1 %collective-permute-start.4 = (bf16[256,640]{1,0:T(8,128)(2,1)}, bf16[256,640]{1,0:T(8,128)(2,1)}, u32[]{:S(2)}, u32[]{:S(2)}) collective-permute-start(bf16[256,640]{1,0:T(8,128)(2,1)} %fusion.20), channel_id=1, source_target_pairs={{0,4},{4,0},{1,5},{5,1},{2,6},{6,2},{3,7},{7,3},{8,12},{12,8},{9,1... | collective-permute-start | bytes 983048 | tf_op jit(solution)/shard_map/ppermute | solution.py:25
  126.9 3.8 %fusion.24 = f32[576,640]{1,0:T(8,128)} fusion(bf16[256,640]{1,0:T(8,128)(2,1)} %fusion.20, s32[]{:T(128)S(6)} %mul.168, s32[576]{0:T(1024)S(1)} %copy-done.9, s32[576]{0:T(1024)} %get-tuple-element.9, s32[576]{0:T(1024)S(1)} %get-tuple-element.7, s32[576]{0:T(1024)} %get-tuple-element.10, pred[576]{0:T(1024)(128)(4,1)} %copy-done.13, ...), kind=kOutput, calls=%fused_computation.45 | convolution fusion | flops 534085632 | bytes 2409092 | tf_op jit(solution)/shard_map/dot_general | solution.py:54
  130.7 2.9 %add_convert_fusion = bf16[576,640]{1,0:T(8,128)(2,1)} fusion(f32[576,640]{1,0:T(8,128)} %fusion.24, bf16[256,576]{0,1:T(8,128)(2,1)} %collective-permute-done.3, bf16[256,640]{1,0:T(8,128)(2,1)} %collective-permute-done.4), kind=kOutput, calls=%fused_computation.16 | convolution fusion | flops 189480960 | bytes 2834432 | tf_op jit(solution)/shard_map/dot_general | solution.py:54
  133.6 2.4 %reshape.71 = bf16[64,45,128]{2,1,0:T(8,128)(2,1)} reshape(bf16[576,640]{1,0:T(8,128)(2,1)} %add_convert_fusion) | data formatting | bytes 1474560 | tf_op jit(solution)/shard_map/reshape | solution.py:123
  136.0 2.1 %pad.11 = bf16[64,48,128]{2,1,0:T(8,128)(2,1)} pad(bf16[64,45,128]{2,1,0:T(8,128)(2,1)} %reshape.71, bf16[]{:T(256)} %constant.72.clone.1), padding=0_0x0_3x0_0 | pad | bytes 1523714 | tf_op jit(solution)/shard_map/jit(_pad)/pad | solution.py:122
  138.1 8.9 %all-to-all-start.2 = ((bf16[64,48,128]{2,1,0:T(8,128)(2,1)}), bf16[64,48,128]{2,1,0:T(8,128)(2,1)}, u32[]{:S(2)}, u32[]{:S(2)}) async-start(bf16[64,48,128]{2,1,0:T(8,128)(2,1)} %pad.11), calls=%async_computation.2 | async-start | bytes 1572864 | tf_op jit(solution)/shard_map/all_to_all | solution.py:125
  148.1 2.3 %collective-permute-start.7 = (bf16[64,1280]{1,0:T(8,128)(2,1)S(1)}, bf16[64,1280]{1,0:T(8,128)(2,1)S(1)}, u32[]{:S(2)}, u32[]{:S(2)}) collective-permute-start(bf16[64,1280]{1,0:T(8,128)(2,1)S(1)} %broadcast_select_fusion), channel_id=1, source_target_pairs={{0,4},{4,0},{1,5},{5,1},{2,6},{6,2},{3,7},{7,3},{8,12},{12,8},{9,1... | collective-permute-start | bytes 491528 | tf_op jit(solution)/shard_map/ppermute | solution.py:25
  151.5 1.3 fusion.47
  154.6 13.8 %all-to-all-done.2 = bf16[64,48,128]{2,1,0:T(8,128)(2,1)} async-done(((bf16[64,48,128]{2,1,0:T(8,128)(2,1)}), bf16[64,48,128]{2,1,0:T(8,128)(2,1)}, u32[]{:S(2)}, u32[]{:S(2)}) %all-to-all-start.2) | async-done | bytes 786464 | tf_op jit(solution)/shard_map/all_to_all | solution.py:125
  168.4 1.3 convert_reduce_fusion
  (90 shorter events, 21.2 us)
Async XLA Ops:
  0.6 25.2 %copy-start = (bf16[640,1152]{1,0:T(8,128)(2,1)S(1)}, bf16[640,1152]{1,0:T(8,128)(2,1)}, u32[]{:S(2)}) copy-start(bf16[640,1152]{1,0:T(8,128)(2,1)} %param.12) | copy-start | bytes 4423684
  0.6 23.5 %copy-start.5 = (bf16[256,1152]{1,0:T(8,128)(2,1)S(1)}, bf16[256,1152]{1,0:T(8,128)(2,1)}, u32[]{:S(2)}) copy-start(bf16[256,1152]{1,0:T(8,128)(2,1)} %param.8) | copy-start | bytes 1769476
  0.7 23.8 %copy-start.15 = (bf16[1152,640]{1,0:T(8,128)(2,1)S(1)}, bf16[1152,640]{1,0:T(8,128)(2,1)}, u32[]{:S(2)}) copy-start(bf16[1152,640]{1,0:T(8,128)(2,1)} %param.10) | copy-start | bytes 4423684
  0.7 23.8 %copy-start.16 = (f32[1152]{0:T(1024)S(1)}, f32[1152]{0:T(1024)}, u32[]{:S(2)}) copy-start(f32[1152]{0:T(1024)} %param.9) | copy-start | bytes 13828
  11.4 24.9 %collective-permute-start = (bf16[128,1152]{1,0:T(8,128)(2,1)S(1)}, bf16[128,1152]{1,0:T(8,128)(2,1)}, u32[]{:S(2)}, u32[]{:S(2)}) collective-permute-start(bf16[128,1152]{1,0:T(8,128)(2,1)S(1)} %all_gather.10), channel_id=1, source_target_pairs={{0,8},{4,12},{8,16},{12,20},{16,24},{20,28},{24,32},{28,36},{32,40... | collective-permute-start | bytes 884744 | tf_op jit(solution)/shard_map/ppermute | solution.py:21
  13.3 25.4 %collective-permute-start.1 = (bf16[128,1152]{1,0:T(8,128)(2,1)S(1)}, bf16[128,1152]{1,0:T(8,128)(2,1)S(1)}, u32[]{:S(2)}, u32[]{:S(2)}) collective-permute-start(bf16[128,1152]{1,0:T(8,128)(2,1)S(1)} %all_gather.10), channel_id=1, source_target_pairs={{0,504},{4,508},{8,0},{12,4},{16,8},{20,12},{24,16},{28,20},{32,24... | collective-permute-start | bytes 884744 | tf_op jit(solution)/shard_map/ppermute | solution.py:21
  20.9 18.6 %collective-permute-start.2 = (bf16[64,1152]{1,0:T(8,128)(2,1)S(1)}, bf16[64,1152]{1,0:T(8,128)(2,1)S(1)}, u32[]{:S(2)}, u32[]{:S(2)}) collective-permute-start(bf16[64,1152]{1,0:T(8,128)(2,1)S(1)} %fusion.41), channel_id=1, source_target_pairs={{500,0},{16,4},{508,8},{24,12},{4,16},{32,20},{12,24},{40,28},{20,... | collective-permute-start | bytes 442376 | tf_op jit(solution)/shard_map/ppermute | solution.py:21
  24.4 1.4 copy-start.12
  25.9 1.5 copy-start.20
  27.4 20.7 %all-to-all-start = ((bf16[4,64,1152]{2,1,0:T(8,128)(2,1)}), bf16[4,64,1152]{2,1,0:T(8,128)(2,1)S(1)}, u32[]{:S(2)}, u32[]{:S(2)}) async-start(bf16[4,64,1152]{2,1,0:T(8,128)(2,1)} %bitcast.20), calls=%async_computation | async-start | bytes 1179648 | tf_op jit(solution)/shard_map/all_to_all | solution.py:58
  39.5 24.7 %copy-start.10 = (s32[448]{0:T(512)S(1)}, s32[448]{0:T(512)}, u32[]{:S(2)}) copy-start(s32[448]{0:T(512)} %fusion.64) | copy-start | bytes 5380
  39.5 24.7 %copy-start.18 = (pred[448]{0:T(512)(128)(4,1)S(1)}, pred[448]{0:T(512)(128)(4,1)}, u32[]{:S(2)}) copy-start(pred[448]{0:T(512)(128)(4,1)} %fusion.67) | copy-start | bytes 1348
  64.1 3.0 %copy-start.8 = (bf16[256,1152]{1,0:T(8,128)(2,1)}, bf16[256,1152]{1,0:T(8,128)(2,1)S(1)}, u32[]{:S(2)}) copy-start(bf16[256,1152]{1,0:T(8,128)(2,1)S(1)} %all_gather.9) | copy-start | bytes 1769476
  67.4 2.6 %copy-start.3 = (f32[448,128]{1,0:T(8,128)}, f32[448,128]{1,0:T(8,128)S(1)}, u32[]{:S(2)}) copy-start(f32[448,128]{1,0:T(8,128)S(1)} %pad_convert_fusion) | copy-start | bytes 688132
  70.0 5.7 %copy-start.11 = (s32[448]{0:T(512)S(1)}, s32[448]{0:T(512)}, u32[]{:S(2)}) copy-start(s32[448]{0:T(512)} %fusion.64) | copy-start | bytes 5380
  70.0 5.8 %copy-start.17 = (f32[256,448]{0,1:T(8,128)S(1)}, f32[256,448]{0,1:T(8,128)}, u32[]{:S(2)}) copy-start(f32[256,448]{0,1:T(8,128)} %get-tuple-element.6) | copy-start | bytes 1376260
  70.0 5.8 %copy-start.19 = (pred[448]{0:T(512)(128)(4,1)S(1)}, pred[448]{0:T(512)(128)(4,1)}, u32[]{:S(2)}) copy-start(pred[448]{0:T(512)(128)(4,1)} %fusion.67) | copy-start | bytes 1348
  70.9 23.0 %collective-permute-start.5 = (bf16[192,1280]{1,0:T(8,128)(2,1)}, bf16[192,1280]{1,0:T(8,128)(2,1)}, u32[]{:S(2)}, u32[]{:S(2)}) collective-permute-start(bf16[192,1280]{1,0:T(8,128)(2,1)} %pad_maximum_fusion), channel_id=1, source_target_pairs={{0,4},{4,0},{1,5},{5,1},{2,6},{6,2},{3,7},{7,3},{8,12},{12,8},{9,1... | collective-permute-start | bytes 1474568 | tf_op jit(solution)/shard_map/ppermute | solution.py:25
  78.5 21.6 %all-to-all-start.1 = ((bf16[4,64,1152]{2,1,0:T(8,128)(2,1)}), bf16[4,64,1152]{2,1,0:T(8,128)(2,1)}, u32[]{:S(2)}, u32[]{:S(2)}) async-start(bf16[4,64,1152]{2,1,0:T(8,128)(2,1)} %bitcast.21), calls=%async_computation.1 | async-start | bytes 1179648 | tf_op jit(solution)/shard_map/all_to_all | solution.py:58
  83.4 2.9 %copy-start.13 = (pred[576]{0:T(1024)(128)(4,1)}, pred[576]{0:T(1024)(128)(4,1)S(1)}, u32[]{:S(2)}) copy-start(pred[576]{0:T(1024)(128)(4,1)S(1)} %get-tuple-element.11) | copy-start | bytes 1732
  83.4 2.9 %copy-start.14 = (pred[576]{0:T(1024)(128)(4,1)}, pred[576]{0:T(1024)(128)(4,1)S(1)}, u32[]{:S(2)}) copy-start(pred[576]{0:T(1024)(128)(4,1)S(1)} %get-tuple-element.12) | copy-start | bytes 1732
  86.3 44.4 %collective-permute-start.3 = (bf16[256,576]{0,1:T(8,128)(2,1)}, bf16[256,576]{0,1:T(8,128)(2,1)}, u32[]{:S(2)}, u32[]{:S(2)}) collective-permute-start(bf16[256,576]{0,1:T(8,128)(2,1)} %fusion.22), channel_id=1, source_target_pairs={{0,4},{4,0},{1,5},{5,1},{2,6},{6,2},{3,7},{7,3},{8,12},{12,8},{9,1... | collective-permute-start | bytes 884744 | tf_op jit(solution)/shard_map/ppermute | solution.py:25
  88.5 6.5 %copy-start.4 = (f32[448,128]{1,0:T(8,128)S(1)}, f32[448,128]{1,0:T(8,128)}, u32[]{:S(2)}) copy-start(f32[448,128]{1,0:T(8,128)} %copy-done.3) | copy-start | bytes 688132
  88.5 61.9 %collective-permute-start.8 = (bf16[64,1280]{1,0:T(8,128)(2,1)}, bf16[64,1280]{1,0:T(8,128)(2,1)}, u32[]{:S(2)}, u32[]{:S(2)}) collective-permute-start(bf16[64,1280]{1,0:T(8,128)(2,1)} %get-tuple-element.3), channel_id=1, source_target_pairs={{0,500},{4,16},{8,508},{12,24},{16,4},{20,32},{24,12},{28,40},{32,... | collective-permute-start | bytes 491528 | tf_op jit(solution)/shard_map/ppermute | solution.py:21
  96.1 51.0 %collective-permute-start.6 = (bf16[128,1280]{1,0:T(8,128)(2,1)}, bf16[128,1280]{1,0:T(8,128)(2,1)}, u32[]{:S(2)}, u32[]{:S(2)}) collective-permute-start(bf16[128,1280]{1,0:T(8,128)(2,1)} %fusion.35), channel_id=1, source_target_pairs={{0,504},{4,12},{8,0},{12,20},{16,8},{20,28},{24,16},{28,36},{32,24... | collective-permute-start | bytes 983048 | tf_op jit(solution)/shard_map/ppermute | solution.py:21
  100.1 2.5 %copy-start.2 = (f32[64,1152]{1,0:T(8,128)S(1)}, f32[64,1152]{1,0:T(8,128)}, u32[]{:S(2)}) copy-start(f32[64,1152]{1,0:T(8,128)} %copy-done.1) | copy-start | bytes 884740
  100.1 21.1 %copy-start.21 = (f32[256,640]{1,0:T(8,128)S(1)}, f32[256,640]{1,0:T(8,128)}, u32[]{:S(2)}) copy-start(f32[256,640]{1,0:T(8,128)} %copy-done.20) | copy-start | bytes 1966084
  121.3 5.6 %copy-start.9 = (s32[576]{0:T(1024)S(1)}, s32[576]{0:T(1024)}, u32[]{:S(2)}) copy-start(s32[576]{0:T(1024)} %get-tuple-element.8) | copy-start | bytes 6916
  122.8 7.9 %collective-permute-start.4 = (bf16[256,640]{1,0:T(8,128)(2,1)}, bf16[256,640]{1,0:T(8,128)(2,1)}, u32[]{:S(2)}, u32[]{:S(2)}) collective-permute-start(bf16[256,640]{1,0:T(8,128)(2,1)} %fusion.20), channel_id=1, source_target_pairs={{0,4},{4,0},{1,5},{5,1},{2,6},{6,2},{3,7},{7,3},{8,12},{12,8},{9,1... | collective-permute-start | bytes 983048 | tf_op jit(solution)/shard_map/ppermute | solution.py:25
  138.1 30.3 %all-to-all-start.2 = ((bf16[64,48,128]{2,1,0:T(8,128)(2,1)}), bf16[64,48,128]{2,1,0:T(8,128)(2,1)}, u32[]{:S(2)}, u32[]{:S(2)}) async-start(bf16[64,48,128]{2,1,0:T(8,128)(2,1)} %pad.11), calls=%async_computation.2 | async-start | bytes 1572864 | tf_op jit(solution)/shard_map/all_to_all | solution.py:125
  148.1 5.4 %copy-start.7 = (bf16[64,1152]{1,0:T(8,128)(2,1)S(1)}, bf16[64,1152]{1,0:T(8,128)(2,1)}, u32[]{:S(2)}) copy-start(bf16[64,1152]{1,0:T(8,128)(2,1)} %param.13) | copy-start | bytes 442372
  148.1 3.4 %collective-permute-start.7 = (bf16[64,1280]{1,0:T(8,128)(2,1)S(1)}, bf16[64,1280]{1,0:T(8,128)(2,1)S(1)}, u32[]{:S(2)}, u32[]{:S(2)}) collective-permute-start(bf16[64,1280]{1,0:T(8,128)(2,1)S(1)} %broadcast_select_fusion), channel_id=1, source_target_pairs={{0,4},{4,0},{1,5},{5,1},{2,6},{6,2},{3,7},{7,3},{8,12},{12,8},{9,1... | collective-permute-start | bytes 491528 | tf_op jit(solution)/shard_map/ppermute | solution.py:25
  (2 other events, 1.8 us)

commit v2 on v1

v2 whole, which is shorter than its diff:
```python
import math

import jax
import jax.numpy as jnp
from jax import lax
from jax.experimental import pallas as pl
from jax.experimental.pallas import tpu as pltpu
from jax.sharding import Mesh, PartitionSpec as P

REACH = 3
WINDOW = 2 * REACH + 1
CHIPS = ("x", "zl", "y")
DP = ("x", "zl", "y", "c")
N_DP = 128
LANES = 128

gelu_coeff = 0.044715
root_two_pi = math.sqrt(2.0 / math.pi)
f32 = jnp.float32
bf16 = jnp.bfloat16
VMEM = pl.BlockSpec(memory_space=pltpu.VMEM)
SMEM = pl.BlockSpec(memory_space=pltpu.SMEM)
ANY = pl.BlockSpec(memory_space=pl.ANY)


def shape(dims, kind):
    return jax.ShapeDtypeStruct(dims, kind)


def call(kernel, outs, ins, *args, scratch=()):
    return pl.pallas_call(
        kernel,
        out_shape=outs,
        in_specs=ins,
        out_specs=jax.tree.map(lambda _: VMEM, outs),
        scratch_shapes=list(scratch),
        compiler_params=pltpu.CompilerParams(vmem_limit_bytes=40 * 1024 * 1024),
    )(*args)


def after(value, *earlier):
    return lax.optimization_barrier((value, *earlier))[0]


def moved(value, pairs):
    return lax.ppermute(value, DP, [(s % N_DP, d % N_DP) for s, d in pairs])


def swapped(value):
    return lax.ppermute(value, "c", [(0, 1), (1, 0)])


def dot(a, b, ca, cb):
    return lax.dot_general(a, b, (((ca,), (cb,)), ((), ())), preferred_element_type=f32)


def unit_rows(rows_float):
    inverse = lax.rsqrt(jnp.sum(rows_float * rows_float, axis=-1, keepdims=True) + 1e-06)
    return (inverse, rows_float * inverse)


def head_kernel(pooled, gain, b_up, w_up, w_down, normed_out, partial, slope, up, down, sems):
    copy_up = pltpu.make_async_copy(w_up, up, sems.at[0])
    copy_down = pltpu.make_async_copy(w_down, down, sems.at[1])
    copy_up.start()
    copy_down.start()
    values = pooled[...].astype(f32)
    center = values - jnp.mean(values, axis=-1, keepdims=True)
    spread = jnp.mean(center * center, axis=-1, keepdims=True)
    normed = (center * lax.rsqrt(spread + 1e-06) * gain[...]).astype(bf16)
    normed_out[...] = normed
    copy_up.wait()
    hidden = jnp.dot(normed, up[...], preferred_element_type=f32) + b_up[...]
    square = hidden * hidden
    tanh_value = jnp.tanh(root_two_pi * (hidden + gelu_coeff * square * hidden))
    half = 0.5 * (1.0 + tanh_value)
    activation = (hidden * half).astype(bf16)
    slope[...] = half + 0.5 * hidden * (1.0 - tanh_value * tanh_value) * (
        root_two_pi * (1.0 + 3.0 * gelu_coeff * square)
    )
    copy_down.wait()
    partial[...] = jnp.dot(activation, down[...], preferred_element_type=f32).astype(bf16)


def text_kernel(text, half):
    half[...] = unit_rows(text[...].astype(f32))[1].astype(bf16)


def select_kernel(info, normed, mine, theirs):
    core = info[0]
    rows = 256
    count, width = mine.shape[0], normed.shape[1]
    normed_value = normed[...]
    for out, parity in ((mine, core), (theirs, 1 - core)):
        for start in range(0, count, rows):
            row = lax.broadcasted_iota(jnp.int32, (rows, 1), 0) + start
            chip = (row % (count // 2)) // 8
            within = jnp.where(row < count // 2, row % 8, 8)
            wanted = 18 * chip + 9 * parity + within
            feature = lax.broadcasted_iota(jnp.int32, (rows, width), 1)
            pick = jnp.where(feature == wanted, 1.0, 0.0).astype(bf16)
            out[start : start + rows, :] = dot(pick, normed_value, 1, 1).astype(bf16)


def embed_kernel(info, parts, pooled, unit, half, inverse):
    quarter = parts.shape[1]
    own = pooled[pl.ds(pl.multiple_of(info[1] * quarter, quarter), quarter), :].astype(f32)
    embedded = own + (
        (parts[0].astype(f32) + parts[1].astype(f32))
        + (parts[2].astype(f32) + parts[3].astype(f32))
    )
    inv, unit_value = unit_rows(embedded)
    unit[...] = unit_value
    half[...] = unit_value.astype(bf16)
    inverse[...] = inv


def coefficients(logits, is_pair, scale):
    small = jnp.exp(-jnp.abs(logits))
    sigmoid = jnp.where(logits >= 0, 1.0, small) / (1.0 + small)
    if is_pair is not None:
        sigmoid = sigmoid - is_pair
    return (sigmoid * (scale / WINDOW)).astype(bf16), small


def image_kernel(info, factors, unit_half, left, pair, right, far, image_part):
    core, group = info[0], info[1]
    scale, bias = factors[0], factors[1]
    images = unit_half[...]
    quarter = far.shape[0]
    total = None
    for ref in (left, pair, right, far):
        texts = ref[...]
        logits = scale * dot(images, texts, 1, 1) + bias
        is_pair = None
        if ref is pair:
            row = lax.broadcasted_iota(jnp.int32, logits.shape, 0) - group * quarter
            col = lax.broadcasted_iota(jnp.int32, logits.shape, 1) - core * quarter
            is_pair = jnp.where((row == col) & (row >= 0) & (row < quarter), 1.0, 0.0)
        coefficient, _ = coefficients(logits, is_pair, scale)
        term = dot(coefficient, texts, 1, 0)
        total = term if total is None else total + term
    image_part[...] = total.astype(bf16)


def text_part_kernel(
    info, factors, unit_half, left, pair, right, far, give, far_part, keep_side, keep_own
):
    core, group = info[0], info[1]
    scale, bias = factors[0], factors[1]
    images = unit_half[...]
    quarter = far.shape[0]
    width = images.shape[1]
    first = core == 0

    def terms(ref):
        logits = scale * dot(ref[...], images, 1, 1) + bias
        is_pair = None
        if ref is pair:
            row = lax.broadcasted_iota(jnp.int32, logits.shape, 0) - core * quarter
            col = lax.broadcasted_iota(jnp.int32, logits.shape, 1) - group * quarter
            is_pair = jnp.where((row == col) & (row >= 0) & (row < quarter), 1.0, 0.0)
        coefficient, small = coefficients(logits, is_pair, scale)
        loss = jnp.maximum(logits, 0.0) + jnp.log1p(small)
        if is_pair is not None:
            loss = loss - is_pair * logits
        loss = jnp.sum(loss, axis=1, keepdims=True)
        lane = lax.broadcasted_iota(jnp.int32, (loss.shape[0], LANES), 1)
        return dot(coefficient, images, 1, 0), jnp.where(lane == 0, loss, 0.0)

    left_terms, pair_terms, right_terms, far_terms = (terms(r) for r in (left, pair, right, far))
    for k, cols in ((0, slice(0, width)), (1, slice(width, width + LANES))):
        keep_side[:, cols] = jnp.where(first, left_terms[k], right_terms[k])
        give[: 2 * quarter, cols] = jnp.where(first, right_terms[k], left_terms[k]).astype(bf16)
        one, two = pair_terms[k][:quarter], pair_terms[k][quarter:]
        keep_own[:, cols] = jnp.where(first, one, two)
        give[2 * quarter :, cols] = jnp.where(first, two, one).astype(bf16)
        far_part[:, cols] = far_terms[k].astype(bf16)


def grad_kernel(parts, unit, inverse, grad):
    grad_sum = (parts[0].astype(f32) + parts[1].astype(f32)) + (
        parts[2].astype(f32) + parts[3].astype(f32)
    )
    unit_value = unit[...]
    radial = jnp.sum(unit_value * grad_sum, axis=-1, keepdims=True)
    grad[...] = (inverse[...] * (grad_sum - unit_value * radial)).astype(bf16)


def pre_kernel(grad_image, w_down, slope, grad_pre):
    grad_act = dot(grad_image[...], w_down[...], 1, 1)
    grad_pre[...] = (grad_act * slope[...]).astype(bf16)


def up_kernel(info, mine, got, grads, wire):
    rows = grads.shape[0] // 2
    core = info[0]
    own = grads[pl.ds(pl.multiple_of(core * rows, rows), rows), :]
    other = grads[pl.ds(pl.multiple_of((1 - core) * rows, rows), rows), :]
    count = mine.shape[0] // 2
    chips = wire.shape[0]
    main = dot(mine[:count, :], own, 1, 0) + dot(got[:count, :], other, 1, 0)
    rest = dot(mine[count:, :], own, 1, 0) + dot(got[count:, :], other, 1, 0)
    place = lax.broadcasted_iota(jnp.int32, (count, LANES), 0) % 8
    blocks = [main[:, k * LANES : (k + 1) * LANES] for k in range(5)]
    ninth = jnp.zeros((count, LANES), f32)
    for k in range(5):
        ninth = jnp.where(place == k, rest[:, k * LANES : (k + 1) * LANES], ninth)
    blocks.append(ninth)
    for k in range(3):
        both = jnp.concatenate(
            [blocks[k].reshape(chips, 8, LANES), blocks[k + 3].reshape(chips, 8, LANES)], axis=1
        )
        wire[:, :, k * LANES : (k + 1) * LANES] = both.astype(bf16)


def up_sum_kernel(terms, up_grad):
    total = jnp.sum(terms[...].astype(f32), axis=0)
    up_grad[:8, : 3 * LANES] = total[:8, :]
    up_grad[:8, 3 * LANES :] = total[8:, : 2 * LANES]
    for k in range(5):
        up_grad[8:9, k * LANES : (k + 1) * LANES] = total[8 + k : 9 + k, 2 * LANES :]


def body(pooled, ln_gain, w_up, b_up, w_down, text, logit_scale, logit_bias):
    rows_count, width = pooled.shape
    q = text.shape[0]
    units = w_up.shape[1]
    core = lax.axis_index("c")
    first = core == 0
    info = jnp.stack([core, lax.axis_index("mp")]).astype(jnp.int32)
    factors = jnp.concatenate([logit_scale, logit_bias])
    wide = width + LANES

    def mp_exchange(partial):
        return lax.all_to_all(partial.reshape(4, q, width), "mp", 0, 0, tiled=True)

    normed, partial_out, slope = call(
        head_kernel,
        (
            shape((rows_count, width), bf16),
            shape((rows_count, width), bf16),
            shape((rows_count, units), f32),
        ),
        [VMEM, VMEM, VMEM, ANY, ANY],
        pooled,
        ln_gain.reshape(1, width),
        b_up.reshape(1, units),
        w_up,
        w_down,
        scratch=(
            pltpu.VMEM(w_up.shape, bf16),
            pltpu.VMEM(w_down.shape, bf16),
            pltpu.SemaphoreType.DMA((2,)),
        ),
    )
    parts = mp_exchange(partial_out)

    text_half = call(text_kernel, shape((q, width), bf16), [VMEM], after(text, partial_out))
    pair = lax.all_gather(text_half, "c", axis=0, tiled=True)
    left = moved(pair, [(i, i + 2) for i in range(N_DP)])
    right = moved(pair, [(i, i - 2) for i in range(N_DP)])
    far_out = [(i - 3, i) if i % 2 == 0 else (i + 3, i) for i in range(N_DP)]
    far = moved(text_half, far_out)
    window = (left, pair, right, far)

    half_rows = shape((1024, rows_count), bf16)
    mine, theirs = call(select_kernel, (half_rows, half_rows), [SMEM, VMEM], info, normed)
    got_rows = swapped(theirs)

    image_unit, image_half, inverse = call(
        embed_kernel,
        (shape((q, width), f32), shape((q, width), bf16), shape((q, 1), f32)),
        [SMEM, VMEM, VMEM],
        info,
        parts,
        pooled,
    )
    unit_half = lax.all_gather(image_half, "mp", axis=0, tiled=True)

    image_part = call(
        image_kernel,
        shape((rows_count, width), bf16),
        [SMEM, SMEM] + [VMEM] * 5,
        info,
        factors,
        unit_half,
        *window,
    )
    grad_parts = mp_exchange(image_part)

    give, far_part, keep_side, keep_own = call(
        text_part_kernel,
        (
            shape((3 * q, wide), bf16),
            shape((q, wide), bf16),
            shape((2 * q, wide), f32),
            shape((q, wide), f32),
        ),
        [SMEM, SMEM] + [VMEM] * 5,
        info,
        factors,
        after(unit_half, image_part),
        *window,
    )
    got = swapped(give).astype(f32)
    side = (keep_side + got[: 2 * q]).astype(bf16)
    own_sum = keep_own + got[2 * q :]
    came = moved(side, [(i, i - 2) if i % 2 == 0 else (i, i + 2) for i in range(N_DP)])
    far_back = moved(far_part, [(d, s) for s, d in far_out])

    grad_own = call(
        grad_kernel, shape((q, width), bf16), [VMEM] * 3, grad_parts, image_unit, inverse
    )
    grad_image = lax.all_gather(grad_own, "mp", axis=0, tiled=True)
    grad_pre = call(
        pre_kernel, shape((rows_count, units), bf16), [VMEM] * 3, grad_image, w_down, slope
    )
    grads = lax.all_gather(grad_pre, "c", axis=0, tiled=True)
    up_wire = call(
        up_kernel,
        shape((N_DP // 2, 16, 3 * LANES), bf16),
        [SMEM] + [VMEM] * 3,
        info,
        mine,
        got_rows,
        grads,
    )
    up_terms = lax.all_to_all(up_wire, CHIPS, 0, 0, tiled=True)

    came = after(came, up_wire)
    came_first, came_second = came[:q], came[q:]
    last = swapped(jnp.where(first, came_second, came_first))
    total = (
        own_sum
        + jnp.where(first, came_first, came_second).astype(f32)
        + last.astype(f32)
        + far_back.astype(f32)
    )
    text_acc = total[:, :width]
    text_loss = total[:, width] / (WINDOW * rows_count)
    text_inv, text_unit = unit_rows(text.astype(f32))
    text_radial = jnp.sum(text_unit * text_acc, axis=-1, keepdims=True)
    text_grad = text_inv * (text_acc - text_unit * text_radial)

    up_grad = call(up_sum_kernel, shape((width // N_DP, units), f32), [VMEM], up_terms)
    return (up_grad, text_grad, text_loss)


def solution(mesh):
    fine = Mesh(mesh.devices.reshape(4, 2, 8, 2, 4), ("x", "zl", "y", "c", "mp"))
    every = (*DP, "mp")
    placed = (
        P(DP, None),
        P(),
        P(None, "mp"),
        P("mp"),
        P("mp", None),
        P(every, None),
        P(),
        P(),
    )
    return jax.shard_map(
        body,
        mesh=fine,
        in_specs=placed,
        out_specs=(P(DP, "mp"), P(every, None), P(every)),
        check_vma=False,
    )
```

time: 173 us -> 159 us (0.919)
  matrix products: 21.6 us -> 0 us
  Pallas kernels: 0 us -> 19 us
  other arithmetic: 18.9 us -> 5.48 us
  blocking collectives: 41.2 us -> 47.5 us
  waiting for transfers between devices: 25 us -> 19.7 us
    dot_general x9 -> x0, matrix products: 21.6 us -> none  [the longest x6 15.8 us: dot(): lax.dot_general(a, b, (((ca,), (cb,)), ((), ())), preferred_element_type=...]
    pallas_call x0 -> x10, Pallas kernels: none -> 19 us  [call(): pl.pallas_call(kernel, out_shape=outs, in_specs=ins, out_specs=jax.tree.m...]
    all_gather x1 -> x2, blocking collectives: 15.1 us -> 28.6 us  [the longest x1 19.8 us: body(): unit_half = lax.all_gather(image_half, 'mp', axis=0, tiled=True)]
    all_to_all x2, waiting for transfers between devices: 10.1 us -> 3.55 us  [mp_exchange(): return lax.all_to_all(partial.reshape(4, q, width), 'mp', 0, 0, tiled=True)]
    all_gather x1, blocking collectives: 8.53 us -> 2.61 us  [body(): pair = lax.all_gather(text_half, 'c', axis=0, tiled=True)]
    unnamed x47 -> x48, local copies, waits for them, and re-layouts: 3.96 us -> 9.56 us
    all_to_all x2, starting transfers between devices: 10.2 us -> 15.7 us  [mp_exchange(): return lax.all_to_all(partial.reshape(4, q, width), 'mp', 0, 0, tiled=True)]
    reduce_sum x6 -> x0, other arithmetic: 5.34 us -> none  [the longest x2 1.33 us: mp_sum_rows(): return jnp.sum(parts.astype(f32), axis=0)]
  transfers between devices with their start and end apart: 12 -> 11, of which waited for: 4 -> 3; matrix products, arithmetic and copies ran while one was open for 23% -> 3% of each run, Pallas kernels for 0% -> 5%
where the time goes in v2:
time: 159 us; the launch traced here: 157 us
  starting transfers between devices  51.9 us (33%)
  blocking collectives  47.5 us (30%)
  waiting for transfers between devices  19.7 us (12%)
  Pallas kernels  19 us (12%)
  local copies, waits for them, and re-layouts  11 us (7%)
  other arithmetic  5.48 us (3%)
  between operations  2.2 us (1%)
    all_gather x1, blocking collectives, body(): unit_half = lax.all_gather(image_half, 'mp', axis=0, tiled=True)  19.8 us
    pallas_call x10, Pallas kernels, call(): pl.pallas_call(kernel, out_shape=outs, in_specs=ins, out_specs=jax.tree.m...  19 us
    all_gather x1, blocking collectives, body(): grad_image = lax.all_gather(grad_own, 'mp', axis=0, tiled=True)  16.3 us
    ppermute x5, starting transfers between devices, moved(): return lax.ppermute(value, DP, [(s % N_DP, d % N_DP) for s, d in pairs])  15.8 us
    all_to_all x2, starting transfers between devices, mp_exchange(): return lax.all_to_all(partial.reshape(4, q, width), 'mp', 0, 0, tiled=True)  15.7 us
    all_to_all x1, waiting for transfers between devices, body(): up_terms = lax.all_to_all(up_wire, CHIPS, 0, 0, tiled=True)  15.1 us
    ppermute x3, starting transfers between devices, swapped(): return lax.ppermute(value, 'c', [(0, 1), (1, 0)])  12 us
    unnamed x48, local copies, waits for them, and re-layouts  9.56 us
  transfers between devices with their start and end apart: 11, of which 3 were waited for; matrix products, arithmetic and copies ran while one was open for 3% of the time, Pallas kernels for 5%

profile of v2, /device:TPU:1, one launch (start us, length us, event | category | flops | bytes accessed | tf_op | source)
XLA Modules:
  0.0 156.9 jit_solution(16581978907618794352)
XLA Ops:
  2.0 1.4 copy-done
  3.4 1.1 copy-done.3
  4.5 1.4 copy-done.5
  5.8 3.5 %shard_map.103 = (bf16[256,1152]{1,0:T(8,128)(2,1)S(1)}, bf16[256,1152]{1,0:T(8,128)(2,1)}, f32[256,640]{1,0:T(8,128)S(1)}) custom-call(bf16[256,1152]{1,0:T(8,128)(2,1)S(1)} %copy-done.3, f32[1,1152]{1,0:T(1,128)S(1)} %reshape.27.gain, f32[1,640]{1,0:T(1,128)S(1)} %reshape.28.b_up, bf16[1152,640]{1,0:T(8,128)(2,1)S(1)} %copy-done.5, ...), custom_call_target="tpu_custom_call" | custom-call | tf_op jit(solution)/shard_map/pallas_call | solution.py:31
  9.3 0.8 copy-done.6
  10.1 11.0 %all-to-all-start = ((bf16[4,64,1152]{2,1,0:T(8,128)(2,1)}), bf16[4,64,1152]{2,1,0:T(8,128)(2,1)S(1)}, u32[]{:S(2)}, u32[]{:S(2)}) async-start(bf16[4,64,1152]{2,1,0:T(8,128)(2,1)} %bitcast.2), calls=%async_computation | async-start | bytes 1179648 | tf_op jit(solution)/shard_map/all_to_all | solution.py:236
  21.2 2.6 %all_gather.13.pair = bf16[128,1152]{1,0:T(8,128)(2,1)S(1)} all-gather(bf16[64,1152]{1,0:T(8,128)(2,1)S(1)} %shard_map.106), channel_id=1, replica_groups=mesh['x'=4,'zl'=2,'y'=8,'c'=2,'mp'=4] {'c'}, dimensions={0}, use_global_device_ids=true | all-gather | bytes 442368 | tf_op jit(solution)/shard_map/all_gather | solution.py:260
  23.8 3.2 %collective-permute-start.1 = (bf16[128,1152]{1,0:T(8,128)(2,1)S(1)}, bf16[128,1152]{1,0:T(8,128)(2,1)S(1)}, u32[]{:S(2)}, u32[]{:S(2)}) collective-permute-start(bf16[128,1152]{1,0:T(8,128)(2,1)S(1)} %all_gather.13.pair), channel_id=1, source_target_pairs={{0,8},{4,12},{8,16},{12,20},{16,24},{20,28},{24,32},{28,36},{32,40... | collective-permute-start | bytes 884744 | tf_op jit(solution)/shard_map/ppermute | solution.py:46
  27.0 6.9 %collective-permute-start.2 = (bf16[128,1152]{1,0:T(8,128)(2,1)S(1)}, bf16[128,1152]{1,0:T(8,128)(2,1)S(1)}, u32[]{:S(2)}, u32[]{:S(2)}) collective-permute-start(bf16[128,1152]{1,0:T(8,128)(2,1)S(1)} %all_gather.13.pair), channel_id=1, source_target_pairs={{0,504},{4,508},{8,0},{12,4},{16,8},{20,12},{24,16},{28,20},{32,24... | collective-permute-start | bytes 884744 | tf_op jit(solution)/shard_map/ppermute | solution.py:46
  34.0 1.9 %collective-permute-start.3 = (bf16[64,1152]{1,0:T(8,128)(2,1)S(1)}, bf16[64,1152]{1,0:T(8,128)(2,1)S(1)}, u32[]{:S(2)}, u32[]{:S(2)}) collective-permute-start(bf16[64,1152]{1,0:T(8,128)(2,1)S(1)} %shard_map.106), channel_id=1, source_target_pairs={{500,0},{16,4},{508,8},{24,12},{4,16},{32,20},{12,24},{40,28},{20,... | collective-permute-start | bytes 442376 | tf_op jit(solution)/shard_map/ppermute | solution.py:46
  38.1 19.8 %all_gather.12.unit_half = bf16[256,1152]{1,0:T(8,128)(2,1)S(1)} all-gather(bf16[64,1152]{1,0:T(8,128)(2,1)S(1)} %get-tuple-element.22), channel_id=1, replica_groups=mesh['x'=4,'zl'=2,'y'=8,'c'=2,'mp'=4] {'mp'}, dimensions={0}, use_global_device_ids=true | all-gather | bytes 737280 | tf_op jit(solution)/shard_map/all_gather | solution.py:279
  57.9 3.4 %shard_map.107 = bf16[256,1152]{1,0:T(8,128)(2,1)} custom-call(s32[2]{0:T(128)S(1)} %pad_add_fusion.info, f32[2]{0:T(128)S(1)} %pad_maximum_fusion.factors, bf16[256,1152]{1,0:T(8,128)(2,1)S(1)} %all_gather.12.unit_half, bf16[128,1152]{1,0:T(8,128)(2,1)S(1)} %collective-permute-done.1.left, bf16[128,1152]{1,0:T(8,128)(2,1)S(1)} %all_gather.13.pair, ...), custom_call_target="tpu_custom_call" | custom-call | tf_op jit(solution)/shard_map/pallas_call | solution.py:31
  61.9 0.9 copy-done.9
  64.2 3.9 %shard_map.112 = (bf16[192,1280]{1,0:T(8,128)(2,1)}, bf16[64,1280]{1,0:T(8,128)(2,1)}, f32[128,1280]{1,0:T(8,128)S(1)}, f32[64,1280]{1,0:T(8,128)S(1)}) custom-call(s32[2]{0:T(128)S(1)} %copy-done.17, f32[2]{0:T(128)S(1)} %copy-done.21, bf16[256,1152]{1,0:T(8,128)(2,1)S(1)} %all_gather.12.unit_half, bf16[128,1152]{1,0:T(8,128)(2,1)S(1)} %collective-permute-done.1.left, ...), custom_call_target="tpu_custom_call" | custom-call | tf_op jit(solution)/shard_map/pallas_call | solution.py:31
  68.1 7.2 %collective-permute-start.4 = (bf16[192,1280]{1,0:T(8,128)(2,1)}, bf16[192,1280]{1,0:T(8,128)(2,1)}, u32[]{:S(2)}, u32[]{:S(2)}) collective-permute-start(bf16[192,1280]{1,0:T(8,128)(2,1)} %get-tuple-element.29), channel_id=1, source_target_pairs={{0,4},{4,0},{1,5},{5,1},{2,6},{6,2},{3,7},{7,3},{8,12},{12,8},{9,1... | collective-permute-start | bytes 1474568 | tf_op jit(solution)/shard_map/ppermute | solution.py:50
  75.3 4.7 %all-to-all-start.1 = ((bf16[4,64,1152]{2,1,0:T(8,128)(2,1)}), bf16[4,64,1152]{2,1,0:T(8,128)(2,1)S(1)}, u32[]{:S(2)}, u32[]{:S(2)}) async-start(bf16[4,64,1152]{2,1,0:T(8,128)(2,1)} %bitcast.3), calls=%async_computation.1 | async-start | bytes 1179648 | tf_op jit(solution)/shard_map/all_to_all | solution.py:236
  80.0 2.9 %shard_map.104 = (bf16[1024,256]{1,0:T(8,128)(2,1)S(1)}, bf16[1024,256]{1,0:T(8,128)(2,1)}) custom-call(s32[2]{0:T(128)S(1)} %copy-done.18, bf16[256,1152]{1,0:T(8,128)(2,1)S(1)} %copy-done.7), custom_call_target="tpu_custom_call" | custom-call | tf_op jit(solution)/shard_map/pallas_call | solution.py:31
  83.7 2.2 %collective-permute-start = (bf16[1024,256]{1,0:T(8,128)(2,1)}, bf16[1024,256]{1,0:T(8,128)(2,1)}, u32[]{:S(2)}, u32[]{:S(2)}) collective-permute-start(bf16[1024,256]{1,0:T(8,128)(2,1)} %get-tuple-element.20), channel_id=1, source_target_pairs={{0,4},{4,0},{1,5},{5,1},{2,6},{6,2},{3,7},{7,3},{8,12},{12,8},{9,1... | collective-permute-start | bytes 1572872 | tf_op jit(solution)/shard_map/ppermute | solution.py:50
  86.5 1.9 %collective-permute-start.7 = (bf16[64,1280]{1,0:T(8,128)(2,1)}, bf16[64,1280]{1,0:T(8,128)(2,1)}, u32[]{:S(2)}, u32[]{:S(2)}) collective-permute-start(bf16[64,1280]{1,0:T(8,128)(2,1)} %get-tuple-element.32), channel_id=1, source_target_pairs={{0,500},{4,16},{8,508},{12,24},{16,4},{20,32},{24,12},{28,40},{32,... | collective-permute-start | bytes 491528 | tf_op jit(solution)/shard_map/ppermute | solution.py:46
  88.4 1.1 convert_element_type.19
  90.6 1.9 %collective-permute-start.5 = (bf16[128,1280]{1,0:T(8,128)(2,1)}, bf16[128,1280]{1,0:T(8,128)(2,1)S(1)}, u32[]{:S(2)}, u32[]{:S(2)}) collective-permute-start(bf16[128,1280]{1,0:T(8,128)(2,1)} %fusion), channel_id=1, source_target_pairs={{0,504},{4,12},{8,0},{12,20},{16,8},{20,28},{24,16},{28,36},{32,24... | collective-permute-start | bytes 983048 | tf_op jit(solution)/shard_map/ppermute | solution.py:46
  92.5 3.6 %all-to-all-done.1.parts = bf16[4,64,1152]{2,1,0:T(8,128)(2,1)S(1)} async-done(((bf16[4,64,1152]{2,1,0:T(8,128)(2,1)}), bf16[4,64,1152]{2,1,0:T(8,128)(2,1)S(1)}, u32[]{:S(2)}, u32[]{:S(2)}) %all-to-all-start.1) | async-done | bytes 589856 | tf_op jit(solution)/shard_map/all_to_all | solution.py:236
  96.1 1.0 copy-done.15
  97.2 16.3 %all_gather.14.grad_image = bf16[256,1152]{1,0:T(8,128)(2,1)S(1)} all-gather(bf16[64,1152]{1,0:T(8,128)(2,1)S(1)} %shard_map.108), channel_id=1, replica_groups=mesh['x'=4,'zl'=2,'y'=8,'c'=2,'mp'=4] {'mp'}, dimensions={0}, use_global_device_ids=true | all-gather | bytes 737280 | tf_op jit(solution)/shard_map/all_gather | solution.py:315
  114.3 8.8 %all_gather.15.grads = bf16[512,640]{1,0:T(8,128)(2,1)S(1)} all-gather(bf16[256,640]{1,0:T(8,128)(2,1)S(1)} %shard_map.109), channel_id=1, replica_groups=mesh['x'=4,'zl'=2,'y'=8,'c'=2,'mp'=4] {'c'}, dimensions={0}, use_global_device_ids=true | all-gather | bytes 983040 | tf_op jit(solution)/shard_map/all_gather | solution.py:319
  123.1 2.9 %shard_map.110 = bf16[64,16,384]{2,1,0:T(8,128)(2,1)} custom-call(s32[2]{0:T(128)S(1)} %copy-done.19, bf16[1024,256]{1,0:T(8,128)(2,1)S(1)} %copy-done.11, bf16[1024,256]{1,0:T(8,128)(2,1)} %collective-permute-done.got, bf16[512,640]{1,0:T(8,128)(2,1)S(1)} %all_gather.15.grads), custom_call_target="tpu_custom_call" | custom-call | tf_op jit(solution)/shard_map/pallas_call | solution.py:31
  126.0 8.5 %all-to-all-start.2 = ((bf16[64,16,384]{2,1,0:T(8,128)(2,1)}), bf16[64,16,384]{2,1,0:T(8,128)(2,1)S(1)}, u32[]{:S(2)}, u32[]{:S(2)}) async-start(bf16[64,16,384]{2,1,0:T(8,128)(2,1)} %shard_map.110), calls=%async_computation.2 | async-start | bytes 1572864 | tf_op jit(solution)/shard_map/all_to_all | solution.py:329
  134.6 2.6 %collective-permute-start.6 = (bf16[64,1280]{1,0:T(8,128)(2,1)S(1)}, bf16[64,1280]{1,0:T(8,128)(2,1)S(1)}, u32[]{:S(2)}, u32[]{:S(2)}) collective-permute-start(bf16[64,1280]{1,0:T(8,128)(2,1)S(1)} %broadcast_select_fusion), channel_id=1, source_target_pairs={{0,4},{4,0},{1,5},{5,1},{2,6},{6,2},{3,7},{7,3},{8,12},{12,8},{9,1... | collective-permute-start | bytes 491528 | tf_op jit(solution)/shard_map/ppermute | solution.py:50
  137.2 1.0 collective-permute-done.6
  138.2 1.1 fusion.5
  140.1 0.8 fusion.8
  140.9 15.1 %all-to-all-done.2.terms = bf16[64,16,384]{2,1,0:T(8,128)(2,1)S(1)} async-done(((bf16[64,16,384]{2,1,0:T(8,128)(2,1)}), bf16[64,16,384]{2,1,0:T(8,128)(2,1)S(1)}, u32[]{:S(2)}, u32[]{:S(2)}) %all-to-all-start.2) | async-done | bytes 786464 | tf_op jit(solution)/shard_map/all_to_all | solution.py:329
  (65 shorter events, 9.4 us)
Async XLA Ops:
  2.0 1.4 copy-start
  3.4 1.1 copy-start.3
  4.5 1.4 copy-start.5
  5.8 15.3 %copy-start.2 = (bf16[64,1152]{1,0:T(8,128)(2,1)S(1)}, bf16[64,1152]{1,0:T(8,128)(2,1)}, u32[]{:S(2)}) copy-start(bf16[64,1152]{1,0:T(8,128)(2,1)} %text) | copy-start | bytes 442372
  9.3 0.8 copy-start.6
  10.1 27.2 %copy-start.4 = (bf16[256,1152]{1,0:T(8,128)(2,1)S(1)}, bf16[256,1152]{1,0:T(8,128)(2,1)}, u32[]{:S(2)}) copy-start(bf16[256,1152]{1,0:T(8,128)(2,1)} %pooled.3) | copy-start | bytes 1769476
  10.1 27.2 %all-to-all-start = ((bf16[4,64,1152]{2,1,0:T(8,128)(2,1)}), bf16[4,64,1152]{2,1,0:T(8,128)(2,1)S(1)}, u32[]{:S(2)}, u32[]{:S(2)}) async-start(bf16[4,64,1152]{2,1,0:T(8,128)(2,1)} %bitcast.2), calls=%async_computation | async-start | bytes 1179648 | tf_op jit(solution)/shard_map/all_to_all | solution.py:236
  23.8 34.0 %collective-permute-start.1 = (bf16[128,1152]{1,0:T(8,128)(2,1)S(1)}, bf16[128,1152]{1,0:T(8,128)(2,1)S(1)}, u32[]{:S(2)}, u32[]{:S(2)}) collective-permute-start(bf16[128,1152]{1,0:T(8,128)(2,1)S(1)} %all_gather.13.pair), channel_id=1, source_target_pairs={{0,8},{4,12},{8,16},{12,20},{16,24},{20,28},{24,32},{28,36},{32,40... | collective-permute-start | bytes 884744 | tf_op jit(solution)/shard_map/ppermute | solution.py:46
  27.0 30.8 %collective-permute-start.2 = (bf16[128,1152]{1,0:T(8,128)(2,1)S(1)}, bf16[128,1152]{1,0:T(8,128)(2,1)S(1)}, u32[]{:S(2)}, u32[]{:S(2)}) collective-permute-start(bf16[128,1152]{1,0:T(8,128)(2,1)S(1)} %all_gather.13.pair), channel_id=1, source_target_pairs={{0,504},{4,508},{8,0},{12,4},{16,8},{20,12},{24,16},{28,20},{32,24... | collective-permute-start | bytes 884744 | tf_op jit(solution)/shard_map/ppermute | solution.py:46
  34.0 23.9 %collective-permute-start.3 = (bf16[64,1152]{1,0:T(8,128)(2,1)S(1)}, bf16[64,1152]{1,0:T(8,128)(2,1)S(1)}, u32[]{:S(2)}, u32[]{:S(2)}) collective-permute-start(bf16[64,1152]{1,0:T(8,128)(2,1)S(1)} %shard_map.106), channel_id=1, source_target_pairs={{500,0},{16,4},{508,8},{24,12},{4,16},{32,20},{12,24},{40,28},{20,... | collective-permute-start | bytes 442376 | tf_op jit(solution)/shard_map/ppermute | solution.py:46
  37.3 20.6 %copy-start.16 = (s32[2]{0:T(128)}, s32[2]{0:T(128)S(1)}, u32[]{:S(2)}) copy-start(s32[2]{0:T(128)S(1)} %pad_add_fusion.info) | copy-start | bytes 28
  37.3 20.6 %copy-start.20 = (f32[2]{0:T(128)}, f32[2]{0:T(128)S(1)}, u32[]{:S(2)}) copy-start(f32[2]{0:T(128)S(1)} %pad_maximum_fusion.factors) | copy-start | bytes 28
  38.1 19.8 %copy-start.14 = (f32[64,1152]{1,0:T(8,128)}, f32[64,1152]{1,0:T(8,128)S(1)}, u32[]{:S(2)}) copy-start(f32[64,1152]{1,0:T(8,128)S(1)} %get-tuple-element.24.unit) | copy-start | bytes 884740
  61.9 0.9 copy-start.9
  64.2 15.8 %copy-start.7 = (bf16[256,1152]{1,0:T(8,128)(2,1)S(1)}, bf16[256,1152]{1,0:T(8,128)(2,1)}, u32[]{:S(2)}) copy-start(bf16[256,1152]{1,0:T(8,128)(2,1)} %copy-done.6) | copy-start | bytes 1769476
  64.2 15.8 %copy-start.18 = (s32[2]{0:T(128)S(1)}, s32[2]{0:T(128)}, u32[]{:S(2)}) copy-start(s32[2]{0:T(128)} %copy-done.16) | copy-start | bytes 28
  68.1 21.5 %copy-start.12 = (f32[64,1280]{1,0:T(8,128)}, f32[64,1280]{1,0:T(8,128)S(1)}, u32[]{:S(2)}) copy-start(f32[64,1280]{1,0:T(8,128)S(1)} %get-tuple-element.28) | copy-start | bytes 983044
  68.1 20.4 %collective-permute-start.4 = (bf16[192,1280]{1,0:T(8,128)(2,1)}, bf16[192,1280]{1,0:T(8,128)(2,1)}, u32[]{:S(2)}, u32[]{:S(2)}) collective-permute-start(bf16[192,1280]{1,0:T(8,128)(2,1)} %get-tuple-element.29), channel_id=1, source_target_pairs={{0,4},{4,0},{1,5},{5,1},{2,6},{6,2},{3,7},{7,3},{8,12},{12,8},{9,1... | collective-permute-start | bytes 1474568 | tf_op jit(solution)/shard_map/ppermute | solution.py:50
  75.3 20.8 %all-to-all-start.1 = ((bf16[4,64,1152]{2,1,0:T(8,128)(2,1)}), bf16[4,64,1152]{2,1,0:T(8,128)(2,1)S(1)}, u32[]{:S(2)}, u32[]{:S(2)}) async-start(bf16[4,64,1152]{2,1,0:T(8,128)(2,1)} %bitcast.3), calls=%async_computation.1 | async-start | bytes 1179648 | tf_op jit(solution)/shard_map/all_to_all | solution.py:236
  82.9 0.8 copy-start.10
  83.7 39.4 %collective-permute-start = (bf16[1024,256]{1,0:T(8,128)(2,1)}, bf16[1024,256]{1,0:T(8,128)(2,1)}, u32[]{:S(2)}, u32[]{:S(2)}) collective-permute-start(bf16[1024,256]{1,0:T(8,128)(2,1)} %get-tuple-element.20), channel_id=1, source_target_pairs={{0,4},{4,0},{1,5},{5,1},{2,6},{6,2},{3,7},{7,3},{8,12},{12,8},{9,1... | collective-permute-start | bytes 1572872 | tf_op jit(solution)/shard_map/ppermute | solution.py:50
  86.5 50.7 %collective-permute-start.7 = (bf16[64,1280]{1,0:T(8,128)(2,1)}, bf16[64,1280]{1,0:T(8,128)(2,1)}, u32[]{:S(2)}, u32[]{:S(2)}) collective-permute-start(bf16[64,1280]{1,0:T(8,128)(2,1)} %get-tuple-element.32), channel_id=1, source_target_pairs={{0,500},{4,16},{8,508},{12,24},{16,4},{20,32},{24,12},{28,40},{32,... | collective-permute-start | bytes 491528 | tf_op jit(solution)/shard_map/ppermute | solution.py:46
  89.5 1.1 copy-start.22
  89.5 24.0 %copy-start.1 = (bf16[640,1152]{1,0:T(8,128)(2,1)S(1)}, bf16[640,1152]{1,0:T(8,128)(2,1)}, u32[]{:S(2)}) copy-start(bf16[640,1152]{1,0:T(8,128)(2,1)} %w_down.3) | copy-start | bytes 4423684
  90.6 43.9 %collective-permute-start.5 = (bf16[128,1280]{1,0:T(8,128)(2,1)}, bf16[128,1280]{1,0:T(8,128)(2,1)S(1)}, u32[]{:S(2)}, u32[]{:S(2)}) collective-permute-start(bf16[128,1280]{1,0:T(8,128)(2,1)} %fusion), channel_id=1, source_target_pairs={{0,504},{4,12},{8,0},{12,20},{16,8},{20,28},{24,16},{28,36},{32,24... | collective-permute-start | bytes 983048 | tf_op jit(solution)/shard_map/ppermute | solution.py:46
  96.1 1.0 copy-start.15
  113.6 9.5 %copy-start.11 = (bf16[1024,256]{1,0:T(8,128)(2,1)S(1)}, bf16[1024,256]{1,0:T(8,128)(2,1)}, u32[]{:S(2)}) copy-start(bf16[1024,256]{1,0:T(8,128)(2,1)} %copy-done.10) | copy-start | bytes 1572868
  113.6 9.5 %copy-start.19 = (s32[2]{0:T(128)S(1)}, s32[2]{0:T(128)}, u32[]{:S(2)}) copy-start(s32[2]{0:T(128)} %copy-done.16) | copy-start | bytes 28
  126.0 11.1 %copy-start.23 = (f32[64]{0:T(128)S(1)}, f32[64]{0:T(128)}, u32[]{:S(2)}) copy-start(f32[64]{0:T(128)} %fusion.9) | copy-start | bytes 772
  126.0 12.1 %copy-start.13 = (f32[64,1280]{1,0:T(8,128)S(1)}, f32[64,1280]{1,0:T(8,128)}, u32[]{:S(2)}) copy-start(f32[64,1280]{1,0:T(8,128)} %copy-done.12) | copy-start | bytes 983044
  126.0 30.0 %all-to-all-start.2 = ((bf16[64,16,384]{2,1,0:T(8,128)(2,1)}), bf16[64,16,384]{2,1,0:T(8,128)(2,1)S(1)}, u32[]{:S(2)}, u32[]{:S(2)}) async-start(bf16[64,16,384]{2,1,0:T(8,128)(2,1)} %shard_map.110), calls=%async_computation.2 | async-start | bytes 1572864 | tf_op jit(solution)/shard_map/all_to_all | solution.py:329
  134.6 3.6 %collective-permute-start.6 = (bf16[64,1280]{1,0:T(8,128)(2,1)S(1)}, bf16[64,1280]{1,0:T(8,128)(2,1)S(1)}, u32[]{:S(2)}, u32[]{:S(2)}) collective-permute-start(bf16[64,1280]{1,0:T(8,128)(2,1)S(1)} %broadcast_select_fusion), channel_id=1, source_target_pairs={{0,4},{4,0},{1,5},{5,1},{2,6},{6,2},{3,7},{7,3},{8,12},{12,8},{9,1... | collective-permute-start | bytes 491528 | tf_op jit(solution)/shard_map/ppermute | solution.py:50
  (3 other events, 2.0 us)

commit v3 on v2

v3 whole, which is shorter than its diff:
```python
import math

import jax
import jax.numpy as jnp
from jax import lax
from jax.experimental import pallas as pl
from jax.experimental.pallas import tpu as pltpu
from jax.sharding import Mesh, PartitionSpec as P

REACH = 3
WINDOW = 2 * REACH + 1
CHIPS = ("x", "zl", "y")
DP = ("x", "zl", "y", "c")
N_DP = 128
LANES = 128

gelu_coeff = 0.044715
root_two_pi = math.sqrt(2.0 / math.pi)
f32 = jnp.float32
bf16 = jnp.bfloat16
VMEM = pl.BlockSpec(memory_space=pltpu.VMEM)
SMEM = pl.BlockSpec(memory_space=pltpu.SMEM)
HBM = pl.BlockSpec(memory_space=pltpu.HBM)


def shape(dims, kind):
    return jax.ShapeDtypeStruct(dims, kind)


def call(kernel, outs, ins, *args, scratch=(), specs=None):
    return pl.pallas_call(
        kernel,
        out_shape=outs,
        in_specs=ins,
        out_specs=specs if specs is not None else jax.tree.map(lambda _: VMEM, outs),
        scratch_shapes=list(scratch),
        cost_estimate=pl.CostEstimate(flops=1, transcendentals=0, bytes_accessed=1),
        compiler_params=pltpu.CompilerParams(vmem_limit_bytes=20 * 1024 * 1024),
    )(*args)


def copied(sems, *pairs):
    copies = [pltpu.make_async_copy(a, b, sems.at[k]) for k, (a, b) in enumerate(pairs)]
    for copy in copies:
        copy.start()
    return copies


def in_hbm(value):
    return pltpu.with_memory_space_constraint(value, pltpu.HBM)


def after(value, *earlier):
    return lax.optimization_barrier((value, *earlier))[0]


def moved(value, pairs):
    return lax.ppermute(value, DP, [(s % N_DP, d % N_DP) for s, d in pairs])


def swapped(value):
    return lax.ppermute(value, "c", [(0, 1), (1, 0)])


def dot(a, b, ca, cb):
    return lax.dot_general(a, b, (((ca,), (cb,)), ((), ())), preferred_element_type=f32)


def unit_rows(rows_float):
    inverse = lax.rsqrt(jnp.sum(rows_float * rows_float, axis=-1, keepdims=True) + 1e-06)
    return (inverse, rows_float * inverse)


def head_kernel(
    info, pooled_in, gain_in, b_up_in, w_up, w_down, normed_out, own, partial, hidden_out,
    pooled, gain, b_up, up, down, normed, hidden, held, sems,
):
    loads = copied(
        sems, (pooled_in, pooled), (gain_in, gain), (b_up_in, b_up), (w_up, up), (w_down, down)
    )
    loads[0].wait()
    loads[1].wait()
    rows, width = pooled.shape
    quarter = own.shape[0]
    own[...] = pooled[pl.ds(pl.multiple_of(info[1] * quarter, quarter), quarter), :]
    values = pooled[...].astype(f32)
    center = values - jnp.mean(values, axis=-1, keepdims=True)
    spread = jnp.mean(center * center, axis=-1, keepdims=True)
    normed[...] = (center * lax.rsqrt(spread + 1e-06) * gain[...].reshape(1, width)).astype(bf16)
    store_normed = pltpu.make_async_copy(normed, normed_out, sems.at[5])
    store_normed.start()
    loads[2].wait()
    loads[3].wait()
    bias = b_up[...].reshape(1, b_up.shape[0])
    pre = jnp.dot(normed[...], up[...], preferred_element_type=f32) + bias
    hidden[...] = pre
    store_hidden = pltpu.make_async_copy(hidden, hidden_out, sems.at[6])
    store_hidden.start()
    tanh_value = jnp.tanh(root_two_pi * (pre + gelu_coeff * pre * pre * pre))
    activation = (0.5 * pre * (1.0 + tanh_value)).astype(bf16)
    loads[4].wait()
    held[...] = jnp.dot(activation, down[...], preferred_element_type=f32).astype(bf16)
    store = pltpu.make_async_copy(held, partial, sems.at[7])
    store.start()
    store_normed.wait()
    store_hidden.wait()
    store.wait()


def text_kernel(text, half):
    half[...] = unit_rows(text[...].astype(f32))[1].astype(bf16)


def select_kernel(info, normed, hidden, mine, theirs, slope_out, slope, sems):
    pre = hidden[...]
    square = pre * pre
    tanh_value = jnp.tanh(root_two_pi * (pre + gelu_coeff * square * pre))
    slope[...] = 0.5 * (1.0 + tanh_value) + 0.5 * pre * (1.0 - tanh_value * tanh_value) * (
        root_two_pi * (1.0 + 3.0 * gelu_coeff * square)
    )
    store = copied(sems, (slope, slope_out))[0]
    core = info[0]
    rows = 256
    count, width = mine.shape[0], normed.shape[1]
    normed_value = normed[...]
    for out, parity in ((mine, core), (theirs, 1 - core)):
        for start in range(0, count, rows):
            row = lax.broadcasted_iota(jnp.int32, (rows, 1), 0) + start
            chip = (row % (count // 2)) // 8
            within = jnp.where(row < count // 2, row % 8, 8)
            wanted = 18 * chip + 9 * parity + within
            feature = lax.broadcasted_iota(jnp.int32, (rows, width), 1)
            pick = jnp.where(feature == wanted, 1.0, 0.0).astype(bf16)
            out[start : start + rows, :] = dot(pick, normed_value, 1, 1).astype(bf16)
    store.wait()


def embed_kernel(parts, own, embedded_out, half_out, half, held, sems):
    embedded = own[...].astype(f32) + (
        (parts[0].astype(f32) + parts[1].astype(f32))
        + (parts[2].astype(f32) + parts[3].astype(f32))
    )
    half[...] = unit_rows(embedded)[1].astype(bf16)
    held[...] = embedded
    stores = copied(
        sems, *[(half, half_out.at[k]) for k in range(4)], (held, embedded_out)
    )
    for store in stores:
        store.wait()


def window_kernel(side_zero, pair, side_one, far, texts):
    count = pair.shape[0]
    texts[:count, :] = side_zero[...]
    texts[count : 2 * count, :] = pair[...]
    texts[2 * count : 3 * count, :] = side_one[...]
    texts[3 * count :, :] = far[...]


def positives(dims, image_dim, info, quarter):
    image = lax.broadcasted_iota(jnp.int32, dims, image_dim) - info[1] * quarter
    text = lax.broadcasted_iota(jnp.int32, dims, 1 - image_dim) - (2 + info[0]) * quarter
    return jnp.where((image == text) & (image >= 0) & (image < quarter), 1.0, 0.0)


def coefficients(logits, is_pair, scale):
    small = jnp.exp(-jnp.abs(logits))
    sigmoid = jnp.where(logits >= 0, 1.0, small) / (1.0 + small)
    return ((sigmoid - is_pair) * (scale / WINDOW)).astype(bf16), small


def image_kernel(info, factors, unit_half, texts, image_part, held, sems):
    scale, bias = factors[0], factors[1]
    quarter = texts.shape[0] // WINDOW
    window = texts[...]
    logits = scale * dot(unit_half[...], window, 1, 1) + bias
    is_pair = positives(logits.shape, 0, info, quarter)
    coefficient, _ = coefficients(logits, is_pair, scale)
    held[...] = dot(coefficient, window, 1, 0).astype(bf16)
    copied(sems, (held, image_part))[0].wait()


def text_part_kernel(info, factors, unit_half, texts, give, far_part, keep_side, keep_own):
    scale, bias = factors[0], factors[1]
    images = unit_half[...]
    q = texts.shape[0] // WINDOW
    width = images.shape[1]
    first = info[0] == 0
    logits = scale * dot(texts[...], images, 1, 1) + bias
    is_pair = positives(logits.shape, 1, info, q)
    coefficient, small = coefficients(logits, is_pair, scale)
    loss = jnp.maximum(logits, 0.0) + jnp.log1p(small) - is_pair * logits
    loss = jnp.sum(loss, axis=1, keepdims=True)
    lane = lax.broadcasted_iota(jnp.int32, (loss.shape[0], LANES), 1)
    for terms, cols in (
        (dot(coefficient, images, 1, 0), slice(0, width)),
        (jnp.where(lane == 0, loss, 0.0), slice(width, width + LANES)),
    ):
        left, right = terms[: 2 * q], terms[4 * q : 6 * q]
        one, two = terms[2 * q : 3 * q], terms[3 * q : 4 * q]
        keep_side[:, cols] = jnp.where(first, left, right)
        give[: 2 * q, cols] = jnp.where(first, right, left).astype(bf16)
        keep_own[:, cols] = jnp.where(first, one, two)
        give[2 * q :, cols] = jnp.where(first, two, one).astype(bf16)
        far_part[:, cols] = terms[6 * q :].astype(bf16)


def grad_kernel(parts, embedded_in, grad_out, embedded, grad, sems):
    load = copied(sems, (embedded_in, embedded))[0]
    grad_sum = (parts[0].astype(f32) + parts[1].astype(f32)) + (
        parts[2].astype(f32) + parts[3].astype(f32)
    )
    load.wait()
    inverse, unit_value = unit_rows(embedded[...])
    radial = jnp.sum(unit_value * grad_sum, axis=-1, keepdims=True)
    grad[...] = (inverse * (grad_sum - unit_value * radial)).astype(bf16)
    stores = copied(sems, *[(grad, grad_out.at[k]) for k in range(4)])
    for store in stores:
        store.wait()


def pre_kernel(grad_image, w_down, slope_in, grad_pre, slope, sems):
    load = copied(sems, (slope_in, slope))[0]
    grad_act = dot(grad_image[...], w_down[...], 1, 1)
    load.wait()
    grad_pre[...] = (grad_act * slope[...]).astype(bf16)


def up_kernel(info, mine, got, grads, wire):
    rows = grads.shape[0] // 2
    core = info[0]
    own = grads[pl.ds(pl.multiple_of(core * rows, rows), rows), :]
    other = grads[pl.ds(pl.multiple_of((1 - core) * rows, rows), rows), :]
    count = mine.shape[0] // 2
    chips = wire.shape[0]
    main = dot(mine[:count, :], own, 1, 0) + dot(got[:count, :], other, 1, 0)
    rest = dot(mine[count:, :], own, 1, 0) + dot(got[count:, :], other, 1, 0)
    place = lax.broadcasted_iota(jnp.int32, (count, LANES), 0) % 8
    blocks = [main[:, k * LANES : (k + 1) * LANES] for k in range(5)]
    ninth = jnp.zeros((count, LANES), f32)
    for k in range(5):
        ninth = jnp.where(place == k, rest[:, k * LANES : (k + 1) * LANES], ninth)
    blocks.append(ninth)
    for k in range(3):
        both = jnp.concatenate(
            [blocks[k].reshape(chips, 8, LANES), blocks[k + 3].reshape(chips, 8, LANES)], axis=1
        )
        wire[:, :, k * LANES : (k + 1) * LANES] = both.astype(bf16)


def up_sum_kernel(terms, up_grad):
    total = jnp.sum(terms[...].astype(f32), axis=0)
    up_grad[:8, : 3 * LANES] = total[:8, :]
    up_grad[:8, 3 * LANES :] = total[8:, : 2 * LANES]
    for k in range(5):
        up_grad[8:9, k * LANES : (k + 1) * LANES] = total[8 + k : 9 + k, 2 * LANES :]


def body(pooled, ln_gain, w_up, b_up, w_down, text, logit_scale, logit_bias):
    rows_count, width = pooled.shape
    q = text.shape[0]
    units = w_up.shape[1]
    core = lax.axis_index("c")
    first = core == 0
    info = jnp.stack([core, lax.axis_index("mp")]).astype(jnp.int32)
    factors = jnp.concatenate([logit_scale, logit_bias])
    wide = width + LANES

    def mp_exchange(partial):
        return lax.all_to_all(partial.reshape(4, q, width), "mp", 0, 0, tiled=True)

    whole = pltpu.HBM((rows_count, width), bf16)
    copies = pltpu.HBM((4, q, width), bf16)
    sems = pltpu.SemaphoreType.DMA((8,))

    normed, own, partial_out, hidden = call(
        head_kernel,
        (
            pltpu.HBM((rows_count, width), bf16),
            shape((q, width), bf16),
            pltpu.HBM((rows_count, width), bf16),
            pltpu.HBM((rows_count, units), f32),
        ),
        [SMEM] + [HBM] * 5,
        info,
        *(in_hbm(a) for a in (pooled, ln_gain, b_up, w_up, w_down)),
        specs=(HBM, VMEM, HBM, HBM),
        scratch=(
            pltpu.VMEM(pooled.shape, bf16),
            pltpu.VMEM((width,), f32),
            pltpu.VMEM((units,), f32),
            pltpu.VMEM(w_up.shape, bf16),
            pltpu.VMEM(w_down.shape, bf16),
            pltpu.VMEM(pooled.shape, bf16),
            pltpu.VMEM((rows_count, units), f32),
            pltpu.VMEM(pooled.shape, bf16),
            sems,
        ),
    )
    parts = mp_exchange(partial_out)

    text_half = call(text_kernel, shape((q, width), bf16), [VMEM], after(text, partial_out))
    pair = lax.all_gather(text_half, "c", axis=0, tiled=True)
    side_in = moved(pair, [(i, i + 2) if i % 2 == 0 else (i, i - 2) for i in range(N_DP)])
    far_out = [(i - 3, i) if i % 2 == 0 else (i + 3, i) for i in range(N_DP)]
    far = moved(text_half, far_out)

    embedded, image_half = call(
        embed_kernel,
        (pltpu.HBM((q, width), f32), copies),
        [VMEM, VMEM],
        parts,
        own,
        specs=(HBM, HBM),
        scratch=(pltpu.VMEM((q, width), bf16), pltpu.VMEM((q, width), f32), sems),
    )
    unit_half = mp_exchange(image_half).reshape(rows_count, width)

    sides = lax.all_gather(after(side_in, image_half), "c", axis=0, tiled=True)
    texts = call(
        window_kernel,
        shape((WINDOW * q, width), bf16),
        [VMEM] * 4,
        sides[: 2 * q],
        pair,
        sides[2 * q :],
        far,
    )

    half_rows = shape((1024, rows_count), bf16)
    mine, theirs, slope = call(
        select_kernel,
        (half_rows, half_rows, pltpu.HBM((rows_count, units), f32)),
        [SMEM, VMEM, VMEM],
        info,
        after(normed, image_half),
        hidden,
        specs=(VMEM, VMEM, HBM),
        scratch=(pltpu.VMEM((rows_count, units), f32), sems),
    )
    got_rows = swapped(theirs)
    texts = after(texts, theirs)

    image_part = call(
        image_kernel,
        whole,
        [SMEM, SMEM, VMEM, VMEM],
        info,
        factors,
        unit_half,
        texts,
        specs=HBM,
        scratch=(pltpu.VMEM((rows_count, width), bf16), sems),
    )
    grad_parts = mp_exchange(image_part)

    give, far_part, keep_side, keep_own = call(
        text_part_kernel,
        (
            shape((3 * q, wide), bf16),
            shape((q, wide), bf16),
            shape((2 * q, wide), f32),
            shape((q, wide), f32),
        ),
        [SMEM, SMEM, VMEM, VMEM],
        info,
        factors,
        after(unit_half, image_part),
        texts,
    )
    got = swapped(give).astype(f32)
    side = (keep_side + got[: 2 * q]).astype(bf16)
    own_sum = keep_own + got[2 * q :]

    grad_own = call(
        grad_kernel,
        copies,
        [VMEM, HBM],
        grad_parts,
        in_hbm(embedded),
        specs=HBM,
        scratch=(pltpu.VMEM((q, width), f32), pltpu.VMEM((q, width), bf16), sems),
    )
    grad_image = mp_exchange(grad_own).reshape(rows_count, width)
    side = after(side, grad_own)
    came = moved(side, [(i, i - 2) if i % 2 == 0 else (i, i + 2) for i in range(N_DP)])
    far_back = moved(after(far_part, grad_own), [(d, s) for s, d in far_out])

    grad_pre = call(
        pre_kernel,
        shape((rows_count, units), bf16),
        [VMEM, VMEM, HBM],
        grad_image,
        w_down,
        in_hbm(slope),
        scratch=(pltpu.VMEM((rows_count, units), f32), sems),
    )
    grads = lax.all_gather(grad_pre, "c", axis=0, tiled=True)
    up_wire = call(
        up_kernel,
        shape((N_DP // 2, 16, 3 * LANES), bf16),
        [SMEM] + [VMEM] * 3,
        info,
        mine,
        got_rows,
        grads,
    )
    up_terms = lax.all_to_all(up_wire, CHIPS, 0, 0, tiled=True)

    came = after(came, up_wire)
    came_first, came_second = came[:q], came[q:]
    last = swapped(jnp.where(first, came_second, came_first))
    total = (
        own_sum
        + jnp.where(first, came_first, came_second).astype(f32)
        + last.astype(f32)
        + far_back.astype(f32)
    )
    text_acc = total[:, :width]
    text_loss = total[:, width] / (WINDOW * rows_count)
    text_inv, text_unit = unit_rows(text.astype(f32))
    text_radial = jnp.sum(text_unit * text_acc, axis=-1, keepdims=True)
    text_grad = text_inv * (text_acc - text_unit * text_radial)

    up_grad = call(up_sum_kernel, shape((width // N_DP, units), f32), [VMEM], up_terms)
    return (up_grad, text_grad, text_loss)


def solution(mesh):
    fine = Mesh(mesh.devices.reshape(4, 2, 8, 2, 4), ("x", "zl", "y", "c", "mp"))
    every = (*DP, "mp")
    placed = (
        P(DP, None),
        P(),
        P(None, "mp"),
        P("mp"),
        P("mp", None),
        P(every, None),
        P(),
        P(),
    )
    return jax.shard_map(
        body,
        mesh=fine,
        in_specs=placed,
        out_specs=(P(DP, "mp"), P(every, None), P(every)),
        check_vma=False,
    )
```

time: 159 us -> 147 us (0.925)
  the two profiles are of different devices: /device:TPU:1 before, /device:TPU:136 now
where the time goes in v3:
time: 147 us; the launch traced here: 146 us
  starting transfers between devices  68.1 us (46%)
  waiting for transfers between devices  38.7 us (26%)
  Pallas kernels  22.7 us (15%)
  blocking collectives  6.72 us (5%)
  other arithmetic  5.02 us (3%)
  local copies, waits for them, and re-layouts  2.36 us (2%)
  between operations  2.19 us (1%)
    all_to_all x4, starting transfers between devices, mp_exchange(): return lax.all_to_all(partial.reshape(4, q, width), 'mp', 0, 0, tiled=True)  25.6 us
    pallas_call x11, Pallas kernels, call(): pl.pallas_call(kernel, out_shape=outs, in_specs=ins, out_specs=specs if s...  22.7 us
    ppermute x4, starting transfers between devices, moved(): return lax.ppermute(value, DP, [(s % N_DP, d % N_DP) for s, d in pairs])  22.6 us
    all_to_all x4, waiting for transfers between devices, mp_exchange(): return lax.all_to_all(partial.reshape(4, q, width), 'mp', 0, 0, tiled=True)  19.4 us
    all_to_all x1, waiting for transfers between devices, body(): up_terms = lax.all_to_all(up_wire, CHIPS, 0, 0, tiled=True)  18 us
    all_to_all x1, starting transfers between devices, body(): up_terms = lax.all_to_all(up_wire, CHIPS, 0, 0, tiled=True)  14 us
    ppermute x3, starting transfers between devices, swapped(): return lax.ppermute(value, 'c', [(0, 1), (1, 0)])  5.87 us
  transfers between devices with their start and end apart: 12, of which 4 were waited for; matrix products, arithmetic and copies ran while one was open for 3% of the time, Pallas kernels for 10%

profile of v3, /device:TPU:136, one launch (start us, length us, event | category | flops | bytes accessed | tf_op | source)
XLA Modules:
  0.0 145.8 jit_solution(11136401687927890413)
XLA Ops:
  0.7 4.5 %shard_map.103 = (bf16[256,1152]{1,0:T(8,128)(2,1)}, bf16[64,1152]{1,0:T(8,128)(2,1)S(1)}, bf16[256,1152]{1,0:T(8,128)(2,1)}, f32[256,640]{1,0:T(8,128)}) custom-call(s32[2]{0:T(128)S(1)} %pad_add_fusion.info, bf16[256,1152]{1,0:T(8,128)(2,1)} %pooled_in.1, f32[1152]{0:T(1024)} %gain_in.1, f32[640]{0:T(1024)} %b_up_in.1, bf16[1152,640]{1,0:T(8,128)(2,1)} %w_up.1, ...), custom_call_target="tpu_custom_call" | custom-call | flops 1 | bytes 1 | tf_op jit(solution)/shard_map/pallas_call | solution.py:31
  5.2 9.1 %all-to-all-start = ((bf16[4,64,1152]{2,1,0:T(8,128)(2,1)}), bf16[4,64,1152]{2,1,0:T(8,128)(2,1)S(1)}, u32[]{:S(2)}, u32[]{:S(2)}) async-start(bf16[4,64,1152]{2,1,0:T(8,128)(2,1)} %bitcast.10), calls=%async_computation | async-start | bytes 1179648 | tf_op jit(solution)/shard_map/all_to_all | solution.py:270
  14.4 2.0 %all_gather.9.pair = bf16[128,1152]{1,0:T(8,128)(2,1)S(1)} all-gather(bf16[64,1152]{1,0:T(8,128)(2,1)S(1)} %shard_map.106), channel_id=1, replica_groups=mesh['x'=4,'zl'=2,'y'=8,'c'=2,'mp'=4] {'c'}, dimensions={0}, use_global_device_ids=true | all-gather | bytes 442368 | tf_op jit(solution)/shard_map/all_gather | solution.py:303
  16.4 3.5 %collective-permute-start.1 = (bf16[128,1152]{1,0:T(8,128)(2,1)S(1)}, bf16[128,1152]{1,0:T(8,128)(2,1)}, u32[]{:S(2)}, u32[]{:S(2)}) collective-permute-start(bf16[128,1152]{1,0:T(8,128)(2,1)S(1)} %all_gather.9.pair), channel_id=1, source_target_pairs={{0,8},{4,508},{8,16},{12,4},{16,24},{20,12},{24,32},{28,20},{32,40... | collective-permute-start | bytes 884744 | tf_op jit(solution)/shard_map/ppermute | solution.py:58
  19.9 10.9 %all-to-all-done.parts = bf16[4,64,1152]{2,1,0:T(8,128)(2,1)S(1)} async-done(((bf16[4,64,1152]{2,1,0:T(8,128)(2,1)}), bf16[4,64,1152]{2,1,0:T(8,128)(2,1)S(1)}, u32[]{:S(2)}, u32[]{:S(2)}) %all-to-all-start) | async-done | bytes 589856 | tf_op jit(solution)/shard_map/all_to_all | solution.py:270
  30.7 1.2 shard_map.104
  31.9 4.4 %all-to-all-start.1 = ((bf16[4,64,1152]{2,1,0:T(8,128)(2,1)}), bf16[4,64,1152]{2,1,0:T(8,128)(2,1)S(1)}, u32[]{:S(2)}, u32[]{:S(2)}) async-start(bf16[4,64,1152]{2,1,0:T(8,128)(2,1)} %get-tuple-element.27), calls=%async_computation.1 | async-start | bytes 1179648 | tf_op jit(solution)/shard_map/all_to_all | solution.py:270
  36.3 9.5 %collective-permute-start.2 = (bf16[64,1152]{1,0:T(8,128)(2,1)S(1)}, bf16[64,1152]{1,0:T(8,128)(2,1)S(1)}, u32[]{:S(2)}, u32[]{:S(2)}) collective-permute-start(bf16[64,1152]{1,0:T(8,128)(2,1)S(1)} %shard_map.106), channel_id=1, source_target_pairs={{500,0},{16,4},{508,8},{24,12},{4,16},{32,20},{12,24},{40,28},{20,... | collective-permute-start | bytes 442376 | tf_op jit(solution)/shard_map/ppermute | solution.py:58
  47.1 2.4 %all_gather.10 = bf16[256,1152]{1,0:T(8,128)(2,1)S(1)} all-gather(bf16[128,1152]{1,0:T(8,128)(2,1)} %collective-permute-done.1), channel_id=1, replica_groups=mesh['x'=4,'zl'=2,'y'=8,'c'=2,'mp'=4] {'c'}, dimensions={0}, use_global_device_ids=true | all-gather | bytes 884736 | tf_op jit(solution)/shard_map/all_gather | solution.py:319
  49.6 3.7 %shard_map.105 = (bf16[1024,256]{1,0:T(8,128)(2,1)S(1)}, bf16[1024,256]{1,0:T(8,128)(2,1)S(1)}, f32[256,640]{1,0:T(8,128)}) custom-call(s32[2]{0:T(128)S(1)} %pad_add_fusion.info, bf16[256,1152]{1,0:T(8,128)(2,1)S(1)} %copy-done.3, f32[256,640]{1,0:T(8,128)S(1)} %copy-done.2), custom_call_target="tpu_custom_call" | custom-call | flops 1 | bytes 1 | tf_op jit(solution)/shard_map/pallas_call | solution.py:31
  54.2 2.6 %shard_map.108 = bf16[256,1152]{1,0:T(8,128)(2,1)} custom-call(s32[2]{0:T(128)S(1)} %pad_add_fusion.info, f32[2]{0:T(128)S(1)} %pad_maximum_fusion.factors, bf16[256,1152]{1,0:T(8,128)(2,1)S(1)} %bitcast.6, bf16[448,1152]{1,0:T(8,128)(2,1)S(1)} %shard_map.107.texts), custom_call_target="tpu_custom_call" | custom-call | flops 1 | bytes 1 | tf_op jit(solution)/shard_map/pallas_call | solution.py:31
  56.8 7.2 %all-to-all-start.2 = ((bf16[4,64,1152]{2,1,0:T(8,128)(2,1)}), bf16[4,64,1152]{2,1,0:T(8,128)(2,1)S(1)}, u32[]{:S(2)}, u32[]{:S(2)}) async-start(bf16[4,64,1152]{2,1,0:T(8,128)(2,1)} %bitcast.9), calls=%async_computation.2 | async-start | bytes 1179648 | tf_op jit(solution)/shard_map/all_to_all | solution.py:270
  64.0 3.0 %shard_map.113 = (bf16[192,1280]{1,0:T(8,128)(2,1)}, bf16[64,1280]{1,0:T(8,128)(2,1)S(1)}, f32[128,1280]{1,0:T(8,128)S(1)}, f32[64,1280]{1,0:T(8,128)S(1)}) custom-call(s32[2]{0:T(128)S(1)} %pad_add_fusion.info, f32[2]{0:T(128)S(1)} %pad_maximum_fusion.factors, bf16[256,1152]{1,0:T(8,128)(2,1)S(1)} %bitcast.7, bf16[448,1152]{1,0:T(8,128)(2,1)S(1)} %shard_map.107.texts), custom_call_target="tpu_custom_call" | custom-call | flops 1 | bytes 1 | tf_op jit(solution)/shard_map/pallas_call | solution.py:31
  68.4 1.9 %collective-permute-start.3 = (bf16[192,1280]{1,0:T(8,128)(2,1)}, bf16[192,1280]{1,0:T(8,128)(2,1)}, u32[]{:S(2)}, u32[]{:S(2)}) collective-permute-start(bf16[192,1280]{1,0:T(8,128)(2,1)} %get-tuple-element.39), channel_id=1, source_target_pairs={{0,4},{4,0},{1,5},{5,1},{2,6},{6,2},{3,7},{7,3},{8,12},{12,8},{9,1... | collective-permute-start | bytes 1474568 | tf_op jit(solution)/shard_map/ppermute | solution.py:62
  70.3 8.5 %all-to-all-done.2.parts = bf16[4,64,1152]{2,1,0:T(8,128)(2,1)S(1)} async-done(((bf16[4,64,1152]{2,1,0:T(8,128)(2,1)}), bf16[4,64,1152]{2,1,0:T(8,128)(2,1)S(1)}, u32[]{:S(2)}, u32[]{:S(2)}) %all-to-all-start.2) | async-done | bytes 589856 | tf_op jit(solution)/shard_map/all_to_all | solution.py:270
  78.9 2.1 %shard_map.109 = bf16[4,64,1152]{2,1,0:T(8,128)(2,1)} custom-call(bf16[4,64,1152]{2,1,0:T(8,128)(2,1)S(1)} %all-to-all-done.2.parts, f32[64,1152]{1,0:T(8,128)} %get-tuple-element.35.embedded_in), custom_call_target="tpu_custom_call" | custom-call | flops 1 | bytes 1 | tf_op jit(solution)/shard_map/pallas_call | solution.py:31
  80.9 4.9 %all-to-all-start.3 = ((bf16[4,64,1152]{2,1,0:T(8,128)(2,1)}), bf16[4,64,1152]{2,1,0:T(8,128)(2,1)S(1)}, u32[]{:S(2)}, u32[]{:S(2)}) async-start(bf16[4,64,1152]{2,1,0:T(8,128)(2,1)} %shard_map.109), calls=%async_computation.3 | async-start | bytes 1179648 | tf_op jit(solution)/shard_map/all_to_all | solution.py:270
  85.9 2.0 %collective-permute-start = (bf16[1024,256]{1,0:T(8,128)(2,1)}, bf16[1024,256]{1,0:T(8,128)(2,1)}, u32[]{:S(2)}, u32[]{:S(2)}) collective-permute-start(bf16[1024,256]{1,0:T(8,128)(2,1)} %copy-done.6), channel_id=1, source_target_pairs={{0,4},{4,0},{1,5},{5,1},{2,6},{6,2},{3,7},{7,3},{8,12},{12,8},{9,1... | collective-permute-start | bytes 1572872 | tf_op jit(solution)/shard_map/ppermute | solution.py:62
  87.9 1.1 convert_element_type.19
  89.0 0.9 fusion
  90.1 2.3 %collective-permute-start.4 = (bf16[128,1280]{1,0:T(8,128)(2,1)}, bf16[128,1280]{1,0:T(8,128)(2,1)S(1)}, u32[]{:S(2)}, u32[]{:S(2)}) collective-permute-start(bf16[128,1280]{1,0:T(8,128)(2,1)} %fusion), channel_id=1, source_target_pairs={{0,504},{4,12},{8,0},{12,20},{16,8},{20,28},{24,16},{28,36},{32,24... | collective-permute-start | bytes 983048 | tf_op jit(solution)/shard_map/ppermute | solution.py:58
  92.5 7.4 %collective-permute-start.6 = (bf16[64,1280]{1,0:T(8,128)(2,1)}, bf16[64,1280]{1,0:T(8,128)(2,1)S(1)}, u32[]{:S(2)}, u32[]{:S(2)}) collective-permute-start(bf16[64,1280]{1,0:T(8,128)(2,1)} %copy-done.7), channel_id=1, source_target_pairs={{0,500},{4,16},{8,508},{12,24},{16,4},{20,32},{24,12},{28,40},{32,... | collective-permute-start | bytes 491528 | tf_op jit(solution)/shard_map/ppermute | solution.py:58
  99.9 1.8 %shard_map.110 = bf16[256,640]{1,0:T(8,128)(2,1)S(1)} custom-call(bf16[256,1152]{1,0:T(8,128)(2,1)S(1)} %bitcast.8, bf16[640,1152]{1,0:T(8,128)(2,1)S(1)} %copy-done, f32[256,640]{1,0:T(8,128)} %get-tuple-element.36.slope_in), custom_call_target="tpu_custom_call" | custom-call | flops 1 | bytes 1 | tf_op jit(solution)/shard_map/pallas_call | solution.py:31
  101.7 2.3 %all_gather.11.grads = bf16[512,640]{1,0:T(8,128)(2,1)S(1)} all-gather(bf16[256,640]{1,0:T(8,128)(2,1)S(1)} %shard_map.110), channel_id=1, replica_groups=mesh['x'=4,'zl'=2,'y'=8,'c'=2,'mp'=4] {'c'}, dimensions={0}, use_global_device_ids=true | all-gather | bytes 983040 | tf_op jit(solution)/shard_map/all_gather | solution.py:398
  104.0 3.0 %shard_map.111 = bf16[64,16,384]{2,1,0:T(8,128)(2,1)} custom-call(s32[2]{0:T(128)S(1)} %pad_add_fusion.info, bf16[1024,256]{1,0:T(8,128)(2,1)S(1)} %get-tuple-element.30.mine, bf16[1024,256]{1,0:T(8,128)(2,1)} %collective-permute-done.got, bf16[512,640]{1,0:T(8,128)(2,1)S(1)} %all_gather.11.grads), custom_call_target="tpu_custom_call" | custom-call | flops 1 | bytes 1 | tf_op jit(solution)/shard_map/pallas_call | solution.py:31
  107.0 14.0 %all-to-all-start.4 = ((bf16[64,16,384]{2,1,0:T(8,128)(2,1)}), bf16[64,16,384]{2,1,0:T(8,128)(2,1)S(1)}, u32[]{:S(2)}, u32[]{:S(2)}) async-start(bf16[64,16,384]{2,1,0:T(8,128)(2,1)} %shard_map.111), calls=%async_computation.4 | async-start | bytes 1572864 | tf_op jit(solution)/shard_map/all_to_all | solution.py:408
  121.0 1.9 %collective-permute-start.5 = (bf16[64,1280]{1,0:T(8,128)(2,1)S(1)}, bf16[64,1280]{1,0:T(8,128)(2,1)S(1)}, u32[]{:S(2)}, u32[]{:S(2)}) collective-permute-start(bf16[64,1280]{1,0:T(8,128)(2,1)S(1)} %broadcast_select_fusion), channel_id=1, source_target_pairs={{0,4},{4,0},{1,5},{5,1},{2,6},{6,2},{3,7},{7,3},{8,12},{12,8},{9,1... | collective-permute-start | bytes 491528 | tf_op jit(solution)/shard_map/ppermute | solution.py:62
  123.0 1.3 collective-permute-done.5
  124.3 1.1 fusion.5
  126.2 0.8 fusion.8
  127.1 18.0 %all-to-all-done.4.terms = bf16[64,16,384]{2,1,0:T(8,128)(2,1)S(1)} async-done(((bf16[64,16,384]{2,1,0:T(8,128)(2,1)}), bf16[64,16,384]{2,1,0:T(8,128)(2,1)S(1)}, u32[]{:S(2)}, u32[]{:S(2)}) %all-to-all-start.4) | async-done | bytes 786464 | tf_op jit(solution)/shard_map/all_to_all | solution.py:408
  145.1 0.8 shard_map.112
  (36 shorter events, 3.7 us)
Async XLA Ops:
  0.7 13.5 %copy-start.1 = (bf16[64,1152]{1,0:T(8,128)(2,1)S(1)}, bf16[64,1152]{1,0:T(8,128)(2,1)}, u32[]{:S(2)}) copy-start(bf16[64,1152]{1,0:T(8,128)(2,1)} %text) | copy-start | bytes 442372
  5.2 25.5 %all-to-all-start = ((bf16[4,64,1152]{2,1,0:T(8,128)(2,1)}), bf16[4,64,1152]{2,1,0:T(8,128)(2,1)S(1)}, u32[]{:S(2)}, u32[]{:S(2)}) async-start(bf16[4,64,1152]{2,1,0:T(8,128)(2,1)} %bitcast.10), calls=%async_computation | async-start | bytes 1179648 | tf_op jit(solution)/shard_map/all_to_all | solution.py:270
  16.4 30.8 %collective-permute-start.1 = (bf16[128,1152]{1,0:T(8,128)(2,1)S(1)}, bf16[128,1152]{1,0:T(8,128)(2,1)}, u32[]{:S(2)}, u32[]{:S(2)}) collective-permute-start(bf16[128,1152]{1,0:T(8,128)(2,1)S(1)} %all_gather.9.pair), channel_id=1, source_target_pairs={{0,8},{4,508},{8,16},{12,4},{16,24},{20,12},{24,32},{28,20},{32,40... | collective-permute-start | bytes 884744 | tf_op jit(solution)/shard_map/ppermute | solution.py:58
  31.9 17.7 %copy-start.2 = (f32[256,640]{1,0:T(8,128)S(1)}, f32[256,640]{1,0:T(8,128)}, u32[]{:S(2)}) copy-start(f32[256,640]{1,0:T(8,128)} %get-tuple-element.29.hidden) | copy-start | bytes 1966084
  31.9 17.7 %copy-start.3 = (bf16[256,1152]{1,0:T(8,128)(2,1)S(1)}, bf16[256,1152]{1,0:T(8,128)(2,1)}, u32[]{:S(2)}) copy-start(bf16[256,1152]{1,0:T(8,128)(2,1)} %get-tuple-element.28.normed) | copy-start | bytes 1769476
  31.9 22.3 %all-to-all-start.1 = ((bf16[4,64,1152]{2,1,0:T(8,128)(2,1)}), bf16[4,64,1152]{2,1,0:T(8,128)(2,1)S(1)}, u32[]{:S(2)}, u32[]{:S(2)}) async-start(bf16[4,64,1152]{2,1,0:T(8,128)(2,1)} %get-tuple-element.27), calls=%async_computation.1 | async-start | bytes 1179648 | tf_op jit(solution)/shard_map/all_to_all | solution.py:270
  36.3 17.1 %collective-permute-start.2 = (bf16[64,1152]{1,0:T(8,128)(2,1)S(1)}, bf16[64,1152]{1,0:T(8,128)(2,1)S(1)}, u32[]{:S(2)}, u32[]{:S(2)}) collective-permute-start(bf16[64,1152]{1,0:T(8,128)(2,1)S(1)} %shard_map.106), channel_id=1, source_target_pairs={{500,0},{16,4},{508,8},{24,12},{4,16},{32,20},{12,24},{40,28},{20,... | collective-permute-start | bytes 442376 | tf_op jit(solution)/shard_map/ppermute | solution.py:58
  53.3 0.8 copy-start.6
  56.8 22.1 %all-to-all-start.2 = ((bf16[4,64,1152]{2,1,0:T(8,128)(2,1)}), bf16[4,64,1152]{2,1,0:T(8,128)(2,1)S(1)}, u32[]{:S(2)}, u32[]{:S(2)}) async-start(bf16[4,64,1152]{2,1,0:T(8,128)(2,1)} %bitcast.9), calls=%async_computation.2 | async-start | bytes 1179648 | tf_op jit(solution)/shard_map/all_to_all | solution.py:270
  67.0 0.7 copy-start.4
  67.7 0.7 copy-start.7
  68.4 19.5 %collective-permute-start.3 = (bf16[192,1280]{1,0:T(8,128)(2,1)}, bf16[192,1280]{1,0:T(8,128)(2,1)}, u32[]{:S(2)}, u32[]{:S(2)}) collective-permute-start(bf16[192,1280]{1,0:T(8,128)(2,1)} %get-tuple-element.39), channel_id=1, source_target_pairs={{0,4},{4,0},{1,5},{5,1},{2,6},{6,2},{3,7},{7,3},{8,12},{12,8},{9,1... | collective-permute-start | bytes 1474568 | tf_op jit(solution)/shard_map/ppermute | solution.py:62
  80.9 19.0 %all-to-all-start.3 = ((bf16[4,64,1152]{2,1,0:T(8,128)(2,1)}), bf16[4,64,1152]{2,1,0:T(8,128)(2,1)S(1)}, u32[]{:S(2)}, u32[]{:S(2)}) async-start(bf16[4,64,1152]{2,1,0:T(8,128)(2,1)} %shard_map.109), calls=%async_computation.3 | async-start | bytes 1179648 | tf_op jit(solution)/shard_map/all_to_all | solution.py:270
  85.9 14.1 %copy-start = (bf16[640,1152]{1,0:T(8,128)(2,1)S(1)}, bf16[640,1152]{1,0:T(8,128)(2,1)}, u32[]{:S(2)}) copy-start(bf16[640,1152]{1,0:T(8,128)(2,1)} %w_down.3) | copy-start | bytes 4423684
  85.9 18.2 %collective-permute-start = (bf16[1024,256]{1,0:T(8,128)(2,1)}, bf16[1024,256]{1,0:T(8,128)(2,1)}, u32[]{:S(2)}, u32[]{:S(2)}) collective-permute-start(bf16[1024,256]{1,0:T(8,128)(2,1)} %copy-done.6), channel_id=1, source_target_pairs={{0,4},{4,0},{1,5},{5,1},{2,6},{6,2},{3,7},{7,3},{8,12},{12,8},{9,1... | collective-permute-start | bytes 1572872 | tf_op jit(solution)/shard_map/ppermute | solution.py:62
  89.0 1.1 copy-start.8
  90.1 30.9 %collective-permute-start.4 = (bf16[128,1280]{1,0:T(8,128)(2,1)}, bf16[128,1280]{1,0:T(8,128)(2,1)S(1)}, u32[]{:S(2)}, u32[]{:S(2)}) collective-permute-start(bf16[128,1280]{1,0:T(8,128)(2,1)} %fusion), channel_id=1, source_target_pairs={{0,504},{4,12},{8,0},{12,20},{16,8},{20,28},{24,16},{28,36},{32,24... | collective-permute-start | bytes 983048 | tf_op jit(solution)/shard_map/ppermute | solution.py:58
  92.5 30.5 %collective-permute-start.6 = (bf16[64,1280]{1,0:T(8,128)(2,1)}, bf16[64,1280]{1,0:T(8,128)(2,1)S(1)}, u32[]{:S(2)}, u32[]{:S(2)}) collective-permute-start(bf16[64,1280]{1,0:T(8,128)(2,1)} %copy-done.7), channel_id=1, source_target_pairs={{0,500},{4,16},{8,508},{12,24},{16,4},{20,32},{24,12},{28,40},{32,... | collective-permute-start | bytes 491528 | tf_op jit(solution)/shard_map/ppermute | solution.py:58
  107.0 17.3 %copy-start.5 = (f32[64,1280]{1,0:T(8,128)S(1)}, f32[64,1280]{1,0:T(8,128)}, u32[]{:S(2)}) copy-start(f32[64,1280]{1,0:T(8,128)} %copy-done.4) | copy-start | bytes 983044
  107.0 38.1 %all-to-all-start.4 = ((bf16[64,16,384]{2,1,0:T(8,128)(2,1)}), bf16[64,16,384]{2,1,0:T(8,128)(2,1)S(1)}, u32[]{:S(2)}, u32[]{:S(2)}) async-start(bf16[64,16,384]{2,1,0:T(8,128)(2,1)} %shard_map.111), calls=%async_computation.4 | async-start | bytes 1572864 | tf_op jit(solution)/shard_map/all_to_all | solution.py:408
  121.0 3.3 %collective-permute-start.5 = (bf16[64,1280]{1,0:T(8,128)(2,1)S(1)}, bf16[64,1280]{1,0:T(8,128)(2,1)S(1)}, u32[]{:S(2)}, u32[]{:S(2)}) collective-permute-start(bf16[64,1280]{1,0:T(8,128)(2,1)S(1)} %broadcast_select_fusion), channel_id=1, source_target_pairs={{0,4},{4,0},{1,5},{5,1},{2,6},{6,2},{3,7},{7,3},{8,12},{12,8},{9,1... | collective-permute-start | bytes 491528 | tf_op jit(solution)/shard_map/ppermute | solution.py:62

commit v4 on v3

--- a/solution.py
+++ b/solution.py
@@ -60,6 +60,10 @@
 
 def swapped(value):
     return lax.ppermute(value, "c", [(0, 1), (1, 0)])
+
+
+def of_both_cores(value):
+    return lax.all_gather(value, "c", axis=0, tiled=True)
 
 
 def dot(a, b, ca, cb):
@@ -205,6 +209,26 @@
         far_part[:, cols] = terms[6 * q :].astype(bf16)
 
 
+def side_kernel(info, gave, keep_side, keep_own, side, own_sum):
+    q = keep_own.shape[0]
+    start = pl.multiple_of((1 - info[0]) * 3 * q, 3 * q)
+    side[...] = (keep_side[...] + gave[pl.ds(start, 2 * q), :].astype(f32)).astype(bf16)
+    own_sum[...] = keep_own[...] + gave[pl.ds(start + 2 * q, q), :].astype(f32)
+
+
+def text_grad_kernel(info, came, own_sum, far_back, text, text_grad, text_loss):
+    q, width = text.shape
+    start = pl.multiple_of(info[0] * q, q)
+    total = (own_sum[...] + far_back[...].astype(f32)) + (
+        came[pl.ds(start, q), :].astype(f32) + came[pl.ds(start + 2 * q, q), :].astype(f32)
+    )
+    inverse, unit_value = unit_rows(text[...].astype(f32))
+    text_acc = total[:, :width]
+    radial = jnp.sum(unit_value * text_acc, axis=-1, keepdims=True)
+    text_grad[...] = inverse * (text_acc - unit_value * radial)
+    text_loss[...] = total[:, width : width + 1] / (WINDOW * 4 * q)
+
+
 def grad_kernel(parts, embedded_in, grad_out, embedded, grad, sems):
     load = copied(sems, (embedded_in, embedded))[0]
     grad_sum = (parts[0].astype(f32) + parts[1].astype(f32)) + (
@@ -261,7 +285,6 @@
     q = text.shape[0]
     units = w_up.shape[1]
     core = lax.axis_index("c")
-    first = core == 0
     info = jnp.stack([core, lax.axis_index("mp")]).astype(jnp.int32)
     factors = jnp.concatenate([logit_scale, logit_bias])
     wide = width + LANES
@@ -300,23 +323,35 @@
     parts = mp_exchange(partial_out)
 
     text_half = call(text_kernel, shape((q, width), bf16), [VMEM], after(text, partial_out))
-    pair = lax.all_gather(text_half, "c", axis=0, tiled=True)
+    pair = of_both_cores(text_half)
     side_in = moved(pair, [(i, i + 2) if i % 2 == 0 else (i, i - 2) for i in range(N_DP)])
     far_out = [(i - 3, i) if i % 2 == 0 else (i + 3, i) for i in range(N_DP)]
     far = moved(text_half, far_out)
+
+    half_rows = shape((1024, rows_count), bf16)
+    mine, theirs, slope = call(
+        select_kernel,
+        (half_rows, half_rows, pltpu.HBM((rows_count, units), f32)),
+        [SMEM, VMEM, VMEM],
+        info,
+        normed,
+        hidden,
+        specs=(VMEM, VMEM, HBM),
+        scratch=(pltpu.VMEM((rows_count, units), f32), sems),
+    )
 
     embedded, image_half = call(
         embed_kernel,
         (pltpu.HBM((q, width), f32), copies),
         [VMEM, VMEM],
         parts,
-        own,
+        after(own, theirs, pair),
         specs=(HBM, HBM),
         scratch=(pltpu.VMEM((q, width), bf16), pltpu.VMEM((q, width), f32), sems),
     )
     unit_half = mp_exchange(image_half).reshape(rows_count, width)
 
-    sides = lax.all_gather(after(side_in, image_half), "c", axis=0, tiled=True)
+    sides = of_both_cores(after(side_in, image_half))
     texts = call(
         window_kernel,
         shape((WINDOW * q, width), bf16),
@@ -327,19 +362,8 @@
         far,
     )
 
-    half_rows = shape((1024, rows_count), bf16)
-    mine, theirs, slope = call(
-        select_kernel,
-        (half_rows, half_rows, pltpu.HBM((rows_count, units), f32)),
-        [SMEM, VMEM, VMEM],
-        info,
-        after(normed, image_half),
-        hidden,
-        specs=(VMEM, VMEM, HBM),
-        scratch=(pltpu.VMEM((rows_count, units), f32), sems),
-    )
-    got_rows = swapped(theirs)
-    texts = after(texts, theirs)
+    got_rows = swapped(after(theirs, image_half))
+    texts = after(texts, got_rows)
 
     image_part = call(
         image_kernel,
@@ -368,15 +392,22 @@
         after(unit_half, image_part),
         texts,
     )
-    got = swapped(give).astype(f32)
-    side = (keep_side + got[: 2 * q]).astype(bf16)
-    own_sum = keep_own + got[2 * q :]
+    far_back = moved(after(far_part, grad_parts), [(d, s) for s, d in far_out])
+    side, own_sum = call(
+        side_kernel,
+        (shape((2 * q, wide), bf16), shape((q, wide), f32)),
+        [SMEM] + [VMEM] * 3,
+        info,
+        of_both_cores(give),
+        keep_side,
+        keep_own,
+    )
 
     grad_own = call(
         grad_kernel,
         copies,
         [VMEM, HBM],
-        grad_parts,
+        after(grad_parts, side),
         in_hbm(embedded),
         specs=HBM,
         scratch=(pltpu.VMEM((q, width), f32), pltpu.VMEM((q, width), bf16), sems),
@@ -384,7 +415,6 @@
     grad_image = mp_exchange(grad_own).reshape(rows_count, width)
     side = after(side, grad_own)
     came = moved(side, [(i, i - 2) if i % 2 == 0 else (i, i + 2) for i in range(N_DP)])
-    far_back = moved(after(far_part, grad_own), [(d, s) for s, d in far_out])
 
     grad_pre = call(
         pre_kernel,
@@ -395,7 +425,7 @@
         in_hbm(slope),
         scratch=(pltpu.VMEM((rows_count, units), f32), sems),
     )
-    grads = lax.all_gather(grad_pre, "c", axis=0, tiled=True)
+    grads = of_both_cores(grad_pre)
     up_wire = call(
         up_kernel,
         shape((N_DP // 2, 16, 3 * LANES), bf16),
@@ -403,24 +433,21 @@
         info,
         mine,
         got_rows,
-        grads,
+        after(grads, came, far_back),
     )
     up_terms = lax.all_to_all(up_wire, CHIPS, 0, 0, tiled=True)
 
-    came = after(came, up_wire)
-    came_first, came_second = came[:q], came[q:]
-    last = swapped(jnp.where(first, came_second, came_first))
-    total = (
-        own_sum
-        + jnp.where(first, came_first, came_second).astype(f32)
-        + last.astype(f32)
-        + far_back.astype(f32)
-    )
-    text_acc = total[:, :width]
-    text_loss = total[:, width] / (WINDOW * rows_count)
-    text_inv, text_unit = unit_rows(text.astype(f32))
-    text_radial = jnp.sum(text_unit * text_acc, axis=-1, keepdims=True)
-    text_grad = text_inv * (text_acc - text_unit * text_radial)
+    text_grad, text_loss = call(
+        text_grad_kernel,
+        (shape((q, width), f32), shape((q, 1), f32)),
+        [SMEM] + [VMEM] * 4,
+        info,
+        of_both_cores(after(came, up_wire)),
+        own_sum,
+        far_back,
+        text,
+    )
+    text_loss = text_loss.reshape(q)
 
     up_grad = call(up_sum_kernel, shape((width // N_DP, units), f32), [VMEM], up_terms)
     return (up_grad, text_grad, text_loss)

time: 147 us -> 147 us (level)
  the two profiles are of different devices: /device:TPU:136 before, /device:TPU:1 now
where the time goes in v4:
time: 147 us; the launch traced here: 145 us
  starting transfers between devices  65.9 us (45%)
  blocking collectives  28.9 us (20%)
  Pallas kernels  24 us (16%)
  waiting for transfers between devices  19.7 us (13%)
  local copies, waits for them, and re-layouts  3.01 us (2%)
  between operations  2.15 us (1%)
    all_to_all x4, starting transfers between devices, mp_exchange(): return lax.all_to_all(partial.reshape(4, q, width), 'mp', 0, 0, tiled=True)  31.8 us
    all_gather x5, blocking collectives, of_both_cores(): return lax.all_gather(value, 'c', axis=0, tiled=True)  28.9 us
    pallas_call x13, Pallas kernels, call(): pl.pallas_call(kernel, out_shape=outs, in_specs=ins, out_specs=specs if s...  24 us
    ppermute x4, starting transfers between devices, moved(): return lax.ppermute(value, DP, [(s % N_DP, d % N_DP) for s, d in pairs])  19.9 us
    all_to_all x1, waiting for transfers between devices, body(): up_terms = lax.all_to_all(up_wire, CHIPS, 0, 0, tiled=True)  16.3 us
    all_to_all x1, starting transfers between devices, body(): up_terms = lax.all_to_all(up_wire, CHIPS, 0, 0, tiled=True)  7.7 us
    ppermute x1, starting transfers between devices, swapped(): return lax.ppermute(value, 'c', [(0, 1), (1, 0)])  6.55 us
    all_to_all x4, waiting for transfers between devices, mp_exchange(): return lax.all_to_all(partial.reshape(4, q, width), 'mp', 0, 0, tiled=True)  3.39 us
  transfers between devices with their start and end apart: 10, of which 2 were waited for; matrix products, arithmetic and copies ran while one was open for 1% of the time, Pallas kernels for 8%

profile of v4, /device:TPU:1, one launch (start us, length us, event | category | flops | bytes accessed | tf_op | source)
XLA Modules:
  0.0 144.5 jit_solution(1079624646183308917)
XLA Ops:
  0.7 4.4 %shard_map.103 = (bf16[256,1152]{1,0:T(8,128)(2,1)}, bf16[64,1152]{1,0:T(8,128)(2,1)S(1)}, bf16[256,1152]{1,0:T(8,128)(2,1)}, f32[256,640]{1,0:T(8,128)}) custom-call(s32[2]{0:T(128)S(1)} %pad_add_fusion.info, bf16[256,1152]{1,0:T(8,128)(2,1)} %pooled_in.1, f32[1152]{0:T(1024)} %gain_in.1, f32[640]{0:T(1024)} %b_up_in.1, bf16[1152,640]{1,0:T(8,128)(2,1)} %w_up.1, ...), custom_call_target="tpu_custom_call" | custom-call | flops 1 | bytes 1 | tf_op jit(solution)/shard_map/pallas_call | solution.py:31
  5.2 11.0 %all-to-all-start = ((bf16[4,64,1152]{2,1,0:T(8,128)(2,1)}), bf16[4,64,1152]{2,1,0:T(8,128)(2,1)S(1)}, u32[]{:S(2)}, u32[]{:S(2)}) async-start(bf16[4,64,1152]{2,1,0:T(8,128)(2,1)} %bitcast.10), calls=%async_computation | async-start | bytes 1179648 | tf_op jit(solution)/shard_map/all_to_all | solution.py:293
  16.3 2.6 %all_gather.15.pair = bf16[128,1152]{1,0:T(8,128)(2,1)S(1)} all-gather(bf16[64,1152]{1,0:T(8,128)(2,1)S(1)} %shard_map.105), channel_id=1, replica_groups=mesh['x'=4,'zl'=2,'y'=8,'c'=2,'mp'=4] {'c'}, dimensions={0}, use_global_device_ids=true | all-gather | bytes 442368 | tf_op jit(solution)/shard_map/all_gather | solution.py:66
  18.9 8.2 %collective-permute-start.1 = (bf16[128,1152]{1,0:T(8,128)(2,1)S(1)}, bf16[128,1152]{1,0:T(8,128)(2,1)}, u32[]{:S(2)}, u32[]{:S(2)}) collective-permute-start(bf16[128,1152]{1,0:T(8,128)(2,1)S(1)} %all_gather.15.pair), channel_id=1, source_target_pairs={{0,8},{4,508},{8,16},{12,4},{16,24},{20,12},{24,32},{28,20},{32,40... | collective-permute-start | bytes 884744 | tf_op jit(solution)/shard_map/ppermute | solution.py:58
  27.1 3.7 %shard_map.104 = (bf16[1024,256]{1,0:T(8,128)(2,1)S(1)}, bf16[1024,256]{1,0:T(8,128)(2,1)S(1)}, f32[256,640]{1,0:T(8,128)}) custom-call(s32[2]{0:T(128)S(1)} %pad_add_fusion.info, bf16[256,1152]{1,0:T(8,128)(2,1)S(1)} %copy-done.3, f32[256,640]{1,0:T(8,128)S(1)} %copy-done.1), custom_call_target="tpu_custom_call" | custom-call | flops 1 | bytes 1 | tf_op jit(solution)/shard_map/pallas_call | solution.py:31
  30.8 0.8 copy-done.6
  31.6 1.2 shard_map.106
  32.8 7.3 %all-to-all-start.1 = ((bf16[4,64,1152]{2,1,0:T(8,128)(2,1)}), bf16[4,64,1152]{2,1,0:T(8,128)(2,1)S(1)}, u32[]{:S(2)}, u32[]{:S(2)}) async-start(bf16[4,64,1152]{2,1,0:T(8,128)(2,1)} %get-tuple-element.39), calls=%async_computation.1 | async-start | bytes 1179648 | tf_op jit(solution)/shard_map/all_to_all | solution.py:293
  40.1 3.0 %collective-permute-start.2 = (bf16[64,1152]{1,0:T(8,128)(2,1)S(1)}, bf16[64,1152]{1,0:T(8,128)(2,1)S(1)}, u32[]{:S(2)}, u32[]{:S(2)}) collective-permute-start(bf16[64,1152]{1,0:T(8,128)(2,1)S(1)} %shard_map.105), channel_id=1, source_target_pairs={{500,0},{16,4},{508,8},{24,12},{4,16},{32,20},{12,24},{40,28},{20,... | collective-permute-start | bytes 442376 | tf_op jit(solution)/shard_map/ppermute | solution.py:58
  44.5 6.6 %collective-permute-start = (bf16[1024,256]{1,0:T(8,128)(2,1)}, bf16[1024,256]{1,0:T(8,128)(2,1)S(1)}, u32[]{:S(2)}, u32[]{:S(2)}) collective-permute-start(bf16[1024,256]{1,0:T(8,128)(2,1)} %copy-done.6), channel_id=1, source_target_pairs={{0,4},{4,0},{1,5},{5,1},{2,6},{6,2},{3,7},{7,3},{8,12},{12,8},{9,1... | collective-permute-start | bytes 1572872 | tf_op jit(solution)/shard_map/ppermute | solution.py:62
  51.1 2.4 %all_gather.16 = bf16[256,1152]{1,0:T(8,128)(2,1)S(1)} all-gather(bf16[128,1152]{1,0:T(8,128)(2,1)} %collective-permute-done.1), channel_id=1, replica_groups=mesh['x'=4,'zl'=2,'y'=8,'c'=2,'mp'=4] {'c'}, dimensions={0}, use_global_device_ids=true | all-gather | bytes 884736 | tf_op jit(solution)/shard_map/all_gather | solution.py:66
  53.7 2.6 %shard_map.108 = bf16[256,1152]{1,0:T(8,128)(2,1)} custom-call(s32[2]{0:T(128)S(1)} %pad_add_fusion.info, f32[2]{0:T(128)S(1)} %pad_maximum_fusion.factors, bf16[256,1152]{1,0:T(8,128)(2,1)S(1)} %bitcast.6, bf16[448,1152]{1,0:T(8,128)(2,1)S(1)} %shard_map.107.texts), custom_call_target="tpu_custom_call" | custom-call | flops 1 | bytes 1 | tf_op jit(solution)/shard_map/pallas_call | solution.py:31
  56.3 6.6 %all-to-all-start.2 = ((bf16[4,64,1152]{2,1,0:T(8,128)(2,1)}), bf16[4,64,1152]{2,1,0:T(8,128)(2,1)S(1)}, u32[]{:S(2)}, u32[]{:S(2)}) async-start(bf16[4,64,1152]{2,1,0:T(8,128)(2,1)} %bitcast.9), calls=%async_computation.2 | async-start | bytes 1179648 | tf_op jit(solution)/shard_map/all_to_all | solution.py:293
  62.9 2.2 %shard_map.109 = (bf16[192,1280]{1,0:T(8,128)(2,1)S(1)}, bf16[64,1280]{1,0:T(8,128)(2,1)S(1)}, f32[128,1280]{1,0:T(8,128)S(1)}, f32[64,1280]{1,0:T(8,128)S(1)}) custom-call(s32[2]{0:T(128)S(1)} %pad_add_fusion.info, f32[2]{0:T(128)S(1)} %pad_maximum_fusion.factors, bf16[256,1152]{1,0:T(8,128)(2,1)S(1)} %bitcast.7, bf16[448,1152]{1,0:T(8,128)(2,1)S(1)} %shard_map.107.texts), custom_call_target="tpu_custom_call" | custom-call | flops 1 | bytes 1 | tf_op jit(solution)/shard_map/pallas_call | solution.py:31
  65.2 0.7 copy-done.8
  65.8 6.9 %all_gather.17.gave = bf16[384,1280]{1,0:T(8,128)(2,1)S(1)} all-gather(bf16[192,1280]{1,0:T(8,128)(2,1)S(1)} %get-tuple-element.44), channel_id=1, replica_groups=mesh['x'=4,'zl'=2,'y'=8,'c'=2,'mp'=4] {'c'}, dimensions={0}, use_global_device_ids=true | all-gather | bytes 1474560 | tf_op jit(solution)/shard_map/all_gather | solution.py:66
  73.4 0.7 copy-done.4
  74.1 0.8 copy-done.7
  74.9 2.2 %shard_map.111 = bf16[4,64,1152]{2,1,0:T(8,128)(2,1)} custom-call(bf16[4,64,1152]{2,1,0:T(8,128)(2,1)S(1)} %all-to-all-done.2.parts, f32[64,1152]{1,0:T(8,128)} %get-tuple-element.49.embedded_in), custom_call_target="tpu_custom_call" | custom-call | flops 1 | bytes 1 | tf_op jit(solution)/shard_map/pallas_call | solution.py:31
  77.1 6.9 %all-to-all-start.3 = ((bf16[4,64,1152]{2,1,0:T(8,128)(2,1)}), bf16[4,64,1152]{2,1,0:T(8,128)(2,1)S(1)}, u32[]{:S(2)}, u32[]{:S(2)}) async-start(bf16[4,64,1152]{2,1,0:T(8,128)(2,1)} %shard_map.111), calls=%async_computation.3 | async-start | bytes 1179648 | tf_op jit(solution)/shard_map/all_to_all | solution.py:293
  84.0 3.0 %collective-permute-start.3 = (bf16[128,1280]{1,0:T(8,128)(2,1)}, bf16[128,1280]{1,0:T(8,128)(2,1)}, u32[]{:S(2)}, u32[]{:S(2)}) collective-permute-start(bf16[128,1280]{1,0:T(8,128)(2,1)} %copy-done.7), channel_id=1, source_target_pairs={{0,504},{4,12},{8,0},{12,20},{16,8},{20,28},{24,16},{28,36},{32,24... | collective-permute-start | bytes 983048 | tf_op jit(solution)/shard_map/ppermute | solution.py:58
  87.0 5.7 %collective-permute-start.4 = (bf16[64,1280]{1,0:T(8,128)(2,1)}, bf16[64,1280]{1,0:T(8,128)(2,1)}, u32[]{:S(2)}, u32[]{:S(2)}) collective-permute-start(bf16[64,1280]{1,0:T(8,128)(2,1)} %copy-done.8), channel_id=1, source_target_pairs={{0,500},{4,16},{8,508},{12,24},{16,4},{20,32},{24,12},{28,40},{32,... | collective-permute-start | bytes 491528 | tf_op jit(solution)/shard_map/ppermute | solution.py:58
  92.7 3.4 %all-to-all-done.3 = bf16[4,64,1152]{2,1,0:T(8,128)(2,1)S(1)} async-done(((bf16[4,64,1152]{2,1,0:T(8,128)(2,1)}), bf16[4,64,1152]{2,1,0:T(8,128)(2,1)S(1)}, u32[]{:S(2)}, u32[]{:S(2)}) %all-to-all-start.3) | async-done | bytes 589856 | tf_op jit(solution)/shard_map/all_to_all | solution.py:293
  96.0 1.8 %shard_map.112 = bf16[256,640]{1,0:T(8,128)(2,1)S(1)} custom-call(bf16[256,1152]{1,0:T(8,128)(2,1)S(1)} %bitcast.8, bf16[640,1152]{1,0:T(8,128)(2,1)S(1)} %copy-done, f32[256,640]{1,0:T(8,128)} %get-tuple-element.50.slope_in), custom_call_target="tpu_custom_call" | custom-call | flops 1 | bytes 1 | tf_op jit(solution)/shard_map/pallas_call | solution.py:31
  97.8 14.2 %all_gather.18.grads = bf16[512,640]{1,0:T(8,128)(2,1)S(1)} all-gather(bf16[256,640]{1,0:T(8,128)(2,1)S(1)} %shard_map.112), channel_id=1, replica_groups=mesh['x'=4,'zl'=2,'y'=8,'c'=2,'mp'=4] {'c'}, dimensions={0}, use_global_device_ids=true | all-gather | bytes 983040 | tf_op jit(solution)/shard_map/all_gather | solution.py:66
  112.1 2.4 %shard_map.113 = bf16[64,16,384]{2,1,0:T(8,128)(2,1)} custom-call(s32[2]{0:T(128)S(1)} %pad_add_fusion.info, bf16[1024,256]{1,0:T(8,128)(2,1)S(1)} %get-tuple-element.33.mine, bf16[1024,256]{1,0:T(8,128)(2,1)S(1)} %collective-permute-done.got, bf16[512,640]{1,0:T(8,128)(2,1)S(1)} %all_gather.18.grads), custom_call_target="tpu_custom_call" | custom-call | flops 1 | bytes 1 | tf_op jit(solution)/shard_map/pallas_call | solution.py:31
  114.5 7.7 %all-to-all-start.4 = ((bf16[64,16,384]{2,1,0:T(8,128)(2,1)}), bf16[64,16,384]{2,1,0:T(8,128)(2,1)S(1)}, u32[]{:S(2)}, u32[]{:S(2)}) async-start(bf16[64,16,384]{2,1,0:T(8,128)(2,1)} %shard_map.113), calls=%async_computation.4 | async-start | bytes 1572864 | tf_op jit(solution)/shard_map/all_to_all | solution.py:438
  122.2 2.8 %all_gather.19.came = bf16[256,1280]{1,0:T(8,128)(2,1)S(1)} all-gather(bf16[128,1280]{1,0:T(8,128)(2,1)} %collective-permute-done.3), channel_id=1, replica_groups=mesh['x'=4,'zl'=2,'y'=8,'c'=2,'mp'=4] {'c'}, dimensions={0}, use_global_device_ids=true | all-gather | bytes 983040 | tf_op jit(solution)/shard_map/all_gather | solution.py:66
  125.0 1.9 %shard_map.115 = (f32[64,1152]{1,0:T(8,128)}, f32[64,1]{1,0:T(8,128)S(1)}) custom-call(s32[2]{0:T(128)S(1)} %pad_add_fusion.info, bf16[256,1280]{1,0:T(8,128)(2,1)S(1)} %all_gather.19.came, f32[64,1280]{1,0:T(8,128)S(1)} %copy-done.5, bf16[64,1280]{1,0:T(8,128)(2,1)} %collective-permute-done.4.far_back, bf16[64,1152]{1,0:T(8,128)(2,1)S(1)} %copy-done.2), custom_call_target="tpu_custom_call" | custom-call | flops 1 | bytes 1 | tf_op jit(solution)/shard_map/pallas_call | solution.py:31
  126.8 0.6 reduce
  127.5 16.3 %all-to-all-done.4.terms = bf16[64,16,384]{2,1,0:T(8,128)(2,1)S(1)} async-done(((bf16[64,16,384]{2,1,0:T(8,128)(2,1)}), bf16[64,16,384]{2,1,0:T(8,128)(2,1)S(1)}, u32[]{:S(2)}, u32[]{:S(2)}) %all-to-all-start.4) | async-done | bytes 786464 | tf_op jit(solution)/shard_map/all_to_all | solution.py:438
  143.8 0.8 shard_map.114
  (28 shorter events, 1.1 us)
Async XLA Ops:
  0.7 15.5 %copy-start.2 = (bf16[64,1152]{1,0:T(8,128)(2,1)S(1)}, bf16[64,1152]{1,0:T(8,128)(2,1)}, u32[]{:S(2)}) copy-start(bf16[64,1152]{1,0:T(8,128)(2,1)} %text.2) | copy-start | bytes 442372
  5.2 21.9 %copy-start.1 = (f32[256,640]{1,0:T(8,128)S(1)}, f32[256,640]{1,0:T(8,128)}, u32[]{:S(2)}) copy-start(f32[256,640]{1,0:T(8,128)} %get-tuple-element.32.hidden) | copy-start | bytes 1966084
  5.2 21.9 %copy-start.3 = (bf16[256,1152]{1,0:T(8,128)(2,1)S(1)}, bf16[256,1152]{1,0:T(8,128)(2,1)}, u32[]{:S(2)}) copy-start(bf16[256,1152]{1,0:T(8,128)(2,1)} %get-tuple-element.31.normed) | copy-start | bytes 1769476
  5.2 26.4 %all-to-all-start = ((bf16[4,64,1152]{2,1,0:T(8,128)(2,1)}), bf16[4,64,1152]{2,1,0:T(8,128)(2,1)S(1)}, u32[]{:S(2)}, u32[]{:S(2)}) async-start(bf16[4,64,1152]{2,1,0:T(8,128)(2,1)} %bitcast.10), calls=%async_computation | async-start | bytes 1179648 | tf_op jit(solution)/shard_map/all_to_all | solution.py:293
  18.9 25.6 %collective-permute-start.1 = (bf16[128,1152]{1,0:T(8,128)(2,1)S(1)}, bf16[128,1152]{1,0:T(8,128)(2,1)}, u32[]{:S(2)}, u32[]{:S(2)}) collective-permute-start(bf16[128,1152]{1,0:T(8,128)(2,1)S(1)} %all_gather.15.pair), channel_id=1, source_target_pairs={{0,8},{4,508},{8,16},{12,4},{16,24},{20,12},{24,32},{28,20},{32,40... | collective-permute-start | bytes 884744 | tf_op jit(solution)/shard_map/ppermute | solution.py:58
  30.8 0.8 copy-start.6
  32.8 20.9 %all-to-all-start.1 = ((bf16[4,64,1152]{2,1,0:T(8,128)(2,1)}), bf16[4,64,1152]{2,1,0:T(8,128)(2,1)S(1)}, u32[]{:S(2)}, u32[]{:S(2)}) async-start(bf16[4,64,1152]{2,1,0:T(8,128)(2,1)} %get-tuple-element.39), calls=%async_computation.1 | async-start | bytes 1179648 | tf_op jit(solution)/shard_map/all_to_all | solution.py:293
  40.1 13.4 %collective-permute-start.2 = (bf16[64,1152]{1,0:T(8,128)(2,1)S(1)}, bf16[64,1152]{1,0:T(8,128)(2,1)S(1)}, u32[]{:S(2)}, u32[]{:S(2)}) collective-permute-start(bf16[64,1152]{1,0:T(8,128)(2,1)S(1)} %shard_map.105), channel_id=1, source_target_pairs={{500,0},{16,4},{508,8},{24,12},{4,16},{32,20},{12,24},{40,28},{20,... | collective-permute-start | bytes 442376 | tf_op jit(solution)/shard_map/ppermute | solution.py:58
  44.5 9.2 %collective-permute-start = (bf16[1024,256]{1,0:T(8,128)(2,1)}, bf16[1024,256]{1,0:T(8,128)(2,1)S(1)}, u32[]{:S(2)}, u32[]{:S(2)}) collective-permute-start(bf16[1024,256]{1,0:T(8,128)(2,1)} %copy-done.6), channel_id=1, source_target_pairs={{0,4},{4,0},{1,5},{5,1},{2,6},{6,2},{3,7},{7,3},{8,12},{12,8},{9,1... | collective-permute-start | bytes 1572872 | tf_op jit(solution)/shard_map/ppermute | solution.py:62
  56.3 18.6 %all-to-all-start.2 = ((bf16[4,64,1152]{2,1,0:T(8,128)(2,1)}), bf16[4,64,1152]{2,1,0:T(8,128)(2,1)S(1)}, u32[]{:S(2)}, u32[]{:S(2)}) async-start(bf16[4,64,1152]{2,1,0:T(8,128)(2,1)} %bitcast.9), calls=%async_computation.2 | async-start | bytes 1179648 | tf_op jit(solution)/shard_map/all_to_all | solution.py:293
  65.1 0.7 copy-start.8
  73.4 0.7 copy-start.4
  74.1 0.8 copy-start.7
  74.9 21.2 %copy-start = (bf16[640,1152]{1,0:T(8,128)(2,1)S(1)}, bf16[640,1152]{1,0:T(8,128)(2,1)}, u32[]{:S(2)}) copy-start(bf16[640,1152]{1,0:T(8,128)(2,1)} %w_down.3) | copy-start | bytes 4423684
  77.1 19.0 %all-to-all-start.3 = ((bf16[4,64,1152]{2,1,0:T(8,128)(2,1)}), bf16[4,64,1152]{2,1,0:T(8,128)(2,1)S(1)}, u32[]{:S(2)}, u32[]{:S(2)}) async-start(bf16[4,64,1152]{2,1,0:T(8,128)(2,1)} %shard_map.111), calls=%async_computation.3 | async-start | bytes 1179648 | tf_op jit(solution)/shard_map/all_to_all | solution.py:293
  84.0 28.1 %collective-permute-start.3 = (bf16[128,1280]{1,0:T(8,128)(2,1)}, bf16[128,1280]{1,0:T(8,128)(2,1)}, u32[]{:S(2)}, u32[]{:S(2)}) collective-permute-start(bf16[128,1280]{1,0:T(8,128)(2,1)} %copy-done.7), channel_id=1, source_target_pairs={{0,504},{4,12},{8,0},{12,20},{16,8},{20,28},{24,16},{28,36},{32,24... | collective-permute-start | bytes 983048 | tf_op jit(solution)/shard_map/ppermute | solution.py:58
  87.0 25.1 %collective-permute-start.4 = (bf16[64,1280]{1,0:T(8,128)(2,1)}, bf16[64,1280]{1,0:T(8,128)(2,1)}, u32[]{:S(2)}, u32[]{:S(2)}) collective-permute-start(bf16[64,1280]{1,0:T(8,128)(2,1)} %copy-done.8), channel_id=1, source_target_pairs={{0,500},{4,16},{8,508},{12,24},{16,4},{20,32},{24,12},{28,40},{32,... | collective-permute-start | bytes 491528 | tf_op jit(solution)/shard_map/ppermute | solution.py:58
  114.5 10.5 %copy-start.5 = (f32[64,1280]{1,0:T(8,128)S(1)}, f32[64,1280]{1,0:T(8,128)}, u32[]{:S(2)}) copy-start(f32[64,1280]{1,0:T(8,128)} %copy-done.4) | copy-start | bytes 983044
  114.5 29.3 %all-to-all-start.4 = ((bf16[64,16,384]{2,1,0:T(8,128)(2,1)}), bf16[64,16,384]{2,1,0:T(8,128)(2,1)S(1)}, u32[]{:S(2)}, u32[]{:S(2)}) async-start(bf16[64,16,384]{2,1,0:T(8,128)(2,1)} %shard_map.113), calls=%async_computation.4 | async-start | bytes 1572864 | tf_op jit(solution)/shard_map/all_to_all | solution.py:438

commit v5 on v4

--- a/solution.py
+++ b/solution.py
@@ -115,19 +115,22 @@
     half[...] = unit_rows(text[...].astype(f32))[1].astype(bf16)
 
 
-def select_kernel(info, normed, hidden, mine, theirs, slope_out, slope, sems):
+def select_kernel(
+    info, normed, hidden, mine_out, theirs_out, slope_out, mine, theirs, slope, sems
+):
     pre = hidden[...]
     square = pre * pre
     tanh_value = jnp.tanh(root_two_pi * (pre + gelu_coeff * square * pre))
     slope[...] = 0.5 * (1.0 + tanh_value) + 0.5 * pre * (1.0 - tanh_value * tanh_value) * (
         root_two_pi * (1.0 + 3.0 * gelu_coeff * square)
     )
-    store = copied(sems, (slope, slope_out))[0]
+    stores = copied(sems, (slope, slope_out))
     core = info[0]
     rows = 256
     count, width = mine.shape[0], normed.shape[1]
     normed_value = normed[...]
-    for out, parity in ((mine, core), (theirs, 1 - core)):
+    places = ((theirs, theirs_out, 1 - core), (mine, mine_out, core))
+    for place, (out, target, parity) in enumerate(places):
         for start in range(0, count, rows):
             row = lax.broadcasted_iota(jnp.int32, (rows, 1), 0) + start
             chip = (row % (count // 2)) // 8
@@ -136,7 +139,10 @@
             feature = lax.broadcasted_iota(jnp.int32, (rows, width), 1)
             pick = jnp.where(feature == wanted, 1.0, 0.0).astype(bf16)
             out[start : start + rows, :] = dot(pick, normed_value, 1, 1).astype(bf16)
-    store.wait()
+        stores.append(pltpu.make_async_copy(out, target, sems.at[1 + place]))
+        stores[-1].start()
+    for store in stores:
+        store.wait()
 
 
 def embed_kernel(parts, own, embedded_out, half_out, half, held, sems):
@@ -209,17 +215,21 @@
         far_part[:, cols] = terms[6 * q :].astype(bf16)
 
 
-def side_kernel(info, gave, keep_side, keep_own, side, own_sum):
+def side_kernel(info, gave, far_got, keep_side, keep_own, side, own_sum):
     q = keep_own.shape[0]
     start = pl.multiple_of((1 - info[0]) * 3 * q, 3 * q)
-    side[...] = (keep_side[...] + gave[pl.ds(start, 2 * q), :].astype(f32)).astype(bf16)
+    far = far_got[...].astype(f32)
+    for half in range(2):
+        rows = slice(half * q, (half + 1) * q)
+        terms = keep_side[rows, :] + gave[pl.ds(start + half * q, q), :].astype(f32)
+        side[rows, :] = (terms + jnp.where(info[0] == 1 - half, far, 0.0)).astype(bf16)
     own_sum[...] = keep_own[...] + gave[pl.ds(start + 2 * q, q), :].astype(f32)
 
 
-def text_grad_kernel(info, came, own_sum, far_back, text, text_grad, text_loss):
+def text_grad_kernel(info, came, own_sum, text, text_grad, text_loss):
     q, width = text.shape
     start = pl.multiple_of(info[0] * q, q)
-    total = (own_sum[...] + far_back[...].astype(f32)) + (
+    total = own_sum[...] + (
         came[pl.ds(start, q), :].astype(f32) + came[pl.ds(start + 2 * q, q), :].astype(f32)
     )
     inverse, unit_value = unit_rows(text[...].astype(f32))
@@ -324,11 +334,11 @@
 
     text_half = call(text_kernel, shape((q, width), bf16), [VMEM], after(text, partial_out))
     pair = of_both_cores(text_half)
-    side_in = moved(pair, [(i, i + 2) if i % 2 == 0 else (i, i - 2) for i in range(N_DP)])
-    far_out = [(i - 3, i) if i % 2 == 0 else (i + 3, i) for i in range(N_DP)]
-    far = moved(text_half, far_out)
-
-    half_rows = shape((1024, rows_count), bf16)
+    inward = [(i, i + 2) if i % 2 == 0 else (i, i - 2) for i in range(N_DP)]
+    outward = [(d, s) for s, d in inward]
+    side_in = moved(pair, inward)
+
+    half_rows = pltpu.HBM((1024, rows_count), bf16)
     mine, theirs, slope = call(
         select_kernel,
         (half_rows, half_rows, pltpu.HBM((rows_count, units), f32)),
@@ -336,8 +346,13 @@
         info,
         normed,
         hidden,
-        specs=(VMEM, VMEM, HBM),
-        scratch=(pltpu.VMEM((rows_count, units), f32), sems),
+        specs=(HBM, HBM, HBM),
+        scratch=(
+            pltpu.VMEM((1024, rows_count), bf16),
+            pltpu.VMEM((1024, rows_count), bf16),
+            pltpu.VMEM((rows_count, units), f32),
+            sems,
+        ),
     )
 
     embedded, image_half = call(
@@ -351,7 +366,9 @@
     )
     unit_half = mp_exchange(image_half).reshape(rows_count, width)
 
-    sides = of_both_cores(after(side_in, image_half))
+    side_in = after(side_in, image_half)
+    far = moved(jnp.where(info[0] == 0, side_in[q:], side_in[:q]), inward)
+    sides = of_both_cores(side_in)
     texts = call(
         window_kernel,
         shape((WINDOW * q, width), bf16),
@@ -392,29 +409,30 @@
         after(unit_half, image_part),
         texts,
     )
-    far_back = moved(after(far_part, grad_parts), [(d, s) for s, d in far_out])
-    side, own_sum = call(
-        side_kernel,
-        (shape((2 * q, wide), bf16), shape((q, wide), f32)),
-        [SMEM] + [VMEM] * 3,
-        info,
-        of_both_cores(give),
-        keep_side,
-        keep_own,
-    )
+    far_got = moved(far_part, outward)
+    gave = of_both_cores(give)
 
     grad_own = call(
         grad_kernel,
         copies,
         [VMEM, HBM],
-        after(grad_parts, side),
+        after(grad_parts, gave, far_got),
         in_hbm(embedded),
         specs=HBM,
         scratch=(pltpu.VMEM((q, width), f32), pltpu.VMEM((q, width), bf16), sems),
     )
     grad_image = mp_exchange(grad_own).reshape(rows_count, width)
-    side = after(side, grad_own)
-    came = moved(side, [(i, i - 2) if i % 2 == 0 else (i, i + 2) for i in range(N_DP)])
+    side, own_sum = call(
+        side_kernel,
+        (shape((2 * q, wide), bf16), shape((q, wide), f32)),
+        [SMEM] + [VMEM] * 4,
+        info,
+        after(gave, grad_own),
+        far_got,
+        keep_side,
+        keep_own,
+    )
+    came = moved(side, outward)
 
     grad_pre = call(
         pre_kernel,
@@ -433,18 +451,17 @@
         info,
         mine,
         got_rows,
-        after(grads, came, far_back),
+        after(grads, came),
     )
     up_terms = lax.all_to_all(up_wire, CHIPS, 0, 0, tiled=True)
 
     text_grad, text_loss = call(
         text_grad_kernel,
         (shape((q, width), f32), shape((q, 1), f32)),
-        [SMEM] + [VMEM] * 4,
+        [SMEM] + [VMEM] * 3,
         info,
         of_both_cores(after(came, up_wire)),
         own_sum,
-        far_back,
         text,
     )
     text_loss = text_loss.reshape(q)

time: 147 us -> 152 us (1.034)
  waiting for transfers between devices: 19.7 us -> 31.8 us
  blocking collectives: 28.9 us -> 22 us
    all_to_all x4, waiting for transfers between devices: 3.39 us -> 11.8 us  [mp_exchange(): return lax.all_to_all(partial.reshape(4, q, width), 'mp', 0, 0, tiled=True)]
    all_gather x5, blocking collectives: 28.9 us -> 22 us  [of_both_cores(): return lax.all_gather(value, 'c', axis=0, tiled=True)]
    ppermute x4, waiting for transfers between devices: 0.01 us -> 3.07 us  [moved(): return lax.ppermute(value, DP, [(s % N_DP, d % N_DP) for s, d in pairs])]
    all_to_all x1, starting transfers between devices: 7.7 us -> 10.5 us  [body(): up_terms = lax.all_to_all(up_wire, CHIPS, 0, 0, tiled=True)]
    unnamed x18 -> x26, local copies, waits for them, and re-layouts: 2.97 us -> 3.44 us
  transfers between devices with their start and end apart: 10 -> 10, of which waited for: 2 -> 5; matrix products, arithmetic and copies ran while one was open for 1% -> 1% of each run, Pallas kernels for 8% -> 8%
where the time goes in v5:
time: 152 us; the launch traced here: 150 us
  starting transfers between devices  64.9 us (43%)
  waiting for transfers between devices  31.8 us (21%)
  Pallas kernels  24.7 us (16%)
  blocking collectives  22 us (14%)
  local copies, waits for them, and re-layouts  3.49 us (2%)
  between operations  2.16 us (1%)
    all_to_all x4, starting transfers between devices, mp_exchange(): return lax.all_to_all(partial.reshape(4, q, width), 'mp', 0, 0, tiled=True)  31 us
    pallas_call x13, Pallas kernels, call(): pl.pallas_call(kernel, out_shape=outs, in_specs=ins, out_specs=specs if s...  24.7 us
    all_gather x5, blocking collectives, of_both_cores(): return lax.all_gather(value, 'c', axis=0, tiled=True)  22 us
    ppermute x4, starting transfers between devices, moved(): return lax.ppermute(value, DP, [(s % N_DP, d % N_DP) for s, d in pairs])  18.4 us
    all_to_all x1, waiting for transfers between devices, body(): up_terms = lax.all_to_all(up_wire, CHIPS, 0, 0, tiled=True)  16.9 us
    all_to_all x4, waiting for transfers between devices, mp_exchange(): return lax.all_to_all(partial.reshape(4, q, width), 'mp', 0, 0, tiled=True)  11.8 us
    all_to_all x1, starting transfers between devices, body(): up_terms = lax.all_to_all(up_wire, CHIPS, 0, 0, tiled=True)  10.5 us
    ppermute x1, starting transfers between devices, swapped(): return lax.ppermute(value, 'c', [(0, 1), (1, 0)])  5.14 us
  transfers between devices with their start and end apart: 10, of which 5 were waited for; matrix products, arithmetic and copies ran while one was open for 1% of the time, Pallas kernels for 8%

profile of v5, /device:TPU:1, one launch (start us, length us, event | category | flops | bytes accessed | tf_op | source)
XLA Modules:
  0.0 149.9 jit_solution(8617607216312418938)
XLA Ops:
  0.7 4.5 %shard_map.103 = (bf16[256,1152]{1,0:T(8,128)(2,1)}, bf16[64,1152]{1,0:T(8,128)(2,1)S(1)}, bf16[256,1152]{1,0:T(8,128)(2,1)}, f32[256,640]{1,0:T(8,128)}) custom-call(s32[2]{0:T(128)S(1)} %pad_add_fusion.info, bf16[256,1152]{1,0:T(8,128)(2,1)} %pooled_in.1, f32[1152]{0:T(1024)} %gain_in.1, f32[640]{0:T(1024)} %b_up_in.1, bf16[1152,640]{1,0:T(8,128)(2,1)} %w_up.1, ...), custom_call_target="tpu_custom_call" | custom-call | flops 1 | bytes 1 | tf_op jit(solution)/shard_map/pallas_call | solution.py:31
  5.2 11.0 %all-to-all-start = ((bf16[4,64,1152]{2,1,0:T(8,128)(2,1)}), bf16[4,64,1152]{2,1,0:T(8,128)(2,1)S(1)}, u32[]{:S(2)}, u32[]{:S(2)}) async-start(bf16[4,64,1152]{2,1,0:T(8,128)(2,1)} %bitcast.10), calls=%async_computation | async-start | bytes 1179648 | tf_op jit(solution)/shard_map/all_to_all | solution.py:303
  16.3 2.6 %all_gather.15.pair = bf16[128,1152]{1,0:T(8,128)(2,1)S(1)} all-gather(bf16[64,1152]{1,0:T(8,128)(2,1)S(1)} %shard_map.105), channel_id=1, replica_groups=mesh['x'=4,'zl'=2,'y'=8,'c'=2,'mp'=4] {'c'}, dimensions={0}, use_global_device_ids=true | all-gather | bytes 442368 | tf_op jit(solution)/shard_map/all_gather | solution.py:66
  18.9 8.2 %collective-permute-start.1 = (bf16[128,1152]{1,0:T(8,128)(2,1)S(1)}, bf16[128,1152]{1,0:T(8,128)(2,1)S(1)}, u32[]{:S(2)}, u32[]{:S(2)}) collective-permute-start(bf16[128,1152]{1,0:T(8,128)(2,1)S(1)} %all_gather.15.pair), channel_id=1, source_target_pairs={{0,8},{4,508},{8,16},{12,4},{16,24},{20,12},{24,32},{28,20},{32,40... | collective-permute-start | bytes 884744 | tf_op jit(solution)/shard_map/ppermute | solution.py:58
  27.1 4.0 %shard_map.104 = (bf16[1024,256]{1,0:T(8,128)(2,1)}, bf16[1024,256]{1,0:T(8,128)(2,1)}, f32[256,640]{1,0:T(8,128)}) custom-call(s32[2]{0:T(128)S(1)} %pad_add_fusion.info, bf16[256,1152]{1,0:T(8,128)(2,1)S(1)} %copy-done.4, f32[256,640]{1,0:T(8,128)S(1)} %copy-done.3), custom_call_target="tpu_custom_call" | custom-call | flops 1 | bytes 1 | tf_op jit(solution)/shard_map/pallas_call | solution.py:31
  32.6 1.2 shard_map.106
  33.7 6.9 %all-to-all-start.1 = ((bf16[4,64,1152]{2,1,0:T(8,128)(2,1)}), bf16[4,64,1152]{2,1,0:T(8,128)(2,1)S(1)}, u32[]{:S(2)}, u32[]{:S(2)}) async-start(bf16[4,64,1152]{2,1,0:T(8,128)(2,1)} %get-tuple-element.38), calls=%async_computation.1 | async-start | bytes 1179648 | tf_op jit(solution)/shard_map/all_to_all | solution.py:303
  40.7 5.1 %collective-permute-start = (bf16[1024,256]{1,0:T(8,128)(2,1)}, bf16[1024,256]{1,0:T(8,128)(2,1)S(1)}, u32[]{:S(2)}, u32[]{:S(2)}) collective-permute-start(bf16[1024,256]{1,0:T(8,128)(2,1)} %get-tuple-element.39), channel_id=1, source_target_pairs={{0,4},{4,0},{1,5},{5,1},{2,6},{6,2},{3,7},{7,3},{8,12},{12,8},{9,1... | collective-permute-start | bytes 1572872 | tf_op jit(solution)/shard_map/ppermute | solution.py:62
  45.8 2.2 %all_gather.16 = bf16[256,1152]{1,0:T(8,128)(2,1)S(1)} all-gather(bf16[128,1152]{1,0:T(8,128)(2,1)S(1)} %collective-permute-done.1), channel_id=1, replica_groups=mesh['x'=4,'zl'=2,'y'=8,'c'=2,'mp'=4] {'c'}, dimensions={0}, use_global_device_ids=true | all-gather | bytes 884736 | tf_op jit(solution)/shard_map/all_gather | solution.py:66
  48.1 6.3 %collective-permute-start.2 = (bf16[64,1152]{1,0:T(8,128)(2,1)S(1)}, bf16[64,1152]{1,0:T(8,128)(2,1)S(1)}, u32[]{:S(2)}, u32[]{:S(2)}) collective-permute-start(bf16[64,1152]{1,0:T(8,128)(2,1)S(1)} %slice_select_fusion), channel_id=1, source_target_pairs={{0,8},{4,508},{8,16},{12,4},{16,24},{20,12},{24,32},{28,20},{32,40... | collective-permute-start | bytes 442376 | tf_op jit(solution)/shard_map/ppermute | solution.py:58
  54.5 2.0 %collective-permute-done.2.far = bf16[64,1152]{1,0:T(8,128)(2,1)S(1)} collective-permute-done((bf16[64,1152]{1,0:T(8,128)(2,1)S(1)}, bf16[64,1152]{1,0:T(8,128)(2,1)S(1)}, u32[]{:S(2)}, u32[]{:S(2)}) %collective-permute-start.2) | collective-permute-done | bytes 147488 | tf_op jit(solution)/shard_map/ppermute | solution.py:58
  56.6 2.6 %shard_map.108 = bf16[256,1152]{1,0:T(8,128)(2,1)} custom-call(s32[2]{0:T(128)S(1)} %pad_add_fusion.info, f32[2]{0:T(128)S(1)} %pad_maximum_fusion.factors, bf16[256,1152]{1,0:T(8,128)(2,1)S(1)} %bitcast.6, bf16[448,1152]{1,0:T(8,128)(2,1)S(1)} %shard_map.107.texts), custom_call_target="tpu_custom_call" | custom-call | flops 1 | bytes 1 | tf_op jit(solution)/shard_map/pallas_call | solution.py:31
  59.3 6.9 %all-to-all-start.2 = ((bf16[4,64,1152]{2,1,0:T(8,128)(2,1)}), bf16[4,64,1152]{2,1,0:T(8,128)(2,1)S(1)}, u32[]{:S(2)}, u32[]{:S(2)}) async-start(bf16[4,64,1152]{2,1,0:T(8,128)(2,1)} %bitcast.9), calls=%async_computation.2 | async-start | bytes 1179648 | tf_op jit(solution)/shard_map/all_to_all | solution.py:303
  66.1 2.2 %shard_map.109 = (bf16[192,1280]{1,0:T(8,128)(2,1)S(1)}, bf16[64,1280]{1,0:T(8,128)(2,1)S(1)}, f32[128,1280]{1,0:T(8,128)S(1)}, f32[64,1280]{1,0:T(8,128)S(1)}) custom-call(s32[2]{0:T(128)S(1)} %pad_add_fusion.info, f32[2]{0:T(128)S(1)} %pad_maximum_fusion.factors, bf16[256,1152]{1,0:T(8,128)(2,1)S(1)} %bitcast.7, bf16[448,1152]{1,0:T(8,128)(2,1)S(1)} %shard_map.107.texts), custom_call_target="tpu_custom_call" | custom-call | flops 1 | bytes 1 | tf_op jit(solution)/shard_map/pallas_call | solution.py:31
  68.4 1.9 %collective-permute-start.3 = (bf16[64,1280]{1,0:T(8,128)(2,1)S(1)}, bf16[64,1280]{1,0:T(8,128)(2,1)S(1)}, u32[]{:S(2)}, u32[]{:S(2)}) collective-permute-start(bf16[64,1280]{1,0:T(8,128)(2,1)S(1)} %get-tuple-element.44), channel_id=1, source_target_pairs={{8,0},{508,4},{16,8},{4,12},{24,16},{12,20},{32,24},{20,28},{40,32... | collective-permute-start | bytes 491528 | tf_op jit(solution)/shard_map/ppermute | solution.py:58
  70.3 8.6 %all_gather.17.gave = bf16[384,1280]{1,0:T(8,128)(2,1)S(1)} all-gather(bf16[192,1280]{1,0:T(8,128)(2,1)S(1)} %get-tuple-element.43), channel_id=1, replica_groups=mesh['x'=4,'zl'=2,'y'=8,'c'=2,'mp'=4] {'c'}, dimensions={0}, use_global_device_ids=true | all-gather | bytes 1474560 | tf_op jit(solution)/shard_map/all_gather | solution.py:66
  78.9 1.0 collective-permute-done.3.far_got
  80.6 0.8 all-to-all-done.2.parts
  81.4 2.1 %shard_map.110 = bf16[4,64,1152]{2,1,0:T(8,128)(2,1)} custom-call(bf16[4,64,1152]{2,1,0:T(8,128)(2,1)S(1)} %all-to-all-done.2.parts, f32[64,1152]{1,0:T(8,128)} %get-tuple-element.46.embedded_in), custom_call_target="tpu_custom_call" | custom-call | flops 1 | bytes 1 | tf_op jit(solution)/shard_map/pallas_call | solution.py:31
  83.5 6.2 %all-to-all-start.3 = ((bf16[4,64,1152]{2,1,0:T(8,128)(2,1)}), bf16[4,64,1152]{2,1,0:T(8,128)(2,1)S(1)}, u32[]{:S(2)}, u32[]{:S(2)}) async-start(bf16[4,64,1152]{2,1,0:T(8,128)(2,1)} %shard_map.110), calls=%async_computation.3 | async-start | bytes 1179648 | tf_op jit(solution)/shard_map/all_to_all | solution.py:303
  89.7 1.1 copy-done.2
  90.8 0.9 copy-done.12
  91.7 1.4 shard_map.112
  93.8 1.9 %collective-permute-start.4 = (bf16[128,1280]{1,0:T(8,128)(2,1)}, bf16[128,1280]{1,0:T(8,128)(2,1)S(1)}, u32[]{:S(2)}, u32[]{:S(2)}) collective-permute-start(bf16[128,1280]{1,0:T(8,128)(2,1)} %get-tuple-element.51), channel_id=1, source_target_pairs={{8,0},{508,4},{16,8},{4,12},{24,16},{12,20},{32,24},{20,28},{40,32... | collective-permute-start | bytes 983048 | tf_op jit(solution)/shard_map/ppermute | solution.py:58
  95.8 11.0 %all-to-all-done.3 = bf16[4,64,1152]{2,1,0:T(8,128)(2,1)S(1)} async-done(((bf16[4,64,1152]{2,1,0:T(8,128)(2,1)}), bf16[4,64,1152]{2,1,0:T(8,128)(2,1)S(1)}, u32[]{:S(2)}, u32[]{:S(2)}) %all-to-all-start.3) | async-done | bytes 589856 | tf_op jit(solution)/shard_map/all_to_all | solution.py:303
  106.8 1.8 %shard_map.111 = bf16[256,640]{1,0:T(8,128)(2,1)S(1)} custom-call(bf16[256,1152]{1,0:T(8,128)(2,1)S(1)} %bitcast.8, bf16[640,1152]{1,0:T(8,128)(2,1)S(1)} %copy-done, f32[256,640]{1,0:T(8,128)} %get-tuple-element.47.slope_in), custom_call_target="tpu_custom_call" | custom-call | flops 1 | bytes 1 | tf_op jit(solution)/shard_map/pallas_call | solution.py:31
  108.6 6.0 %all_gather.18.grads = bf16[512,640]{1,0:T(8,128)(2,1)S(1)} all-gather(bf16[256,640]{1,0:T(8,128)(2,1)S(1)} %shard_map.111), channel_id=1, replica_groups=mesh['x'=4,'zl'=2,'y'=8,'c'=2,'mp'=4] {'c'}, dimensions={0}, use_global_device_ids=true | all-gather | bytes 983040 | tf_op jit(solution)/shard_map/all_gather | solution.py:66
  114.6 2.4 %shard_map.113 = bf16[64,16,384]{2,1,0:T(8,128)(2,1)} custom-call(s32[2]{0:T(128)S(1)} %pad_add_fusion.info, bf16[1024,256]{1,0:T(8,128)(2,1)S(1)} %copy-done.6, bf16[1024,256]{1,0:T(8,128)(2,1)S(1)} %copy-done.8, bf16[512,640]{1,0:T(8,128)(2,1)S(1)} %all_gather.18.grads), custom_call_target="tpu_custom_call" | custom-call | flops 1 | bytes 1 | tf_op jit(solution)/shard_map/pallas_call | solution.py:31
  117.1 10.5 %all-to-all-start.4 = ((bf16[64,16,384]{2,1,0:T(8,128)(2,1)}), bf16[64,16,384]{2,1,0:T(8,128)(2,1)S(1)}, u32[]{:S(2)}, u32[]{:S(2)}) async-start(bf16[64,16,384]{2,1,0:T(8,128)(2,1)} %shard_map.113), calls=%async_computation.4 | async-start | bytes 1572864 | tf_op jit(solution)/shard_map/all_to_all | solution.py:456
  127.5 2.6 %all_gather.19.came = bf16[256,1280]{1,0:T(8,128)(2,1)S(1)} all-gather(bf16[128,1280]{1,0:T(8,128)(2,1)S(1)} %collective-permute-done.4), channel_id=1, replica_groups=mesh['x'=4,'zl'=2,'y'=8,'c'=2,'mp'=4] {'c'}, dimensions={0}, use_global_device_ids=true | all-gather | bytes 983040 | tf_op jit(solution)/shard_map/all_gather | solution.py:66
  130.1 1.5 shard_map.115
  132.2 16.9 %all-to-all-done.4.terms = bf16[64,16,384]{2,1,0:T(8,128)(2,1)S(1)} async-done(((bf16[64,16,384]{2,1,0:T(8,128)(2,1)}), bf16[64,16,384]{2,1,0:T(8,128)(2,1)S(1)}, u32[]{:S(2)}, u32[]{:S(2)}) %all-to-all-start.4) | async-done | bytes 786464 | tf_op jit(solution)/shard_map/all_to_all | solution.py:456
  (37 shorter events, 3.3 us)
Async XLA Ops:
  0.7 15.5 %copy-start.5 = (bf16[64,1152]{1,0:T(8,128)(2,1)S(1)}, bf16[64,1152]{1,0:T(8,128)(2,1)}, u32[]{:S(2)}) copy-start(bf16[64,1152]{1,0:T(8,128)(2,1)} %text.2) | copy-start | bytes 442372
  5.2 21.9 %copy-start.3 = (f32[256,640]{1,0:T(8,128)S(1)}, f32[256,640]{1,0:T(8,128)}, u32[]{:S(2)}) copy-start(f32[256,640]{1,0:T(8,128)} %get-tuple-element.31.hidden) | copy-start | bytes 1966084
  5.2 21.9 %copy-start.4 = (bf16[256,1152]{1,0:T(8,128)(2,1)S(1)}, bf16[256,1152]{1,0:T(8,128)(2,1)}, u32[]{:S(2)}) copy-start(bf16[256,1152]{1,0:T(8,128)(2,1)} %get-tuple-element.30.normed) | copy-start | bytes 1769476
  5.2 27.3 %all-to-all-start = ((bf16[4,64,1152]{2,1,0:T(8,128)(2,1)}), bf16[4,64,1152]{2,1,0:T(8,128)(2,1)S(1)}, u32[]{:S(2)}, u32[]{:S(2)}) async-start(bf16[4,64,1152]{2,1,0:T(8,128)(2,1)} %bitcast.10), calls=%async_computation | async-start | bytes 1179648 | tf_op jit(solution)/shard_map/all_to_all | solution.py:303
  18.9 21.7 %collective-permute-start.1 = (bf16[128,1152]{1,0:T(8,128)(2,1)S(1)}, bf16[128,1152]{1,0:T(8,128)(2,1)S(1)}, u32[]{:S(2)}, u32[]{:S(2)}) collective-permute-start(bf16[128,1152]{1,0:T(8,128)(2,1)S(1)} %all_gather.15.pair), channel_id=1, source_target_pairs={{0,8},{4,508},{8,16},{12,4},{16,24},{20,12},{24,32},{28,20},{32,40... | collective-permute-start | bytes 884744 | tf_op jit(solution)/shard_map/ppermute | solution.py:58
  33.7 22.9 %all-to-all-start.1 = ((bf16[4,64,1152]{2,1,0:T(8,128)(2,1)}), bf16[4,64,1152]{2,1,0:T(8,128)(2,1)S(1)}, u32[]{:S(2)}, u32[]{:S(2)}) async-start(bf16[4,64,1152]{2,1,0:T(8,128)(2,1)} %get-tuple-element.38), calls=%async_computation.1 | async-start | bytes 1179648 | tf_op jit(solution)/shard_map/all_to_all | solution.py:303
  40.7 15.9 %collective-permute-start = (bf16[1024,256]{1,0:T(8,128)(2,1)}, bf16[1024,256]{1,0:T(8,128)(2,1)S(1)}, u32[]{:S(2)}, u32[]{:S(2)}) collective-permute-start(bf16[1024,256]{1,0:T(8,128)(2,1)} %get-tuple-element.39), channel_id=1, source_target_pairs={{0,4},{4,0},{1,5},{5,1},{2,6},{6,2},{3,7},{7,3},{8,12},{12,8},{9,1... | collective-permute-start | bytes 1572872 | tf_op jit(solution)/shard_map/ppermute | solution.py:62
  48.1 8.4 %collective-permute-start.2 = (bf16[64,1152]{1,0:T(8,128)(2,1)S(1)}, bf16[64,1152]{1,0:T(8,128)(2,1)S(1)}, u32[]{:S(2)}, u32[]{:S(2)}) collective-permute-start(bf16[64,1152]{1,0:T(8,128)(2,1)S(1)} %slice_select_fusion), channel_id=1, source_target_pairs={{0,8},{4,508},{8,16},{12,4},{16,24},{20,12},{24,32},{28,20},{32,40... | collective-permute-start | bytes 442376 | tf_op jit(solution)/shard_map/ppermute | solution.py:58
  56.6 2.7 %copy-start.7 = (bf16[1024,256]{1,0:T(8,128)(2,1)}, bf16[1024,256]{1,0:T(8,128)(2,1)S(1)}, u32[]{:S(2)}) copy-start(bf16[1024,256]{1,0:T(8,128)(2,1)S(1)} %collective-permute-done.got) | copy-start | bytes 1572868
  59.3 22.1 %all-to-all-start.2 = ((bf16[4,64,1152]{2,1,0:T(8,128)(2,1)}), bf16[4,64,1152]{2,1,0:T(8,128)(2,1)S(1)}, u32[]{:S(2)}, u32[]{:S(2)}) async-start(bf16[4,64,1152]{2,1,0:T(8,128)(2,1)} %bitcast.9), calls=%async_computation.2 | async-start | bytes 1179648 | tf_op jit(solution)/shard_map/all_to_all | solution.py:303
  68.4 10.5 %copy-start.1 = (f32[128,1280]{1,0:T(8,128)}, f32[128,1280]{1,0:T(8,128)S(1)}, u32[]{:S(2)}) copy-start(f32[128,1280]{1,0:T(8,128)S(1)} %get-tuple-element.49.keep_side) | copy-start | bytes 1966084
  68.4 11.6 %collective-permute-start.3 = (bf16[64,1280]{1,0:T(8,128)(2,1)S(1)}, bf16[64,1280]{1,0:T(8,128)(2,1)S(1)}, u32[]{:S(2)}, u32[]{:S(2)}) collective-permute-start(bf16[64,1280]{1,0:T(8,128)(2,1)S(1)} %get-tuple-element.44), channel_id=1, source_target_pairs={{8,0},{508,4},{16,8},{4,12},{24,16},{12,20},{32,24},{20,28},{40,32... | collective-permute-start | bytes 491528 | tf_op jit(solution)/shard_map/ppermute | solution.py:58
  79.9 0.7 copy-start.11
  83.5 23.3 %copy-start = (bf16[640,1152]{1,0:T(8,128)(2,1)S(1)}, bf16[640,1152]{1,0:T(8,128)(2,1)}, u32[]{:S(2)}) copy-start(bf16[640,1152]{1,0:T(8,128)(2,1)} %w_down.3) | copy-start | bytes 4423684
  83.5 23.3 %all-to-all-start.3 = ((bf16[4,64,1152]{2,1,0:T(8,128)(2,1)}), bf16[4,64,1152]{2,1,0:T(8,128)(2,1)S(1)}, u32[]{:S(2)}, u32[]{:S(2)}) async-start(bf16[4,64,1152]{2,1,0:T(8,128)(2,1)} %shard_map.110), calls=%async_computation.3 | async-start | bytes 1179648 | tf_op jit(solution)/shard_map/all_to_all | solution.py:303
  89.7 1.1 copy-start.2
  90.8 0.9 copy-start.12
  93.1 0.7 copy-start.9
  93.8 20.8 %collective-permute-start.4 = (bf16[128,1280]{1,0:T(8,128)(2,1)}, bf16[128,1280]{1,0:T(8,128)(2,1)S(1)}, u32[]{:S(2)}, u32[]{:S(2)}) collective-permute-start(bf16[128,1280]{1,0:T(8,128)(2,1)} %get-tuple-element.51), channel_id=1, source_target_pairs={{8,0},{508,4},{16,8},{4,12},{24,16},{12,20},{32,24},{20,28},{40,32... | collective-permute-start | bytes 983048 | tf_op jit(solution)/shard_map/ppermute | solution.py:58
  106.8 7.8 %copy-start.6 = (bf16[1024,256]{1,0:T(8,128)(2,1)S(1)}, bf16[1024,256]{1,0:T(8,128)(2,1)}, u32[]{:S(2)}) copy-start(bf16[1024,256]{1,0:T(8,128)(2,1)} %get-tuple-element.32.mine) | copy-start | bytes 1572868
  106.8 7.8 %copy-start.8 = (bf16[1024,256]{1,0:T(8,128)(2,1)S(1)}, bf16[1024,256]{1,0:T(8,128)(2,1)}, u32[]{:S(2)}) copy-start(bf16[1024,256]{1,0:T(8,128)(2,1)} %copy-done.7) | copy-start | bytes 1572868
  117.1 13.0 %copy-start.10 = (f32[64,1280]{1,0:T(8,128)S(1)}, f32[64,1280]{1,0:T(8,128)}, u32[]{:S(2)}) copy-start(f32[64,1280]{1,0:T(8,128)} %copy-done.9) | copy-start | bytes 983044
  117.1 32.0 %all-to-all-start.4 = ((bf16[64,16,384]{2,1,0:T(8,128)(2,1)}), bf16[64,16,384]{2,1,0:T(8,128)(2,1)S(1)}, u32[]{:S(2)}, u32[]{:S(2)}) async-start(bf16[64,16,384]{2,1,0:T(8,128)(2,1)} %shard_map.113), calls=%async_computation.4 | async-start | bytes 1572864 | tf_op jit(solution)/shard_map/all_to_all | solution.py:456

commit v6 on v4

--- a/solution.py
+++ b/solution.py
@@ -416,6 +416,19 @@
     side = after(side, grad_own)
     came = moved(side, [(i, i - 2) if i % 2 == 0 else (i, i + 2) for i in range(N_DP)])
 
+    text_grad, text_loss = call(
+        text_grad_kernel,
+        (shape((q, width), f32), shape((q, 1), f32)),
+        [SMEM] + [VMEM] * 4,
+        info,
+        of_both_cores(came),
+        own_sum,
+        far_back,
+        text,
+    )
+    text_loss = text_loss.reshape(q)
+
+    grad_image = after(grad_image, text_grad, text_loss)
     grad_pre = call(
         pre_kernel,
         shape((rows_count, units), bf16),
@@ -433,21 +446,9 @@
         info,
         mine,
         got_rows,
-        after(grads, came, far_back),
+        grads,
     )
     up_terms = lax.all_to_all(up_wire, CHIPS, 0, 0, tiled=True)
-
-    text_grad, text_loss = call(
-        text_grad_kernel,
-        (shape((q, width), f32), shape((q, 1), f32)),
-        [SMEM] + [VMEM] * 4,
-        info,
-        of_both_cores(after(came, up_wire)),
-        own_sum,
-        far_back,
-        text,
-    )
-    text_loss = text_loss.reshape(q)
 
     up_grad = call(up_sum_kernel, shape((width // N_DP, units), f32), [VMEM], up_terms)
     return (up_grad, text_grad, text_loss)

time: 147 us -> 147 us (level)
  blocking collectives: 28.9 us -> 51.2 us
  waiting for transfers between devices: 19.7 us -> 5.6 us
  starting transfers between devices: 65.9 us -> 58.5 us
    all_to_all x0 -> x1, blocking collectives: none -> 29.1 us  [body(): up_terms = lax.all_to_all(up_wire, CHIPS, 0, 0, tiled=True)]
    all_to_all x1 -> x0, waiting for transfers between devices: 16.3 us -> none  [body(): up_terms = lax.all_to_all(up_wire, CHIPS, 0, 0, tiled=True)]
    all_to_all x1 -> x0, starting transfers between devices: 7.7 us -> none  [body(): up_terms = lax.all_to_all(up_wire, CHIPS, 0, 0, tiled=True)]
    all_gather x5, blocking collectives: 28.9 us -> 22.2 us  [of_both_cores(): return lax.all_gather(value, 'c', axis=0, tiled=True)]
    ppermute x4, waiting for transfers between devices: 0.01 us -> 5.59 us  [moved(): return lax.ppermute(value, DP, [(s % N_DP, d % N_DP) for s, d in pairs])]
    all_to_all x4, waiting for transfers between devices: 3.39 us -> 0.01 us  [mp_exchange(): return lax.all_to_all(partial.reshape(4, q, width), 'mp', 0, 0, tiled=True)]
  transfers between devices with their start and end apart: 10 -> 9, of which waited for: 2 -> 1; matrix products, arithmetic and copies ran while one was open for 1% -> 1% of each run, Pallas kernels for 8% -> 6%
where the time goes in v6:
time: 147 us; the launch traced here: 145 us
  starting transfers between devices  58.5 us (40%)
  blocking collectives  51.2 us (35%)
  Pallas kernels  22.6 us (15%)
  waiting for transfers between devices  5.6 us (4%)
  local copies, waits for them, and re-layouts  3.95 us (3%)
  between operations  2.15 us (1%)
    all_to_all x4, starting transfers between devices, mp_exchange(): return lax.all_to_all(partial.reshape(4, q, width), 'mp', 0, 0, tiled=True)  31.9 us
    all_to_all x1, blocking collectives, body(): up_terms = lax.all_to_all(up_wire, CHIPS, 0, 0, tiled=True)  29.1 us
    pallas_call x13, Pallas kernels, call(): pl.pallas_call(kernel, out_shape=outs, in_specs=ins, out_specs=specs if s...  22.6 us
    all_gather x5, blocking collectives, of_both_cores(): return lax.all_gather(value, 'c', axis=0, tiled=True)  22.2 us
    ppermute x4, starting transfers between devices, moved(): return lax.ppermute(value, DP, [(s % N_DP, d % N_DP) for s, d in pairs])  20 us
    ppermute x1, starting transfers between devices, swapped(): return lax.ppermute(value, 'c', [(0, 1), (1, 0)])  6.55 us
    ppermute x4, waiting for transfers between devices, moved(): return lax.ppermute(value, DP, [(s % N_DP, d % N_DP) for s, d in pairs])  5.59 us
    unnamed x18, local copies, waits for them, and re-layouts  3.91 us
  transfers between devices with their start and end apart: 9, of which 1 were waited for; matrix products, arithmetic and copies ran while one was open for 1% of the time, Pallas kernels for 6%

profile of v6, /device:TPU:1, one launch (start us, length us, event | category | flops | bytes accessed | tf_op | source)
XLA Modules:
  0.0 144.8 jit_solution(14576250237167158589)
XLA Ops:
  0.7 4.4 %shard_map.103 = (bf16[256,1152]{1,0:T(8,128)(2,1)}, bf16[64,1152]{1,0:T(8,128)(2,1)S(1)}, bf16[256,1152]{1,0:T(8,128)(2,1)}, f32[256,640]{1,0:T(8,128)}) custom-call(s32[2]{0:T(128)S(1)} %pad_add_fusion.info, bf16[256,1152]{1,0:T(8,128)(2,1)} %pooled_in.1, f32[1152]{0:T(1024)} %gain_in.1, f32[640]{0:T(1024)} %b_up_in.1, bf16[1152,640]{1,0:T(8,128)(2,1)} %w_up.1, ...), custom_call_target="tpu_custom_call" | custom-call | flops 1 | bytes 1 | tf_op jit(solution)/shard_map/pallas_call | solution.py:31
  5.2 11.0 %all-to-all-start = ((bf16[4,64,1152]{2,1,0:T(8,128)(2,1)}), bf16[4,64,1152]{2,1,0:T(8,128)(2,1)S(1)}, u32[]{:S(2)}, u32[]{:S(2)}) async-start(bf16[4,64,1152]{2,1,0:T(8,128)(2,1)} %bitcast.10), calls=%async_computation | async-start | bytes 1179648 | tf_op jit(solution)/shard_map/all_to_all | solution.py:293
  16.3 2.6 %all_gather.15.pair = bf16[128,1152]{1,0:T(8,128)(2,1)S(1)} all-gather(bf16[64,1152]{1,0:T(8,128)(2,1)S(1)} %shard_map.105), channel_id=1, replica_groups=mesh['x'=4,'zl'=2,'y'=8,'c'=2,'mp'=4] {'c'}, dimensions={0}, use_global_device_ids=true | all-gather | bytes 442368 | tf_op jit(solution)/shard_map/all_gather | solution.py:66
  18.9 8.2 %collective-permute-start.1 = (bf16[128,1152]{1,0:T(8,128)(2,1)S(1)}, bf16[128,1152]{1,0:T(8,128)(2,1)}, u32[]{:S(2)}, u32[]{:S(2)}) collective-permute-start(bf16[128,1152]{1,0:T(8,128)(2,1)S(1)} %all_gather.15.pair), channel_id=1, source_target_pairs={{0,8},{4,508},{8,16},{12,4},{16,24},{20,12},{24,32},{28,20},{32,40... | collective-permute-start | bytes 884744 | tf_op jit(solution)/shard_map/ppermute | solution.py:58
  27.1 3.7 %shard_map.104 = (bf16[1024,256]{1,0:T(8,128)(2,1)S(1)}, bf16[1024,256]{1,0:T(8,128)(2,1)S(1)}, f32[256,640]{1,0:T(8,128)}) custom-call(s32[2]{0:T(128)S(1)} %pad_add_fusion.info, bf16[256,1152]{1,0:T(8,128)(2,1)S(1)} %copy-done.3, f32[256,640]{1,0:T(8,128)S(1)} %copy-done.1), custom_call_target="tpu_custom_call" | custom-call | flops 1 | bytes 1 | tf_op jit(solution)/shard_map/pallas_call | solution.py:31
  30.8 0.8 copy-done.6
  31.6 1.2 shard_map.106
  32.8 7.3 %all-to-all-start.1 = ((bf16[4,64,1152]{2,1,0:T(8,128)(2,1)}), bf16[4,64,1152]{2,1,0:T(8,128)(2,1)S(1)}, u32[]{:S(2)}, u32[]{:S(2)}) async-start(bf16[4,64,1152]{2,1,0:T(8,128)(2,1)} %get-tuple-element.38), calls=%async_computation.1 | async-start | bytes 1179648 | tf_op jit(solution)/shard_map/all_to_all | solution.py:293
  40.1 3.0 %collective-permute-start.2 = (bf16[64,1152]{1,0:T(8,128)(2,1)S(1)}, bf16[64,1152]{1,0:T(8,128)(2,1)S(1)}, u32[]{:S(2)}, u32[]{:S(2)}) collective-permute-start(bf16[64,1152]{1,0:T(8,128)(2,1)S(1)} %shard_map.105), channel_id=1, source_target_pairs={{500,0},{16,4},{508,8},{24,12},{4,16},{32,20},{12,24},{40,28},{20,... | collective-permute-start | bytes 442376 | tf_op jit(solution)/shard_map/ppermute | solution.py:58
  44.5 6.6 %collective-permute-start = (bf16[1024,256]{1,0:T(8,128)(2,1)}, bf16[1024,256]{1,0:T(8,128)(2,1)S(1)}, u32[]{:S(2)}, u32[]{:S(2)}) collective-permute-start(bf16[1024,256]{1,0:T(8,128)(2,1)} %copy-done.6), channel_id=1, source_target_pairs={{0,4},{4,0},{1,5},{5,1},{2,6},{6,2},{3,7},{7,3},{8,12},{12,8},{9,1... | collective-permute-start | bytes 1572872 | tf_op jit(solution)/shard_map/ppermute | solution.py:62
  51.1 2.4 %all_gather.16 = bf16[256,1152]{1,0:T(8,128)(2,1)S(1)} all-gather(bf16[128,1152]{1,0:T(8,128)(2,1)} %collective-permute-done.1), channel_id=1, replica_groups=mesh['x'=4,'zl'=2,'y'=8,'c'=2,'mp'=4] {'c'}, dimensions={0}, use_global_device_ids=true | all-gather | bytes 884736 | tf_op jit(solution)/shard_map/all_gather | solution.py:66
  53.7 2.6 %shard_map.108 = bf16[256,1152]{1,0:T(8,128)(2,1)} custom-call(s32[2]{0:T(128)S(1)} %pad_add_fusion.info, f32[2]{0:T(128)S(1)} %pad_maximum_fusion.factors, bf16[256,1152]{1,0:T(8,128)(2,1)S(1)} %bitcast.6, bf16[448,1152]{1,0:T(8,128)(2,1)S(1)} %shard_map.107.texts), custom_call_target="tpu_custom_call" | custom-call | flops 1 | bytes 1 | tf_op jit(solution)/shard_map/pallas_call | solution.py:31
  56.3 6.6 %all-to-all-start.2 = ((bf16[4,64,1152]{2,1,0:T(8,128)(2,1)}), bf16[4,64,1152]{2,1,0:T(8,128)(2,1)S(1)}, u32[]{:S(2)}, u32[]{:S(2)}) async-start(bf16[4,64,1152]{2,1,0:T(8,128)(2,1)} %bitcast.9), calls=%async_computation.2 | async-start | bytes 1179648 | tf_op jit(solution)/shard_map/all_to_all | solution.py:293
  62.9 2.2 %shard_map.109 = (bf16[192,1280]{1,0:T(8,128)(2,1)S(1)}, bf16[64,1280]{1,0:T(8,128)(2,1)S(1)}, f32[128,1280]{1,0:T(8,128)S(1)}, f32[64,1280]{1,0:T(8,128)S(1)}) custom-call(s32[2]{0:T(128)S(1)} %pad_add_fusion.info, f32[2]{0:T(128)S(1)} %pad_maximum_fusion.factors, bf16[256,1152]{1,0:T(8,128)(2,1)S(1)} %bitcast.7, bf16[448,1152]{1,0:T(8,128)(2,1)S(1)} %shard_map.107.texts), custom_call_target="tpu_custom_call" | custom-call | flops 1 | bytes 1 | tf_op jit(solution)/shard_map/pallas_call | solution.py:31
  65.1 0.7 copy-done.8
  65.8 6.9 %all_gather.17.gave = bf16[384,1280]{1,0:T(8,128)(2,1)S(1)} all-gather(bf16[192,1280]{1,0:T(8,128)(2,1)S(1)} %get-tuple-element.43), channel_id=1, replica_groups=mesh['x'=4,'zl'=2,'y'=8,'c'=2,'mp'=4] {'c'}, dimensions={0}, use_global_device_ids=true | all-gather | bytes 1474560 | tf_op jit(solution)/shard_map/all_gather | solution.py:66
  73.4 0.7 copy-done.4
  74.1 0.7 copy-done.7
  74.8 2.1 %shard_map.111 = bf16[4,64,1152]{2,1,0:T(8,128)(2,1)} custom-call(bf16[4,64,1152]{2,1,0:T(8,128)(2,1)S(1)} %all-to-all-done.2.parts, f32[64,1152]{1,0:T(8,128)} %get-tuple-element.48.embedded_in), custom_call_target="tpu_custom_call" | custom-call | flops 1 | bytes 1 | tf_op jit(solution)/shard_map/pallas_call | solution.py:31
  76.9 7.0 %all-to-all-start.3 = ((bf16[4,64,1152]{2,1,0:T(8,128)(2,1)}), bf16[4,64,1152]{2,1,0:T(8,128)(2,1)S(1)}, u32[]{:S(2)}, u32[]{:S(2)}) async-start(bf16[4,64,1152]{2,1,0:T(8,128)(2,1)} %shard_map.111), calls=%async_computation.3 | async-start | bytes 1179648 | tf_op jit(solution)/shard_map/all_to_all | solution.py:293
  83.9 3.1 %collective-permute-start.3 = (bf16[128,1280]{1,0:T(8,128)(2,1)}, bf16[128,1280]{1,0:T(8,128)(2,1)S(1)}, u32[]{:S(2)}, u32[]{:S(2)}) collective-permute-start(bf16[128,1280]{1,0:T(8,128)(2,1)} %copy-done.7), channel_id=1, source_target_pairs={{0,504},{4,12},{8,0},{12,20},{16,8},{20,28},{24,16},{28,36},{32,24... | collective-permute-start | bytes 983048 | tf_op jit(solution)/shard_map/ppermute | solution.py:58
  87.1 5.7 %collective-permute-start.4 = (bf16[64,1280]{1,0:T(8,128)(2,1)}, bf16[64,1280]{1,0:T(8,128)(2,1)S(1)}, u32[]{:S(2)}, u32[]{:S(2)}) collective-permute-start(bf16[64,1280]{1,0:T(8,128)(2,1)} %copy-done.8), channel_id=1, source_target_pairs={{0,500},{4,16},{8,508},{12,24},{16,4},{20,32},{24,12},{28,40},{32,... | collective-permute-start | bytes 491528 | tf_op jit(solution)/shard_map/ppermute | solution.py:58
  92.8 5.6 %collective-permute-done.3 = bf16[128,1280]{1,0:T(8,128)(2,1)S(1)} collective-permute-done((bf16[128,1280]{1,0:T(8,128)(2,1)}, bf16[128,1280]{1,0:T(8,128)(2,1)S(1)}, u32[]{:S(2)}, u32[]{:S(2)}) %collective-permute-start.3) | collective-permute-done | bytes 327712 | tf_op jit(solution)/shard_map/ppermute | solution.py:58
  98.4 4.7 %all_gather.18.came = bf16[256,1280]{1,0:T(8,128)(2,1)S(1)} all-gather(bf16[128,1280]{1,0:T(8,128)(2,1)S(1)} %collective-permute-done.3), channel_id=1, replica_groups=mesh['x'=4,'zl'=2,'y'=8,'c'=2,'mp'=4] {'c'}, dimensions={0}, use_global_device_ids=true | all-gather | bytes 983040 | tf_op jit(solution)/shard_map/all_gather | solution.py:66
  103.1 1.0 copy-done.5
  104.0 1.5 %shard_map.112 = (f32[64,1152]{1,0:T(8,128)}, f32[64,1]{1,0:T(8,128)S(1)}) custom-call(s32[2]{0:T(128)S(1)} %pad_add_fusion.info, bf16[256,1280]{1,0:T(8,128)(2,1)S(1)} %all_gather.18.came, f32[64,1280]{1,0:T(8,128)S(1)} %copy-done.5, bf16[64,1280]{1,0:T(8,128)(2,1)S(1)} %collective-permute-done.4.far_back, bf16[64,1152]{1,0:T(8,128)(2,1)S(1)} %copy-done.2), custom_call_target="tpu_custom_call" | custom-call | flops 1 | bytes 1 | tf_op jit(solution)/shard_map/pallas_call | solution.py:31
  105.5 0.6 reduce
  106.2 1.8 %shard_map.113 = bf16[256,640]{1,0:T(8,128)(2,1)S(1)} custom-call(bf16[256,1152]{1,0:T(8,128)(2,1)S(1)} %bitcast.8, bf16[640,1152]{1,0:T(8,128)(2,1)S(1)} %copy-done, f32[256,640]{1,0:T(8,128)} %get-tuple-element.56.slope_in), custom_call_target="tpu_custom_call" | custom-call | flops 1 | bytes 1 | tf_op jit(solution)/shard_map/pallas_call | solution.py:31
  107.9 5.5 %all_gather.19.grads = bf16[512,640]{1,0:T(8,128)(2,1)S(1)} all-gather(bf16[256,640]{1,0:T(8,128)(2,1)S(1)} %shard_map.113), channel_id=1, replica_groups=mesh['x'=4,'zl'=2,'y'=8,'c'=2,'mp'=4] {'c'}, dimensions={0}, use_global_device_ids=true | all-gather | bytes 983040 | tf_op jit(solution)/shard_map/all_gather | solution.py:66
  113.4 1.5 %shard_map.114 = bf16[64,16,384]{2,1,0:T(8,128)(2,1)S(1)} custom-call(s32[2]{0:T(128)S(1)} %pad_add_fusion.info, bf16[1024,256]{1,0:T(8,128)(2,1)S(1)} %get-tuple-element.32.mine, bf16[1024,256]{1,0:T(8,128)(2,1)S(1)} %collective-permute-done.got, bf16[512,640]{1,0:T(8,128)(2,1)S(1)} %all_gather.19.grads), custom_call_target="tpu_custom_call" | custom-call | flops 1 | bytes 1 | tf_op jit(solution)/shard_map/pallas_call | solution.py:31
  115.0 29.1 %all_to_all.25.terms = bf16[64,16,384]{2,1,0:T(8,128)(2,1)S(1)} all-to-all(bf16[64,16,384]{2,1,0:T(8,128)(2,1)S(1)} %shard_map.114), channel_id=1, replica_groups=mesh['x'=4,'zl'=2,'y'=8,'c'=2,'mp'=4] {'x','zl','y'}, dimensions={0} | all-to-all | bytes 1572864 | tf_op jit(solution)/shard_map/all_to_all | solution.py:451
  144.1 0.8 shard_map.115
  (27 shorter events, 1.1 us)
Async XLA Ops:
  0.7 15.5 %copy-start.2 = (bf16[64,1152]{1,0:T(8,128)(2,1)S(1)}, bf16[64,1152]{1,0:T(8,128)(2,1)}, u32[]{:S(2)}) copy-start(bf16[64,1152]{1,0:T(8,128)(2,1)} %text.2) | copy-start | bytes 442372
  5.2 21.9 %copy-start.1 = (f32[256,640]{1,0:T(8,128)S(1)}, f32[256,640]{1,0:T(8,128)}, u32[]{:S(2)}) copy-start(f32[256,640]{1,0:T(8,128)} %get-tuple-element.31.hidden) | copy-start | bytes 1966084
  5.2 21.9 %copy-start.3 = (bf16[256,1152]{1,0:T(8,128)(2,1)S(1)}, bf16[256,1152]{1,0:T(8,128)(2,1)}, u32[]{:S(2)}) copy-start(bf16[256,1152]{1,0:T(8,128)(2,1)} %get-tuple-element.30.normed) | copy-start | bytes 1769476
  5.2 26.4 %all-to-all-start = ((bf16[4,64,1152]{2,1,0:T(8,128)(2,1)}), bf16[4,64,1152]{2,1,0:T(8,128)(2,1)S(1)}, u32[]{:S(2)}, u32[]{:S(2)}) async-start(bf16[4,64,1152]{2,1,0:T(8,128)(2,1)} %bitcast.10), calls=%async_computation | async-start | bytes 1179648 | tf_op jit(solution)/shard_map/all_to_all | solution.py:293
  18.9 25.6 %collective-permute-start.1 = (bf16[128,1152]{1,0:T(8,128)(2,1)S(1)}, bf16[128,1152]{1,0:T(8,128)(2,1)}, u32[]{:S(2)}, u32[]{:S(2)}) collective-permute-start(bf16[128,1152]{1,0:T(8,128)(2,1)S(1)} %all_gather.15.pair), channel_id=1, source_target_pairs={{0,8},{4,508},{8,16},{12,4},{16,24},{20,12},{24,32},{28,20},{32,40... | collective-permute-start | bytes 884744 | tf_op jit(solution)/shard_map/ppermute | solution.py:58
  30.8 0.8 copy-start.6
  32.8 20.9 %all-to-all-start.1 = ((bf16[4,64,1152]{2,1,0:T(8,128)(2,1)}), bf16[4,64,1152]{2,1,0:T(8,128)(2,1)S(1)}, u32[]{:S(2)}, u32[]{:S(2)}) async-start(bf16[4,64,1152]{2,1,0:T(8,128)(2,1)} %get-tuple-element.38), calls=%async_computation.1 | async-start | bytes 1179648 | tf_op jit(solution)/shard_map/all_to_all | solution.py:293
  40.1 13.4 %collective-permute-start.2 = (bf16[64,1152]{1,0:T(8,128)(2,1)S(1)}, bf16[64,1152]{1,0:T(8,128)(2,1)S(1)}, u32[]{:S(2)}, u32[]{:S(2)}) collective-permute-start(bf16[64,1152]{1,0:T(8,128)(2,1)S(1)} %shard_map.105), channel_id=1, source_target_pairs={{500,0},{16,4},{508,8},{24,12},{4,16},{32,20},{12,24},{40,28},{20,... | collective-permute-start | bytes 442376 | tf_op jit(solution)/shard_map/ppermute | solution.py:58
  44.5 9.2 %collective-permute-start = (bf16[1024,256]{1,0:T(8,128)(2,1)}, bf16[1024,256]{1,0:T(8,128)(2,1)S(1)}, u32[]{:S(2)}, u32[]{:S(2)}) collective-permute-start(bf16[1024,256]{1,0:T(8,128)(2,1)} %copy-done.6), channel_id=1, source_target_pairs={{0,4},{4,0},{1,5},{5,1},{2,6},{6,2},{3,7},{7,3},{8,12},{12,8},{9,1... | collective-permute-start | bytes 1572872 | tf_op jit(solution)/shard_map/ppermute | solution.py:62
  56.3 18.5 %all-to-all-start.2 = ((bf16[4,64,1152]{2,1,0:T(8,128)(2,1)}), bf16[4,64,1152]{2,1,0:T(8,128)(2,1)S(1)}, u32[]{:S(2)}, u32[]{:S(2)}) async-start(bf16[4,64,1152]{2,1,0:T(8,128)(2,1)} %bitcast.9), calls=%async_computation.2 | async-start | bytes 1179648 | tf_op jit(solution)/shard_map/all_to_all | solution.py:293
  65.1 0.7 copy-start.8
  73.4 0.7 copy-start.4
  74.1 0.7 copy-start.7
  76.9 29.3 %copy-start = (bf16[640,1152]{1,0:T(8,128)(2,1)S(1)}, bf16[640,1152]{1,0:T(8,128)(2,1)}, u32[]{:S(2)}) copy-start(bf16[640,1152]{1,0:T(8,128)(2,1)} %w_down.3) | copy-start | bytes 4423684
  76.9 29.2 %all-to-all-start.3 = ((bf16[4,64,1152]{2,1,0:T(8,128)(2,1)}), bf16[4,64,1152]{2,1,0:T(8,128)(2,1)S(1)}, u32[]{:S(2)}, u32[]{:S(2)}) async-start(bf16[4,64,1152]{2,1,0:T(8,128)(2,1)} %shard_map.111), calls=%async_computation.3 | async-start | bytes 1179648 | tf_op jit(solution)/shard_map/all_to_all | solution.py:293
  83.9 14.4 %collective-permute-start.3 = (bf16[128,1280]{1,0:T(8,128)(2,1)}, bf16[128,1280]{1,0:T(8,128)(2,1)S(1)}, u32[]{:S(2)}, u32[]{:S(2)}) collective-permute-start(bf16[128,1280]{1,0:T(8,128)(2,1)} %copy-done.7), channel_id=1, source_target_pairs={{0,504},{4,12},{8,0},{12,20},{16,8},{20,28},{24,16},{28,36},{32,24... | collective-permute-start | bytes 983048 | tf_op jit(solution)/shard_map/ppermute | solution.py:58
  87.1 16.0 %collective-permute-start.4 = (bf16[64,1280]{1,0:T(8,128)(2,1)}, bf16[64,1280]{1,0:T(8,128)(2,1)S(1)}, u32[]{:S(2)}, u32[]{:S(2)}) collective-permute-start(bf16[64,1280]{1,0:T(8,128)(2,1)} %copy-done.8), channel_id=1, source_target_pairs={{0,500},{4,16},{8,508},{12,24},{16,4},{20,32},{24,12},{28,40},{32,... | collective-permute-start | bytes 491528 | tf_op jit(solution)/shard_map/ppermute | solution.py:58
  103.1 1.0 copy-start.5

commit v7 on v4

--- a/solution.py
+++ b/solution.py
@@ -173,8 +173,8 @@
     return ((sigmoid - is_pair) * (scale / WINDOW)).astype(bf16), small
 
 
-def image_kernel(info, factors, unit_half, texts, image_part, held, sems):
-    scale, bias = factors[0], factors[1]
+def image_kernel(info, logit_scale, logit_bias, unit_half, texts, image_part, held, sems):
+    scale, bias = logit_scale[0], logit_bias[0]
     quarter = texts.shape[0] // WINDOW
     window = texts[...]
     logits = scale * dot(unit_half[...], window, 1, 1) + bias
@@ -184,8 +184,8 @@
     copied(sems, (held, image_part))[0].wait()
 
 
-def text_part_kernel(info, factors, unit_half, texts, give, far_part, keep_side, keep_own):
-    scale, bias = factors[0], factors[1]
+def text_part_kernel(info, logit_scale, logit_bias, unit_half, texts, give, far_part, keep_side, keep_own):
+    scale, bias = logit_scale[0], logit_bias[0]
     images = unit_half[...]
     q = texts.shape[0] // WINDOW
     width = images.shape[1]
@@ -286,7 +286,6 @@
     units = w_up.shape[1]
     core = lax.axis_index("c")
     info = jnp.stack([core, lax.axis_index("mp")]).astype(jnp.int32)
-    factors = jnp.concatenate([logit_scale, logit_bias])
     wide = width + LANES
 
     def mp_exchange(partial):
@@ -345,7 +344,7 @@
         (pltpu.HBM((q, width), f32), copies),
         [VMEM, VMEM],
         parts,
-        after(own, theirs, pair),
+        after(own, theirs, pair, far),
         specs=(HBM, HBM),
         scratch=(pltpu.VMEM((q, width), bf16), pltpu.VMEM((q, width), f32), sems),
     )
@@ -362,21 +361,21 @@
         far,
     )
 
-    got_rows = swapped(after(theirs, image_half))
-    texts = after(texts, got_rows)
 
     image_part = call(
         image_kernel,
         whole,
-        [SMEM, SMEM, VMEM, VMEM],
-        info,
-        factors,
+        [SMEM] * 3 + [VMEM] * 2,
+        info,
+        logit_scale,
+        logit_bias,
         unit_half,
         texts,
         specs=HBM,
         scratch=(pltpu.VMEM((rows_count, width), bf16), sems),
     )
     grad_parts = mp_exchange(image_part)
+    got_rows = swapped(after(theirs, image_part))
 
     give, far_part, keep_side, keep_own = call(
         text_part_kernel,
@@ -386,9 +385,10 @@
             shape((2 * q, wide), f32),
             shape((q, wide), f32),
         ),
-        [SMEM, SMEM, VMEM, VMEM],
-        info,
-        factors,
+        [SMEM] * 3 + [VMEM] * 2,
+        info,
+        logit_scale,
+        logit_bias,
         after(unit_half, image_part),
         texts,
     )

time: 147 us -> 143 us (0.973)
  waiting for transfers between devices: 19.7 us -> 33.4 us
  starting transfers between devices: 65.9 us -> 56.3 us
  blocking collectives: 28.9 us -> 22.4 us
    all_to_all x4, waiting for transfers between devices: 3.39 us -> 17.1 us  [mp_exchange(): return lax.all_to_all(partial.reshape(4, q, width), 'mp', 0, 0, tiled=True)]
    all_gather x5, blocking collectives: 28.9 us -> 22.4 us  [of_both_cores(): return lax.all_gather(value, 'c', axis=0, tiled=True)]
    ppermute x4, starting transfers between devices: 19.9 us -> 14.1 us  [moved(): return lax.ppermute(value, DP, [(s % N_DP, d % N_DP) for s, d in pairs])]
    all_to_all x4, starting transfers between devices: 31.8 us -> 26.5 us  [mp_exchange(): return lax.all_to_all(partial.reshape(4, q, width), 'mp', 0, 0, tiled=True)]
    all_to_all x1, starting transfers between devices: 7.7 us -> 11.5 us  [body(): up_terms = lax.all_to_all(up_wire, CHIPS, 0, 0, tiled=True)]
    ppermute x1, starting transfers between devices: 6.55 us -> 4.25 us  [swapped(): return lax.ppermute(value, 'c', [(0, 1), (1, 0)])]
  transfers between devices with their start and end apart: 10 -> 10, of which waited for: 2 -> 4; matrix products, arithmetic and copies ran while one was open for 1% -> 0% of each run, Pallas kernels for 8% -> 8%
where the time goes in v7:
time: 143 us; the launch traced here: 141 us
  starting transfers between devices  56.3 us (39%)
  waiting for transfers between devices  33.4 us (23%)
  Pallas kernels  23.9 us (17%)
  blocking collectives  22.4 us (16%)
  local copies, waits for them, and re-layouts  2.22 us (2%)
  between operations  2.15 us (2%)
    all_to_all x4, starting transfers between devices, mp_exchange(): return lax.all_to_all(partial.reshape(4, q, width), 'mp', 0, 0, tiled=True)  26.5 us
    pallas_call x13, Pallas kernels, call(): pl.pallas_call(kernel, out_shape=outs, in_specs=ins, out_specs=specs if s...  23.9 us
    all_gather x5, blocking collectives, of_both_cores(): return lax.all_gather(value, 'c', axis=0, tiled=True)  22.4 us
    all_to_all x4, waiting for transfers between devices, mp_exchange(): return lax.all_to_all(partial.reshape(4, q, width), 'mp', 0, 0, tiled=True)  17.1 us
    all_to_all x1, waiting for transfers between devices, body(): up_terms = lax.all_to_all(up_wire, CHIPS, 0, 0, tiled=True)  16.3 us
    ppermute x4, starting transfers between devices, moved(): return lax.ppermute(value, DP, [(s % N_DP, d % N_DP) for s, d in pairs])  14.1 us
    all_to_all x1, starting transfers between devices, body(): up_terms = lax.all_to_all(up_wire, CHIPS, 0, 0, tiled=True)  11.5 us
    ppermute x1, starting transfers between devices, swapped(): return lax.ppermute(value, 'c', [(0, 1), (1, 0)])  4.25 us
  transfers between devices with their start and end apart: 10, of which 4 were waited for; matrix products, arithmetic and copies ran while one was open for 0% of the time, Pallas kernels for 8%

profile of v7, /device:TPU:1, one launch (start us, length us, event | category | flops | bytes accessed | tf_op | source)
XLA Modules:
  0.0 141.1 jit_solution(1056693755345960208)
XLA Ops:
  0.7 4.4 %shard_map.103 = (bf16[256,1152]{1,0:T(8,128)(2,1)}, bf16[64,1152]{1,0:T(8,128)(2,1)S(1)}, bf16[256,1152]{1,0:T(8,128)(2,1)}, f32[256,640]{1,0:T(8,128)}) custom-call(s32[2]{0:T(128)S(1)} %pad_add_fusion.info, bf16[256,1152]{1,0:T(8,128)(2,1)} %pooled_in.1, f32[1152]{0:T(1024)} %gain_in.1, f32[640]{0:T(1024)} %b_up_in.1, bf16[1152,640]{1,0:T(8,128)(2,1)} %w_up.1, ...), custom_call_target="tpu_custom_call" | custom-call | flops 1 | bytes 1 | tf_op jit(solution)/shard_map/pallas_call | solution.py:31
  5.2 11.0 %all-to-all-start = ((bf16[4,64,1152]{2,1,0:T(8,128)(2,1)}), bf16[4,64,1152]{2,1,0:T(8,128)(2,1)S(1)}, u32[]{:S(2)}, u32[]{:S(2)}) async-start(bf16[4,64,1152]{2,1,0:T(8,128)(2,1)} %bitcast.10), calls=%async_computation | async-start | bytes 1179648 | tf_op jit(solution)/shard_map/all_to_all | solution.py:292
  16.3 5.1 %collective-permute-start = (bf16[64,1152]{1,0:T(8,128)(2,1)S(1)}, bf16[64,1152]{1,0:T(8,128)(2,1)S(1)}, u32[]{:S(2)}, u32[]{:S(2)}) collective-permute-start(bf16[64,1152]{1,0:T(8,128)(2,1)S(1)} %shard_map.105), channel_id=1, source_target_pairs={{500,0},{16,4},{508,8},{24,12},{4,16},{32,20},{12,24},{40,28},{20,... | collective-permute-start | bytes 442376 | tf_op jit(solution)/shard_map/ppermute | solution.py:58
  21.4 6.0 %all_gather.15.pair = bf16[128,1152]{1,0:T(8,128)(2,1)S(1)} all-gather(bf16[64,1152]{1,0:T(8,128)(2,1)S(1)} %shard_map.105), channel_id=1, replica_groups=mesh['x'=4,'zl'=2,'y'=8,'c'=2,'mp'=4] {'c'}, dimensions={0}, use_global_device_ids=true | all-gather | bytes 442368 | tf_op jit(solution)/shard_map/all_gather | solution.py:66
  27.3 3.0 %collective-permute-start.1 = (bf16[128,1152]{1,0:T(8,128)(2,1)S(1)}, bf16[128,1152]{1,0:T(8,128)(2,1)}, u32[]{:S(2)}, u32[]{:S(2)}) collective-permute-start(bf16[128,1152]{1,0:T(8,128)(2,1)S(1)} %all_gather.15.pair), channel_id=1, source_target_pairs={{0,8},{4,508},{8,16},{12,4},{16,24},{20,12},{24,32},{28,20},{32,40... | collective-permute-start | bytes 884744 | tf_op jit(solution)/shard_map/ppermute | solution.py:58
  30.3 3.7 %shard_map.104 = (bf16[1024,256]{1,0:T(8,128)(2,1)S(1)}, bf16[1024,256]{1,0:T(8,128)(2,1)S(1)}, f32[256,640]{1,0:T(8,128)}) custom-call(s32[2]{0:T(128)S(1)} %pad_add_fusion.info, bf16[256,1152]{1,0:T(8,128)(2,1)S(1)} %copy-done.3, f32[256,640]{1,0:T(8,128)S(1)} %copy-done.1), custom_call_target="tpu_custom_call" | custom-call | flops 1 | bytes 1 | tf_op jit(solution)/shard_map/pallas_call | solution.py:31
  34.1 0.8 copy-done.6
  34.8 1.2 shard_map.106
  36.0 6.6 %all-to-all-start.1 = ((bf16[4,64,1152]{2,1,0:T(8,128)(2,1)}), bf16[4,64,1152]{2,1,0:T(8,128)(2,1)S(1)}, u32[]{:S(2)}, u32[]{:S(2)}) async-start(bf16[4,64,1152]{2,1,0:T(8,128)(2,1)} %get-tuple-element.38), calls=%async_computation.1 | async-start | bytes 1179648 | tf_op jit(solution)/shard_map/all_to_all | solution.py:292
  44.0 3.2 %all_gather.16 = bf16[256,1152]{1,0:T(8,128)(2,1)S(1)} all-gather(bf16[128,1152]{1,0:T(8,128)(2,1)} %collective-permute-done.1), channel_id=1, replica_groups=mesh['x'=4,'zl'=2,'y'=8,'c'=2,'mp'=4] {'c'}, dimensions={0}, use_global_device_ids=true | all-gather | bytes 884736 | tf_op jit(solution)/shard_map/all_gather | solution.py:66
  47.3 10.4 %all-to-all-done.1 = bf16[4,64,1152]{2,1,0:T(8,128)(2,1)S(1)} async-done(((bf16[4,64,1152]{2,1,0:T(8,128)(2,1)}), bf16[4,64,1152]{2,1,0:T(8,128)(2,1)S(1)}, u32[]{:S(2)}, u32[]{:S(2)}) %all-to-all-start.1) | async-done | bytes 589856 | tf_op jit(solution)/shard_map/all_to_all | solution.py:292
  57.7 2.6 %shard_map.108 = bf16[256,1152]{1,0:T(8,128)(2,1)} custom-call(s32[2]{0:T(128)S(1)} %pad_add_fusion.info, f32[1]{0:T(128)S(6)} %copy.11.logit_scale, f32[1]{0:T(128)S(6)} %copy.12.logit_bias, bf16[256,1152]{1,0:T(8,128)(2,1)S(1)} %bitcast.6, bf16[448,1152]{1,0:T(8,128)(2,1)S(1)} %shard_map.107.texts), custom_call_target="tpu_custom_call" | custom-call | flops 1 | bytes 1 | tf_op jit(solution)/shard_map/pallas_call | solution.py:31
  60.4 5.1 %all-to-all-start.2 = ((bf16[4,64,1152]{2,1,0:T(8,128)(2,1)}), bf16[4,64,1152]{2,1,0:T(8,128)(2,1)S(1)}, u32[]{:S(2)}, u32[]{:S(2)}) async-start(bf16[4,64,1152]{2,1,0:T(8,128)(2,1)} %bitcast.9), calls=%async_computation.2 | async-start | bytes 1179648 | tf_op jit(solution)/shard_map/all_to_all | solution.py:292
  65.5 2.2 %shard_map.109 = (bf16[192,1280]{1,0:T(8,128)(2,1)S(1)}, bf16[64,1280]{1,0:T(8,128)(2,1)S(1)}, f32[128,1280]{1,0:T(8,128)S(1)}, f32[64,1280]{1,0:T(8,128)S(1)}) custom-call(s32[2]{0:T(128)S(1)} %pad_add_fusion.info, f32[1]{0:T(128)S(6)} %copy.11.logit_scale, f32[1]{0:T(128)S(6)} %copy.12.logit_bias, bf16[256,1152]{1,0:T(8,128)(2,1)S(1)} %bitcast.7, ...), custom_call_target="tpu_custom_call" | custom-call | flops 1 | bytes 1 | tf_op jit(solution)/shard_map/pallas_call | solution.py:31
  67.7 0.6 copy-done.8
  68.4 2.9 %all_gather.17.gave = bf16[384,1280]{1,0:T(8,128)(2,1)S(1)} all-gather(bf16[192,1280]{1,0:T(8,128)(2,1)S(1)} %get-tuple-element.42), channel_id=1, replica_groups=mesh['x'=4,'zl'=2,'y'=8,'c'=2,'mp'=4] {'c'}, dimensions={0}, use_global_device_ids=true | all-gather | bytes 1474560 | tf_op jit(solution)/shard_map/all_gather | solution.py:66
  71.9 0.7 copy-done.7
  72.6 6.6 %all-to-all-done.2.parts = bf16[4,64,1152]{2,1,0:T(8,128)(2,1)S(1)} async-done(((bf16[4,64,1152]{2,1,0:T(8,128)(2,1)}), bf16[4,64,1152]{2,1,0:T(8,128)(2,1)S(1)}, u32[]{:S(2)}, u32[]{:S(2)}) %all-to-all-start.2) | async-done | bytes 589856 | tf_op jit(solution)/shard_map/all_to_all | solution.py:292
  79.2 2.1 %shard_map.111 = bf16[4,64,1152]{2,1,0:T(8,128)(2,1)} custom-call(bf16[4,64,1152]{2,1,0:T(8,128)(2,1)S(1)} %all-to-all-done.2.parts, f32[64,1152]{1,0:T(8,128)} %get-tuple-element.47.embedded_in), custom_call_target="tpu_custom_call" | custom-call | flops 1 | bytes 1 | tf_op jit(solution)/shard_map/pallas_call | solution.py:31
  81.3 3.7 %all-to-all-start.3 = ((bf16[4,64,1152]{2,1,0:T(8,128)(2,1)}), bf16[4,64,1152]{2,1,0:T(8,128)(2,1)S(1)}, u32[]{:S(2)}, u32[]{:S(2)}) async-start(bf16[4,64,1152]{2,1,0:T(8,128)(2,1)} %shard_map.111), calls=%async_computation.3 | async-start | bytes 1179648 | tf_op jit(solution)/shard_map/all_to_all | solution.py:292
  85.0 4.3 %collective-permute-start.2 = (bf16[1024,256]{1,0:T(8,128)(2,1)}, bf16[1024,256]{1,0:T(8,128)(2,1)S(1)}, u32[]{:S(2)}, u32[]{:S(2)}) collective-permute-start(bf16[1024,256]{1,0:T(8,128)(2,1)} %copy-done.6), channel_id=1, source_target_pairs={{0,4},{4,0},{1,5},{5,1},{2,6},{6,2},{3,7},{7,3},{8,12},{12,8},{9,1... | collective-permute-start | bytes 1572872 | tf_op jit(solution)/shard_map/ppermute | solution.py:62
  89.3 2.8 %collective-permute-start.3 = (bf16[128,1280]{1,0:T(8,128)(2,1)}, bf16[128,1280]{1,0:T(8,128)(2,1)}, u32[]{:S(2)}, u32[]{:S(2)}) collective-permute-start(bf16[128,1280]{1,0:T(8,128)(2,1)} %copy-done.7), channel_id=1, source_target_pairs={{0,504},{4,12},{8,0},{12,20},{16,8},{20,28},{24,16},{28,36},{32,24... | collective-permute-start | bytes 983048 | tf_op jit(solution)/shard_map/ppermute | solution.py:58
  92.1 3.3 %collective-permute-start.4 = (bf16[64,1280]{1,0:T(8,128)(2,1)}, bf16[64,1280]{1,0:T(8,128)(2,1)}, u32[]{:S(2)}, u32[]{:S(2)}) collective-permute-start(bf16[64,1280]{1,0:T(8,128)(2,1)} %copy-done.8), channel_id=1, source_target_pairs={{0,500},{4,16},{8,508},{12,24},{16,4},{20,32},{24,12},{28,40},{32,... | collective-permute-start | bytes 491528 | tf_op jit(solution)/shard_map/ppermute | solution.py:58
  95.5 1.8 %shard_map.112 = bf16[256,640]{1,0:T(8,128)(2,1)S(1)} custom-call(bf16[256,1152]{1,0:T(8,128)(2,1)S(1)} %bitcast.8, bf16[640,1152]{1,0:T(8,128)(2,1)S(1)} %copy-done, f32[256,640]{1,0:T(8,128)} %get-tuple-element.48.slope_in), custom_call_target="tpu_custom_call" | custom-call | flops 1 | bytes 1 | tf_op jit(solution)/shard_map/pallas_call | solution.py:31
  97.2 7.5 %all_gather.18.grads = bf16[512,640]{1,0:T(8,128)(2,1)S(1)} all-gather(bf16[256,640]{1,0:T(8,128)(2,1)S(1)} %shard_map.112), channel_id=1, replica_groups=mesh['x'=4,'zl'=2,'y'=8,'c'=2,'mp'=4] {'c'}, dimensions={0}, use_global_device_ids=true | all-gather | bytes 983040 | tf_op jit(solution)/shard_map/all_gather | solution.py:66
  104.8 2.4 %shard_map.113 = bf16[64,16,384]{2,1,0:T(8,128)(2,1)} custom-call(s32[2]{0:T(128)S(1)} %pad_add_fusion.info, bf16[1024,256]{1,0:T(8,128)(2,1)S(1)} %get-tuple-element.32.mine, bf16[1024,256]{1,0:T(8,128)(2,1)S(1)} %collective-permute-done.2.got, bf16[512,640]{1,0:T(8,128)(2,1)S(1)} %all_gather.18.grads), custom_call_target="tpu_custom_call" | custom-call | flops 1 | bytes 1 | tf_op jit(solution)/shard_map/pallas_call | solution.py:31
  107.2 11.5 %all-to-all-start.4 = ((bf16[64,16,384]{2,1,0:T(8,128)(2,1)}), bf16[64,16,384]{2,1,0:T(8,128)(2,1)S(1)}, u32[]{:S(2)}, u32[]{:S(2)}) async-start(bf16[64,16,384]{2,1,0:T(8,128)(2,1)} %shard_map.113), calls=%async_computation.4 | async-start | bytes 1572864 | tf_op jit(solution)/shard_map/all_to_all | solution.py:438
  118.8 2.8 %all_gather.19.came = bf16[256,1280]{1,0:T(8,128)(2,1)S(1)} all-gather(bf16[128,1280]{1,0:T(8,128)(2,1)} %collective-permute-done.3), channel_id=1, replica_groups=mesh['x'=4,'zl'=2,'y'=8,'c'=2,'mp'=4] {'c'}, dimensions={0}, use_global_device_ids=true | all-gather | bytes 983040 | tf_op jit(solution)/shard_map/all_gather | solution.py:66
  121.6 1.9 %shard_map.115 = (f32[64,1152]{1,0:T(8,128)}, f32[64,1]{1,0:T(8,128)S(1)}) custom-call(s32[2]{0:T(128)S(1)} %pad_add_fusion.info, bf16[256,1280]{1,0:T(8,128)(2,1)S(1)} %all_gather.19.came, f32[64,1280]{1,0:T(8,128)S(1)} %copy-done.5, bf16[64,1280]{1,0:T(8,128)(2,1)} %collective-permute-done.4.far_back, bf16[64,1152]{1,0:T(8,128)(2,1)S(1)} %copy-done.2), custom_call_target="tpu_custom_call" | custom-call | flops 1 | bytes 1 | tf_op jit(solution)/shard_map/pallas_call | solution.py:31
  123.4 0.6 reduce
  124.0 16.3 %all-to-all-done.4.terms = bf16[64,16,384]{2,1,0:T(8,128)(2,1)S(1)} async-done(((bf16[64,16,384]{2,1,0:T(8,128)(2,1)}), bf16[64,16,384]{2,1,0:T(8,128)(2,1)S(1)}, u32[]{:S(2)}, u32[]{:S(2)}) %all-to-all-start.4) | async-done | bytes 786464 | tf_op jit(solution)/shard_map/all_to_all | solution.py:438
  140.3 0.8 shard_map.114
  (27 shorter events, 1.1 us)
Async XLA Ops:
  0.7 15.5 %copy-start.2 = (bf16[64,1152]{1,0:T(8,128)(2,1)S(1)}, bf16[64,1152]{1,0:T(8,128)(2,1)}, u32[]{:S(2)}) copy-start(bf16[64,1152]{1,0:T(8,128)(2,1)} %text.2) | copy-start | bytes 442372
  5.2 25.2 %copy-start.1 = (f32[256,640]{1,0:T(8,128)S(1)}, f32[256,640]{1,0:T(8,128)}, u32[]{:S(2)}) copy-start(f32[256,640]{1,0:T(8,128)} %get-tuple-element.31.hidden) | copy-start | bytes 1966084
  5.2 25.2 %copy-start.3 = (bf16[256,1152]{1,0:T(8,128)(2,1)S(1)}, bf16[256,1152]{1,0:T(8,128)(2,1)}, u32[]{:S(2)}) copy-start(bf16[256,1152]{1,0:T(8,128)(2,1)} %get-tuple-element.30.normed) | copy-start | bytes 1769476
  5.2 29.6 %all-to-all-start = ((bf16[4,64,1152]{2,1,0:T(8,128)(2,1)}), bf16[4,64,1152]{2,1,0:T(8,128)(2,1)S(1)}, u32[]{:S(2)}, u32[]{:S(2)}) async-start(bf16[4,64,1152]{2,1,0:T(8,128)(2,1)} %bitcast.10), calls=%async_computation | async-start | bytes 1179648 | tf_op jit(solution)/shard_map/all_to_all | solution.py:292
  16.3 17.7 %collective-permute-start = (bf16[64,1152]{1,0:T(8,128)(2,1)S(1)}, bf16[64,1152]{1,0:T(8,128)(2,1)S(1)}, u32[]{:S(2)}, u32[]{:S(2)}) collective-permute-start(bf16[64,1152]{1,0:T(8,128)(2,1)S(1)} %shard_map.105), channel_id=1, source_target_pairs={{500,0},{16,4},{508,8},{24,12},{4,16},{32,20},{12,24},{40,28},{20,... | collective-permute-start | bytes 442376 | tf_op jit(solution)/shard_map/ppermute | solution.py:58
  27.3 16.6 %collective-permute-start.1 = (bf16[128,1152]{1,0:T(8,128)(2,1)S(1)}, bf16[128,1152]{1,0:T(8,128)(2,1)}, u32[]{:S(2)}, u32[]{:S(2)}) collective-permute-start(bf16[128,1152]{1,0:T(8,128)(2,1)S(1)} %all_gather.15.pair), channel_id=1, source_target_pairs={{0,8},{4,508},{8,16},{12,4},{16,24},{20,12},{24,32},{28,20},{32,40... | collective-permute-start | bytes 884744 | tf_op jit(solution)/shard_map/ppermute | solution.py:58
  34.0 0.8 copy-start.6
  36.0 21.7 %all-to-all-start.1 = ((bf16[4,64,1152]{2,1,0:T(8,128)(2,1)}), bf16[4,64,1152]{2,1,0:T(8,128)(2,1)S(1)}, u32[]{:S(2)}, u32[]{:S(2)}) async-start(bf16[4,64,1152]{2,1,0:T(8,128)(2,1)} %get-tuple-element.38), calls=%async_computation.1 | async-start | bytes 1179648 | tf_op jit(solution)/shard_map/all_to_all | solution.py:292
  60.4 18.9 %all-to-all-start.2 = ((bf16[4,64,1152]{2,1,0:T(8,128)(2,1)}), bf16[4,64,1152]{2,1,0:T(8,128)(2,1)S(1)}, u32[]{:S(2)}, u32[]{:S(2)}) async-start(bf16[4,64,1152]{2,1,0:T(8,128)(2,1)} %bitcast.9), calls=%async_computation.2 | async-start | bytes 1179648 | tf_op jit(solution)/shard_map/all_to_all | solution.py:292
  67.7 0.7 copy-start.8
  71.9 0.7 copy-start.7
  72.6 8.7 %copy-start.4 = (f32[64,1280]{1,0:T(8,128)}, f32[64,1280]{1,0:T(8,128)S(1)}, u32[]{:S(2)}) copy-start(f32[64,1280]{1,0:T(8,128)S(1)} %get-tuple-element.54.own_sum) | copy-start | bytes 983044
  72.6 22.8 %copy-start = (bf16[640,1152]{1,0:T(8,128)(2,1)S(1)}, bf16[640,1152]{1,0:T(8,128)(2,1)}, u32[]{:S(2)}) copy-start(bf16[640,1152]{1,0:T(8,128)(2,1)} %w_down.3) | copy-start | bytes 4423684
  81.3 14.1 %all-to-all-start.3 = ((bf16[4,64,1152]{2,1,0:T(8,128)(2,1)}), bf16[4,64,1152]{2,1,0:T(8,128)(2,1)S(1)}, u32[]{:S(2)}, u32[]{:S(2)}) async-start(bf16[4,64,1152]{2,1,0:T(8,128)(2,1)} %shard_map.111), calls=%async_computation.3 | async-start | bytes 1179648 | tf_op jit(solution)/shard_map/all_to_all | solution.py:292
  85.0 19.7 %collective-permute-start.2 = (bf16[1024,256]{1,0:T(8,128)(2,1)}, bf16[1024,256]{1,0:T(8,128)(2,1)S(1)}, u32[]{:S(2)}, u32[]{:S(2)}) collective-permute-start(bf16[1024,256]{1,0:T(8,128)(2,1)} %copy-done.6), channel_id=1, source_target_pairs={{0,4},{4,0},{1,5},{5,1},{2,6},{6,2},{3,7},{7,3},{8,12},{12,8},{9,1... | collective-permute-start | bytes 1572872 | tf_op jit(solution)/shard_map/ppermute | solution.py:62
  89.3 15.5 %collective-permute-start.3 = (bf16[128,1280]{1,0:T(8,128)(2,1)}, bf16[128,1280]{1,0:T(8,128)(2,1)}, u32[]{:S(2)}, u32[]{:S(2)}) collective-permute-start(bf16[128,1280]{1,0:T(8,128)(2,1)} %copy-done.7), channel_id=1, source_target_pairs={{0,504},{4,12},{8,0},{12,20},{16,8},{20,28},{24,16},{28,36},{32,24... | collective-permute-start | bytes 983048 | tf_op jit(solution)/shard_map/ppermute | solution.py:58
  92.1 12.7 %collective-permute-start.4 = (bf16[64,1280]{1,0:T(8,128)(2,1)}, bf16[64,1280]{1,0:T(8,128)(2,1)}, u32[]{:S(2)}, u32[]{:S(2)}) collective-permute-start(bf16[64,1280]{1,0:T(8,128)(2,1)} %copy-done.8), channel_id=1, source_target_pairs={{0,500},{4,16},{8,508},{12,24},{16,4},{20,32},{24,12},{28,40},{32,... | collective-permute-start | bytes 491528 | tf_op jit(solution)/shard_map/ppermute | solution.py:58
  107.2 14.3 %copy-start.5 = (f32[64,1280]{1,0:T(8,128)S(1)}, f32[64,1280]{1,0:T(8,128)}, u32[]{:S(2)}) copy-start(f32[64,1280]{1,0:T(8,128)} %copy-done.4) | copy-start | bytes 983044
  107.2 33.1 %all-to-all-start.4 = ((bf16[64,16,384]{2,1,0:T(8,128)(2,1)}), bf16[64,16,384]{2,1,0:T(8,128)(2,1)S(1)}, u32[]{:S(2)}, u32[]{:S(2)}) async-start(bf16[64,16,384]{2,1,0:T(8,128)(2,1)} %shard_map.113), calls=%async_computation.4 | async-start | bytes 1572864 | tf_op jit(solution)/shard_map/all_to_all | solution.py:438

commit v8 on v7

--- a/solution.py
+++ b/solution.py
@@ -230,15 +230,26 @@
 
 
 def grad_kernel(parts, embedded_in, grad_out, embedded, grad, sems):
-    load = copied(sems, (embedded_in, embedded))[0]
-    grad_sum = (parts[0].astype(f32) + parts[1].astype(f32)) + (
-        parts[2].astype(f32) + parts[3].astype(f32)
-    )
+    load = pltpu.make_async_copy(embedded_in, embedded, sems.at[8])
+    load.start()
     load.wait()
-    inverse, unit_value = unit_rows(embedded[...])
-    radial = jnp.sum(unit_value * grad_sum, axis=-1, keepdims=True)
-    grad[...] = (inverse * (grad_sum - unit_value * radial)).astype(bf16)
-    stores = copied(sems, *[(grad, grad_out.at[k]) for k in range(4)])
+    rows = grad.shape[0] // 2
+    stores = []
+    for half in range(2):
+        chunk = pl.ds(half * rows, rows)
+        grad_sum = (parts[0, chunk, :].astype(f32) + parts[1, chunk, :].astype(f32)) + (
+            parts[2, chunk, :].astype(f32) + parts[3, chunk, :].astype(f32)
+        )
+        inverse, unit_value = unit_rows(embedded[chunk, :])
+        radial = jnp.sum(unit_value * grad_sum, axis=-1, keepdims=True)
+        grad[chunk, :] = (inverse * (grad_sum - unit_value * radial)).astype(bf16)
+        for k in range(4):
+            stores.append(
+                pltpu.make_async_copy(
+                    grad.at[chunk], grad_out.at[k, chunk], sems.at[4 * half + k]
+                )
+            )
+            stores[-1].start()
     for store in stores:
         store.wait()
 
@@ -250,13 +261,13 @@
     grad_pre[...] = (grad_act * slope[...]).astype(bf16)
 
 
-def up_kernel(info, mine, got, grads, wire):
+def up_kernel(info, mine, got, grads, wire_out, wire, sems):
     rows = grads.shape[0] // 2
     core = info[0]
     own = grads[pl.ds(pl.multiple_of(core * rows, rows), rows), :]
     other = grads[pl.ds(pl.multiple_of((1 - core) * rows, rows), rows), :]
     count = mine.shape[0] // 2
-    chips = wire.shape[0]
+    chips = wire.shape[1]
     main = dot(mine[:count, :], own, 1, 0) + dot(got[:count, :], other, 1, 0)
     rest = dot(mine[count:, :], own, 1, 0) + dot(got[count:, :], other, 1, 0)
     place = lax.broadcasted_iota(jnp.int32, (count, LANES), 0) % 8
@@ -265,11 +276,20 @@
     for k in range(5):
         ninth = jnp.where(place == k, rest[:, k * LANES : (k + 1) * LANES], ninth)
     blocks.append(ninth)
+    stores = []
     for k in range(3):
         both = jnp.concatenate(
             [blocks[k].reshape(chips, 8, LANES), blocks[k + 3].reshape(chips, 8, LANES)], axis=1
         )
-        wire[:, :, k * LANES : (k + 1) * LANES] = both.astype(bf16)
+        wire[k] = both.astype(bf16)
+        stores.append(
+            pltpu.make_async_copy(
+                wire.at[k], wire_out.at[:, :, pl.ds(k * LANES, LANES)], sems.at[k]
+            )
+        )
+        stores[-1].start()
+    for store in stores:
+        store.wait()
 
 
 def up_sum_kernel(terms, up_grad):
@@ -293,7 +313,7 @@
 
     whole = pltpu.HBM((rows_count, width), bf16)
     copies = pltpu.HBM((4, q, width), bf16)
-    sems = pltpu.SemaphoreType.DMA((8,))
+    sems = pltpu.SemaphoreType.DMA((9,))
 
     normed, own, partial_out, hidden = call(
         head_kernel,
@@ -428,12 +448,14 @@
     grads = of_both_cores(grad_pre)
     up_wire = call(
         up_kernel,
-        shape((N_DP // 2, 16, 3 * LANES), bf16),
+        pltpu.HBM((N_DP // 2, 16, 3 * LANES), bf16),
         [SMEM] + [VMEM] * 3,
         info,
         mine,
         got_rows,
         after(grads, came, far_back),
+        specs=HBM,
+        scratch=(pltpu.VMEM((3, N_DP // 2, 16, LANES), bf16), sems),
     )
     up_terms = lax.all_to_all(up_wire, CHIPS, 0, 0, tiled=True)
 

time: 143 us -> 143 us (level)
  no operation moved by 1% of the time
where the time goes in v8:
time: 143 us; the launch traced here: 141 us
  starting transfers between devices  56.4 us (39%)
  waiting for transfers between devices  33.4 us (23%)
  Pallas kernels  23.9 us (17%)
  blocking collectives  22.4 us (16%)
  local copies, waits for them, and re-layouts  2.22 us (2%)
  between operations  2.17 us (2%)
    all_to_all x4, starting transfers between devices, mp_exchange(): return lax.all_to_all(partial.reshape(4, q, width), 'mp', 0, 0, tiled=True)  26.5 us
    pallas_call x13, Pallas kernels, call(): pl.pallas_call(kernel, out_shape=outs, in_specs=ins, out_specs=specs if s...  23.9 us
    all_gather x5, blocking collectives, of_both_cores(): return lax.all_gather(value, 'c', axis=0, tiled=True)  22.4 us
    all_to_all x4, waiting for transfers between devices, mp_exchange(): return lax.all_to_all(partial.reshape(4, q, width), 'mp', 0, 0, tiled=True)  17.1 us
    all_to_all x1, waiting for transfers between devices, body(): up_terms = lax.all_to_all(up_wire, CHIPS, 0, 0, tiled=True)  16.3 us
    ppermute x4, starting transfers between devices, moved(): return lax.ppermute(value, DP, [(s % N_DP, d % N_DP) for s, d in pairs])  14.1 us
    all_to_all x1, starting transfers between devices, body(): up_terms = lax.all_to_all(up_wire, CHIPS, 0, 0, tiled=True)  11.5 us
    ppermute x1, starting transfers between devices, swapped(): return lax.ppermute(value, 'c', [(0, 1), (1, 0)])  4.25 us
  transfers between devices with their start and end apart: 10, of which 4 were waited for; matrix products, arithmetic and copies ran while one was open for 0% of the time, Pallas kernels for 8%

profile of v8, /device:TPU:1, one launch (start us, length us, event | category | flops | bytes accessed | tf_op | source)
XLA Modules:
  0.0 141.1 jit_solution(10799271075672968687)
XLA Ops:
  0.7 4.5 %shard_map.103 = (bf16[256,1152]{1,0:T(8,128)(2,1)}, bf16[64,1152]{1,0:T(8,128)(2,1)S(1)}, bf16[256,1152]{1,0:T(8,128)(2,1)}, f32[256,640]{1,0:T(8,128)}) custom-call(s32[2]{0:T(128)S(1)} %pad_add_fusion.info, bf16[256,1152]{1,0:T(8,128)(2,1)} %pooled_in.1, f32[1152]{0:T(1024)} %gain_in.1, f32[640]{0:T(1024)} %b_up_in.1, bf16[1152,640]{1,0:T(8,128)(2,1)} %w_up.1, ...), custom_call_target="tpu_custom_call" | custom-call | flops 1 | bytes 1 | tf_op jit(solution)/shard_map/pallas_call | solution.py:31
  5.2 11.0 %all-to-all-start = ((bf16[4,64,1152]{2,1,0:T(8,128)(2,1)}), bf16[4,64,1152]{2,1,0:T(8,128)(2,1)S(1)}, u32[]{:S(2)}, u32[]{:S(2)}) async-start(bf16[4,64,1152]{2,1,0:T(8,128)(2,1)} %bitcast.10), calls=%async_computation | async-start | bytes 1179648 | tf_op jit(solution)/shard_map/all_to_all | solution.py:312
  16.3 5.1 %collective-permute-start = (bf16[64,1152]{1,0:T(8,128)(2,1)S(1)}, bf16[64,1152]{1,0:T(8,128)(2,1)S(1)}, u32[]{:S(2)}, u32[]{:S(2)}) collective-permute-start(bf16[64,1152]{1,0:T(8,128)(2,1)S(1)} %shard_map.105), channel_id=1, source_target_pairs={{500,0},{16,4},{508,8},{24,12},{4,16},{32,20},{12,24},{40,28},{20,... | collective-permute-start | bytes 442376 | tf_op jit(solution)/shard_map/ppermute | solution.py:58
  21.4 6.0 %all_gather.15.pair = bf16[128,1152]{1,0:T(8,128)(2,1)S(1)} all-gather(bf16[64,1152]{1,0:T(8,128)(2,1)S(1)} %shard_map.105), channel_id=1, replica_groups=mesh['x'=4,'zl'=2,'y'=8,'c'=2,'mp'=4] {'c'}, dimensions={0}, use_global_device_ids=true | all-gather | bytes 442368 | tf_op jit(solution)/shard_map/all_gather | solution.py:66
  27.4 3.0 %collective-permute-start.1 = (bf16[128,1152]{1,0:T(8,128)(2,1)S(1)}, bf16[128,1152]{1,0:T(8,128)(2,1)}, u32[]{:S(2)}, u32[]{:S(2)}) collective-permute-start(bf16[128,1152]{1,0:T(8,128)(2,1)S(1)} %all_gather.15.pair), channel_id=1, source_target_pairs={{0,8},{4,508},{8,16},{12,4},{16,24},{20,12},{24,32},{28,20},{32,40... | collective-permute-start | bytes 884744 | tf_op jit(solution)/shard_map/ppermute | solution.py:58
  30.4 3.7 %shard_map.104 = (bf16[1024,256]{1,0:T(8,128)(2,1)S(1)}, bf16[1024,256]{1,0:T(8,128)(2,1)S(1)}, f32[256,640]{1,0:T(8,128)}) custom-call(s32[2]{0:T(128)S(1)} %pad_add_fusion.info, bf16[256,1152]{1,0:T(8,128)(2,1)S(1)} %copy-done.3, f32[256,640]{1,0:T(8,128)S(1)} %copy-done.1), custom_call_target="tpu_custom_call" | custom-call | flops 1 | bytes 1 | tf_op jit(solution)/shard_map/pallas_call | solution.py:31
  34.1 0.8 copy-done.6
  34.9 1.2 shard_map.106
  36.0 6.6 %all-to-all-start.1 = ((bf16[4,64,1152]{2,1,0:T(8,128)(2,1)}), bf16[4,64,1152]{2,1,0:T(8,128)(2,1)S(1)}, u32[]{:S(2)}, u32[]{:S(2)}) async-start(bf16[4,64,1152]{2,1,0:T(8,128)(2,1)} %get-tuple-element.38), calls=%async_computation.1 | async-start | bytes 1179648 | tf_op jit(solution)/shard_map/all_to_all | solution.py:312
  44.0 3.2 %all_gather.16 = bf16[256,1152]{1,0:T(8,128)(2,1)S(1)} all-gather(bf16[128,1152]{1,0:T(8,128)(2,1)} %collective-permute-done.1), channel_id=1, replica_groups=mesh['x'=4,'zl'=2,'y'=8,'c'=2,'mp'=4] {'c'}, dimensions={0}, use_global_device_ids=true | all-gather | bytes 884736 | tf_op jit(solution)/shard_map/all_gather | solution.py:66
  47.4 10.4 %all-to-all-done.1 = bf16[4,64,1152]{2,1,0:T(8,128)(2,1)S(1)} async-done(((bf16[4,64,1152]{2,1,0:T(8,128)(2,1)}), bf16[4,64,1152]{2,1,0:T(8,128)(2,1)S(1)}, u32[]{:S(2)}, u32[]{:S(2)}) %all-to-all-start.1) | async-done | bytes 589856 | tf_op jit(solution)/shard_map/all_to_all | solution.py:312
  57.8 2.6 %shard_map.108 = bf16[256,1152]{1,0:T(8,128)(2,1)} custom-call(s32[2]{0:T(128)S(1)} %pad_add_fusion.info, f32[1]{0:T(128)S(6)} %copy.11.logit_scale, f32[1]{0:T(128)S(6)} %copy.12.logit_bias, bf16[256,1152]{1,0:T(8,128)(2,1)S(1)} %bitcast.6, bf16[448,1152]{1,0:T(8,128)(2,1)S(1)} %shard_map.107.texts), custom_call_target="tpu_custom_call" | custom-call | flops 1 | bytes 1 | tf_op jit(solution)/shard_map/pallas_call | solution.py:31
  60.4 5.1 %all-to-all-start.2 = ((bf16[4,64,1152]{2,1,0:T(8,128)(2,1)}), bf16[4,64,1152]{2,1,0:T(8,128)(2,1)S(1)}, u32[]{:S(2)}, u32[]{:S(2)}) async-start(bf16[4,64,1152]{2,1,0:T(8,128)(2,1)} %bitcast.9), calls=%async_computation.2 | async-start | bytes 1179648 | tf_op jit(solution)/shard_map/all_to_all | solution.py:312
  65.5 2.2 %shard_map.109 = (bf16[192,1280]{1,0:T(8,128)(2,1)S(1)}, bf16[64,1280]{1,0:T(8,128)(2,1)S(1)}, f32[128,1280]{1,0:T(8,128)S(1)}, f32[64,1280]{1,0:T(8,128)S(1)}) custom-call(s32[2]{0:T(128)S(1)} %pad_add_fusion.info, f32[1]{0:T(128)S(6)} %copy.11.logit_scale, f32[1]{0:T(128)S(6)} %copy.12.logit_bias, bf16[256,1152]{1,0:T(8,128)(2,1)S(1)} %bitcast.7, ...), custom_call_target="tpu_custom_call" | custom-call | flops 1 | bytes 1 | tf_op jit(solution)/shard_map/pallas_call | solution.py:31
  67.8 0.6 copy-done.8
  68.4 2.9 %all_gather.17.gave = bf16[384,1280]{1,0:T(8,128)(2,1)S(1)} all-gather(bf16[192,1280]{1,0:T(8,128)(2,1)S(1)} %get-tuple-element.42), channel_id=1, replica_groups=mesh['x'=4,'zl'=2,'y'=8,'c'=2,'mp'=4] {'c'}, dimensions={0}, use_global_device_ids=true | all-gather | bytes 1474560 | tf_op jit(solution)/shard_map/all_gather | solution.py:66
  72.0 0.7 copy-done.7
  72.7 6.6 %all-to-all-done.2.parts = bf16[4,64,1152]{2,1,0:T(8,128)(2,1)S(1)} async-done(((bf16[4,64,1152]{2,1,0:T(8,128)(2,1)}), bf16[4,64,1152]{2,1,0:T(8,128)(2,1)S(1)}, u32[]{:S(2)}, u32[]{:S(2)}) %all-to-all-start.2) | async-done | bytes 589856 | tf_op jit(solution)/shard_map/all_to_all | solution.py:312
  79.3 2.1 %shard_map.111 = bf16[4,64,1152]{2,1,0:T(8,128)(2,1)} custom-call(bf16[4,64,1152]{2,1,0:T(8,128)(2,1)S(1)} %all-to-all-done.2.parts, f32[64,1152]{1,0:T(8,128)} %get-tuple-element.47.embedded_in), custom_call_target="tpu_custom_call" | custom-call | flops 1 | bytes 1 | tf_op jit(solution)/shard_map/pallas_call | solution.py:31
  81.3 3.7 %all-to-all-start.3 = ((bf16[4,64,1152]{2,1,0:T(8,128)(2,1)}), bf16[4,64,1152]{2,1,0:T(8,128)(2,1)S(1)}, u32[]{:S(2)}, u32[]{:S(2)}) async-start(bf16[4,64,1152]{2,1,0:T(8,128)(2,1)} %shard_map.111), calls=%async_computation.3 | async-start | bytes 1179648 | tf_op jit(solution)/shard_map/all_to_all | solution.py:312
  85.1 4.3 %collective-permute-start.2 = (bf16[1024,256]{1,0:T(8,128)(2,1)}, bf16[1024,256]{1,0:T(8,128)(2,1)S(1)}, u32[]{:S(2)}, u32[]{:S(2)}) collective-permute-start(bf16[1024,256]{1,0:T(8,128)(2,1)} %copy-done.6), channel_id=1, source_target_pairs={{0,4},{4,0},{1,5},{5,1},{2,6},{6,2},{3,7},{7,3},{8,12},{12,8},{9,1... | collective-permute-start | bytes 1572872 | tf_op jit(solution)/shard_map/ppermute | solution.py:62
  89.3 2.8 %collective-permute-start.3 = (bf16[128,1280]{1,0:T(8,128)(2,1)}, bf16[128,1280]{1,0:T(8,128)(2,1)}, u32[]{:S(2)}, u32[]{:S(2)}) collective-permute-start(bf16[128,1280]{1,0:T(8,128)(2,1)} %copy-done.7), channel_id=1, source_target_pairs={{0,504},{4,12},{8,0},{12,20},{16,8},{20,28},{24,16},{28,36},{32,24... | collective-permute-start | bytes 983048 | tf_op jit(solution)/shard_map/ppermute | solution.py:58
  92.1 3.3 %collective-permute-start.4 = (bf16[64,1280]{1,0:T(8,128)(2,1)}, bf16[64,1280]{1,0:T(8,128)(2,1)}, u32[]{:S(2)}, u32[]{:S(2)}) collective-permute-start(bf16[64,1280]{1,0:T(8,128)(2,1)} %copy-done.8), channel_id=1, source_target_pairs={{0,500},{4,16},{8,508},{12,24},{16,4},{20,32},{24,12},{28,40},{32,... | collective-permute-start | bytes 491528 | tf_op jit(solution)/shard_map/ppermute | solution.py:58
  95.5 1.8 %shard_map.112 = bf16[256,640]{1,0:T(8,128)(2,1)S(1)} custom-call(bf16[256,1152]{1,0:T(8,128)(2,1)S(1)} %bitcast.8, bf16[640,1152]{1,0:T(8,128)(2,1)S(1)} %copy-done, f32[256,640]{1,0:T(8,128)} %get-tuple-element.48.slope_in), custom_call_target="tpu_custom_call" | custom-call | flops 1 | bytes 1 | tf_op jit(solution)/shard_map/pallas_call | solution.py:31
  97.3 7.5 %all_gather.18.grads = bf16[512,640]{1,0:T(8,128)(2,1)S(1)} all-gather(bf16[256,640]{1,0:T(8,128)(2,1)S(1)} %shard_map.112), channel_id=1, replica_groups=mesh['x'=4,'zl'=2,'y'=8,'c'=2,'mp'=4] {'c'}, dimensions={0}, use_global_device_ids=true | all-gather | bytes 983040 | tf_op jit(solution)/shard_map/all_gather | solution.py:66
  104.8 2.4 %shard_map.113 = bf16[64,16,384]{2,1,0:T(8,128)(2,1)} custom-call(s32[2]{0:T(128)S(1)} %pad_add_fusion.info, bf16[1024,256]{1,0:T(8,128)(2,1)S(1)} %get-tuple-element.32.mine, bf16[1024,256]{1,0:T(8,128)(2,1)S(1)} %collective-permute-done.2.got, bf16[512,640]{1,0:T(8,128)(2,1)S(1)} %all_gather.18.grads), custom_call_target="tpu_custom_call" | custom-call | flops 1 | bytes 1 | tf_op jit(solution)/shard_map/pallas_call | solution.py:31
  107.2 11.5 %all-to-all-start.4 = ((bf16[64,16,384]{2,1,0:T(8,128)(2,1)}), bf16[64,16,384]{2,1,0:T(8,128)(2,1)S(1)}, u32[]{:S(2)}, u32[]{:S(2)}) async-start(bf16[64,16,384]{2,1,0:T(8,128)(2,1)} %shard_map.113), calls=%async_computation.4 | async-start | bytes 1572864 | tf_op jit(solution)/shard_map/all_to_all | solution.py:460
  118.7 2.8 %all_gather.19.came = bf16[256,1280]{1,0:T(8,128)(2,1)S(1)} all-gather(bf16[128,1280]{1,0:T(8,128)(2,1)} %collective-permute-done.3), channel_id=1, replica_groups=mesh['x'=4,'zl'=2,'y'=8,'c'=2,'mp'=4] {'c'}, dimensions={0}, use_global_device_ids=true | all-gather | bytes 983040 | tf_op jit(solution)/shard_map/all_gather | solution.py:66
  121.5 1.9 %shard_map.115 = (f32[64,1152]{1,0:T(8,128)}, f32[64,1]{1,0:T(8,128)S(1)}) custom-call(s32[2]{0:T(128)S(1)} %pad_add_fusion.info, bf16[256,1280]{1,0:T(8,128)(2,1)S(1)} %all_gather.19.came, f32[64,1280]{1,0:T(8,128)S(1)} %copy-done.5, bf16[64,1280]{1,0:T(8,128)(2,1)} %collective-permute-done.4.far_back, bf16[64,1152]{1,0:T(8,128)(2,1)S(1)} %copy-done.2), custom_call_target="tpu_custom_call" | custom-call | flops 1 | bytes 1 | tf_op jit(solution)/shard_map/pallas_call | solution.py:31
  123.4 0.6 reduce
  124.0 16.3 %all-to-all-done.4.terms = bf16[64,16,384]{2,1,0:T(8,128)(2,1)S(1)} async-done(((bf16[64,16,384]{2,1,0:T(8,128)(2,1)}), bf16[64,16,384]{2,1,0:T(8,128)(2,1)S(1)}, u32[]{:S(2)}, u32[]{:S(2)}) %all-to-all-start.4) | async-done | bytes 786464 | tf_op jit(solution)/shard_map/all_to_all | solution.py:460
  140.3 0.8 shard_map.114
  (27 shorter events, 1.1 us)
Async XLA Ops:
  0.7 15.5 %copy-start.2 = (bf16[64,1152]{1,0:T(8,128)(2,1)S(1)}, bf16[64,1152]{1,0:T(8,128)(2,1)}, u32[]{:S(2)}) copy-start(bf16[64,1152]{1,0:T(8,128)(2,1)} %text.2) | copy-start | bytes 442372
  5.2 25.2 %copy-start.1 = (f32[256,640]{1,0:T(8,128)S(1)}, f32[256,640]{1,0:T(8,128)}, u32[]{:S(2)}) copy-start(f32[256,640]{1,0:T(8,128)} %get-tuple-element.31.hidden) | copy-start | bytes 1966084
  5.2 25.2 %copy-start.3 = (bf16[256,1152]{1,0:T(8,128)(2,1)S(1)}, bf16[256,1152]{1,0:T(8,128)(2,1)}, u32[]{:S(2)}) copy-start(bf16[256,1152]{1,0:T(8,128)(2,1)} %get-tuple-element.30.normed) | copy-start | bytes 1769476
  5.2 29.7 %all-to-all-start = ((bf16[4,64,1152]{2,1,0:T(8,128)(2,1)}), bf16[4,64,1152]{2,1,0:T(8,128)(2,1)S(1)}, u32[]{:S(2)}, u32[]{:S(2)}) async-start(bf16[4,64,1152]{2,1,0:T(8,128)(2,1)} %bitcast.10), calls=%async_computation | async-start | bytes 1179648 | tf_op jit(solution)/shard_map/all_to_all | solution.py:312
  16.3 17.8 %collective-permute-start = (bf16[64,1152]{1,0:T(8,128)(2,1)S(1)}, bf16[64,1152]{1,0:T(8,128)(2,1)S(1)}, u32[]{:S(2)}, u32[]{:S(2)}) collective-permute-start(bf16[64,1152]{1,0:T(8,128)(2,1)S(1)} %shard_map.105), channel_id=1, source_target_pairs={{500,0},{16,4},{508,8},{24,12},{4,16},{32,20},{12,24},{40,28},{20,... | collective-permute-start | bytes 442376 | tf_op jit(solution)/shard_map/ppermute | solution.py:58
  27.4 16.6 %collective-permute-start.1 = (bf16[128,1152]{1,0:T(8,128)(2,1)S(1)}, bf16[128,1152]{1,0:T(8,128)(2,1)}, u32[]{:S(2)}, u32[]{:S(2)}) collective-permute-start(bf16[128,1152]{1,0:T(8,128)(2,1)S(1)} %all_gather.15.pair), channel_id=1, source_target_pairs={{0,8},{4,508},{8,16},{12,4},{16,24},{20,12},{24,32},{28,20},{32,40... | collective-permute-start | bytes 884744 | tf_op jit(solution)/shard_map/ppermute | solution.py:58
  34.1 0.8 copy-start.6
  36.0 21.7 %all-to-all-start.1 = ((bf16[4,64,1152]{2,1,0:T(8,128)(2,1)}), bf16[4,64,1152]{2,1,0:T(8,128)(2,1)S(1)}, u32[]{:S(2)}, u32[]{:S(2)}) async-start(bf16[4,64,1152]{2,1,0:T(8,128)(2,1)} %get-tuple-element.38), calls=%async_computation.1 | async-start | bytes 1179648 | tf_op jit(solution)/shard_map/all_to_all | solution.py:312
  60.4 18.9 %all-to-all-start.2 = ((bf16[4,64,1152]{2,1,0:T(8,128)(2,1)}), bf16[4,64,1152]{2,1,0:T(8,128)(2,1)S(1)}, u32[]{:S(2)}, u32[]{:S(2)}) async-start(bf16[4,64,1152]{2,1,0:T(8,128)(2,1)} %bitcast.9), calls=%async_computation.2 | async-start | bytes 1179648 | tf_op jit(solution)/shard_map/all_to_all | solution.py:312
  67.8 0.7 copy-start.8
  71.9 0.7 copy-start.7
  72.7 8.7 %copy-start.4 = (f32[64,1280]{1,0:T(8,128)}, f32[64,1280]{1,0:T(8,128)S(1)}, u32[]{:S(2)}) copy-start(f32[64,1280]{1,0:T(8,128)S(1)} %get-tuple-element.54.own_sum) | copy-start | bytes 983044
  72.7 22.8 %copy-start = (bf16[640,1152]{1,0:T(8,128)(2,1)S(1)}, bf16[640,1152]{1,0:T(8,128)(2,1)}, u32[]{:S(2)}) copy-start(bf16[640,1152]{1,0:T(8,128)(2,1)} %w_down.3) | copy-start | bytes 4423684
  81.3 14.1 %all-to-all-start.3 = ((bf16[4,64,1152]{2,1,0:T(8,128)(2,1)}), bf16[4,64,1152]{2,1,0:T(8,128)(2,1)S(1)}, u32[]{:S(2)}, u32[]{:S(2)}) async-start(bf16[4,64,1152]{2,1,0:T(8,128)(2,1)} %shard_map.111), calls=%async_computation.3 | async-start | bytes 1179648 | tf_op jit(solution)/shard_map/all_to_all | solution.py:312
  85.1 19.7 %collective-permute-start.2 = (bf16[1024,256]{1,0:T(8,128)(2,1)}, bf16[1024,256]{1,0:T(8,128)(2,1)S(1)}, u32[]{:S(2)}, u32[]{:S(2)}) collective-permute-start(bf16[1024,256]{1,0:T(8,128)(2,1)} %copy-done.6), channel_id=1, source_target_pairs={{0,4},{4,0},{1,5},{5,1},{2,6},{6,2},{3,7},{7,3},{8,12},{12,8},{9,1... | collective-permute-start | bytes 1572872 | tf_op jit(solution)/shard_map/ppermute | solution.py:62
  89.3 15.5 %collective-permute-start.3 = (bf16[128,1280]{1,0:T(8,128)(2,1)}, bf16[128,1280]{1,0:T(8,128)(2,1)}, u32[]{:S(2)}, u32[]{:S(2)}) collective-permute-start(bf16[128,1280]{1,0:T(8,128)(2,1)} %copy-done.7), channel_id=1, source_target_pairs={{0,504},{4,12},{8,0},{12,20},{16,8},{20,28},{24,16},{28,36},{32,24... | collective-permute-start | bytes 983048 | tf_op jit(solution)/shard_map/ppermute | solution.py:58
  92.1 12.7 %collective-permute-start.4 = (bf16[64,1280]{1,0:T(8,128)(2,1)}, bf16[64,1280]{1,0:T(8,128)(2,1)}, u32[]{:S(2)}, u32[]{:S(2)}) collective-permute-start(bf16[64,1280]{1,0:T(8,128)(2,1)} %copy-done.8), channel_id=1, source_target_pairs={{0,500},{4,16},{8,508},{12,24},{16,4},{20,32},{24,12},{28,40},{32,... | collective-permute-start | bytes 491528 | tf_op jit(solution)/shard_map/ppermute | solution.py:58
  107.2 14.3 %copy-start.5 = (f32[64,1280]{1,0:T(8,128)S(1)}, f32[64,1280]{1,0:T(8,128)}, u32[]{:S(2)}) copy-start(f32[64,1280]{1,0:T(8,128)} %copy-done.4) | copy-start | bytes 983044
  107.2 33.1 %all-to-all-start.4 = ((bf16[64,16,384]{2,1,0:T(8,128)(2,1)}), bf16[64,16,384]{2,1,0:T(8,128)(2,1)S(1)}, u32[]{:S(2)}, u32[]{:S(2)}) async-start(bf16[64,16,384]{2,1,0:T(8,128)(2,1)} %shard_map.113), calls=%async_computation.4 | async-start | bytes 1572864 | tf_op jit(solution)/shard_map/all_to_all | solution.py:460
